TPU v7x, 32 devices: a whole 2x2x4 slice. The times are simulated.
32 devices in a mesh: groups: 1, slab: 32 (over z, y, x, core).
Axes of the slice: x: 2, y: 2, z: 4, core: 2. Of those that a mesh axis runs over, the one named last changes fastest.
Arguments:
- velocity: float32 [3, 128, 64, 256], P(None, ('groups', 'slab')), may hold values from -6 to 6
- pressure_shift: float32 [128, 64, 256], P(('groups', 'slab')), may hold values from 0.02 to 0.5
- owner_rank: int32 [32768, 1], P(('groups', 'slab')), may hold values from 0 to 31; in each aligned block of 1024 rows (0 to 1023, 1024 to 2047, ...) at most 32 rows name the same one
- node_index: int32 [32768], P(('groups', 'slab')), may hold values from 0 to 8191
- map_weight: int32 [32768], P(('groups', 'slab')), may hold values from 1 to 8
- shell_load: float32 [3, 256, 1024], P(None, ('groups', 'slab')), may hold values from -4 to 4
- shell_stiffness: float32 [256, 1024], P(('groups', 'slab')), may hold values from 0.02 to 0.5
- displacement: float32 [3, 256, 1024], P(None, ('groups', 'slab')), may hold values from -6 to 6
- residual_prev: float32 [3, 256, 1024], P(None, ('groups', 'slab')), may hold values from -6 to 6
- solved_prev: float32 [3, 256, 1024], P(None, ('groups', 'slab')), may hold values from -6 to 6
- residual_history: float32 [4, 3, 256, 1024], P(None, None, ('groups', 'slab')), may hold values from -12 to 12, as said below
- solved_history: float32 [4, 3, 256, 1024], P(None, None, ('groups', 'slab')), may hold values from -6 to 6
Outputs:
- pressure: float32 [128, 64, 256], P(('groups', 'slab'))
- new_displacement: float32 [3, 256, 1024], P(None, ('groups', 'slab'))
- wall_displacement: float32 [3, 32768], P(None, ('groups', 'slab'))
Inputs may be any that keep to these rules, and one draw needn't show every extreme that they name: `owner_rank`: among the 1024 wall cells of one device at most 32 name the same owner, and some device has exactly 32 cells with one owner. `residual_history`: independent entries.
All inputs are finite; a program needn't handle non-finite values.
Results may differ from a plain program's by a relative error of at most 0.0001.
Values sent between devices are 32-bit elements; how exact they have to be, the bound alone decides.
No kernel may reach another device: no remote copies, remote signals or barrier semaphores. Data moves between devices by JAX's collectives and lax.ppermute only.
A program may use at most 320 MiB of HBM per device.

v0:
```python
import jax
import jax.numpy as jnp
from jax import lax
from jax.sharding import PartitionSpec as P

CAP = 32
PITERS = 5
SITERS = 8


NU = 0.15
MU = 0.5
WALL = 4.0


def with_halo(cells, sides, width):
    for axis, dim in sides:
        count = lax.axis_size(axis)
        ends = count - 1
        head = lax.slice_in_dim(cells, 0, width, axis=dim)
        tail = lax.slice_in_dim(cells, cells.shape[dim] - width, cells.shape[dim], axis=dim)
        cells = jnp.concatenate(
            [
                lax.ppermute(tail, axis, [(i, (i + 1) % count) for i in range(ends)]),
                cells,
                lax.ppermute(head, axis, [((i + 1) % count, i) for i in range(ends)]),
            ],
            axis=dim,
        )
    return cells


def both_ways(core, axis):
    length = core.shape[axis]
    zero_slab = jnp.zeros_like(lax.slice_in_dim(core, 0, 1, axis=axis))
    ahead = jnp.concatenate([lax.slice_in_dim(core, 1, length, axis=axis), zero_slab], axis)
    behind = jnp.concatenate([zero_slab, lax.slice_in_dim(core, 0, length - 1, axis=axis)], axis)
    return (ahead, behind)


def plane_sum(core):
    ahead_y, behind_y = both_ways(core, core.ndim - 2)
    ahead_z, behind_z = both_ways(core, core.ndim - 1)
    return ahead_y + behind_y + ahead_z + behind_z


def pressure_apply(field, shift):
    extended = with_halo(field, (("slab", 0),), 1)
    beside = extended[2:] + extended[:-2] + plane_sum(field)
    return (6.0 + shift) * field - beside


def pressure_total(value):
    return lax.psum(value, "slab")


def shell_apply(field, stiffness):
    extended = with_halo(field, (("slab", 1),), 1)
    ahead_c, behind_c = both_ways(field, 2)
    beside = extended[:, 2:] + extended[:, :-2] + ahead_c + behind_c
    return (4.0 + stiffness) * field - beside


def shell_total(value):
    return lax.psum(value, "slab")


def small_solve(gram, target):
    factor = jnp.linalg.cholesky(gram)
    gram_size = gram.shape[0]
    forward = []
    for across in range(gram_size):
        partial_sum = target[across] - sum(
            (factor[across, within] * forward[within] for within in range(across))
        )
        forward.append(partial_sum / factor[across, across])
    backward = [None] * gram_size
    for across in reversed(range(gram_size)):
        partial_sum = forward[across] - sum(
            (factor[within, across] * backward[within] for within in range(across + 1, gram_size))
        )
        backward[across] = partial_sum / factor[across, across]
    return jnp.stack(backward)


def on_device(
    velocity,
    pressure_shift,
    owner_rank,
    node_index,
    map_weight,
    shell_load,
    shell_stiffness,
    displacement,
    residual_prev,
    solved_prev,
    residual_history,
    solved_history,
):
    slab_count = lax.axis_size("slab")
    kept = residual_history.shape[0]
    shell_rows = displacement.shape[1]
    shell_cols = displacement.shape[2]
    node_count = shell_rows * shell_cols
    extended = with_halo(velocity, (("slab", 1),), 1)
    predicted = velocity + NU * (
        extended[:, 2:] + extended[:, :-2] + plane_sum(velocity) - 6.0 * velocity
    )
    along_first = with_halo(predicted[0], (("slab", 0),), 1)
    ahead_y, behind_y = both_ways(predicted[1], 1)
    ahead_z, behind_z = both_ways(predicted[2], 2)
    spread = along_first[2:] - along_first[:-2] + ahead_y - behind_y + ahead_z - behind_z
    source = -0.5 * spread
    pressure = jnp.zeros_like(source)
    residual = source
    direction = source
    norm_now = pressure_total(jnp.sum(residual * residual))
    for sweep in range(PITERS):
        image = pressure_apply(direction, pressure_shift)
        step_size = norm_now / lax.psum(jnp.sum(direction * image), "slab")
        pressure = pressure + step_size * direction
        residual = residual - step_size * image
        norm_next = pressure_total(jnp.sum(residual * residual))
        direction = residual + norm_next / norm_now * direction
        norm_now = norm_next
    traction = jnp.stack(
        [
            MU * (predicted[0, :, 1, :] - predicted[0, :, 0, :]),
            WALL * pressure[:, 0, :],
            MU * (predicted[2, :, 1, :] - predicted[2, :, 0, :]),
        ]
    ).reshape(3, -1)
    owners = owner_rank[:, 0]
    ranks = jnp.arange(slab_count, dtype=jnp.int32)
    member = (owners[:, None] == ranks[None, :]).astype(jnp.int32)
    slots = jnp.sum((jnp.cumsum(member, 0) - 1) * member, 1)
    scaled = map_weight.astype(jnp.float32)
    packed = jnp.concatenate([traction * scaled[None, :], scaled[None, :]], 0).T
    send_values = (
        jnp.zeros((slab_count, 4, CAP), jnp.float32)
        .at[owners, :, slots]
        .set(packed)
        .reshape(slab_count, 4 * CAP)
    )
    send_nodes = (
        jnp.full((slab_count, CAP), node_count, jnp.int32).at[owners, slots].set(node_index)
    )
    got_values, got_nodes = (
        lax.all_to_all(send_values, "slab", split_axis=0, concat_axis=0, tiled=True),
        lax.all_to_all(send_nodes, "slab", split_axis=0, concat_axis=0, tiled=True),
    )
    flat_values = got_values.reshape(slab_count, 4, CAP).transpose(0, 2, 1).reshape(-1, 4)
    totals = jax.ops.segment_sum(flat_values, got_nodes.reshape(-1), num_segments=node_count + 1)[
        :node_count
    ]
    force = (totals[:, :3] / jnp.maximum(totals[:, 3], 1.0)[:, None]).T.reshape(
        3, shell_rows, shell_cols
    )
    shell_source = force + shell_load
    solved = displacement
    residual = shell_source - shell_apply(solved, shell_stiffness)
    direction = residual
    norm_now = shell_total(jnp.sum(residual * residual))
    for sweep in range(SITERS):
        image = shell_apply(direction, shell_stiffness)
        step_size = norm_now / lax.psum(jnp.sum(direction * image), "slab")
        solved = solved + step_size * direction
        residual = residual - step_size * image
        norm_next = shell_total(jnp.sum(residual * residual))
        direction = residual + norm_next / norm_now * direction
        norm_now = norm_next
    moved = solved - displacement
    newest_v = moved - residual_prev
    newest_w = solved - solved_prev
    columns = jnp.concatenate([newest_v[None], residual_history], 0).reshape(kept + 1, -1)
    outputs_w = jnp.concatenate([newest_w[None], solved_history], 0)
    moved_flat = moved.reshape(-1)
    gram_local = jnp.dot(columns, columns.T, precision=lax.Precision.HIGHEST)
    target_local = jnp.dot(columns, moved_flat, precision=lax.Precision.HIGHEST)
    gram, target = lax.psum((gram_local, target_local), "slab")
    coefficients = -small_solve(gram, target)
    new_displacement = solved + jnp.einsum(
        "k,kabc->abc", coefficients, outputs_w, precision=lax.Precision.HIGHEST
    )
    shell_flat = new_displacement.reshape(3, node_count)
    requested = jnp.minimum(got_nodes, node_count - 1)
    answers = shell_flat[:, requested].transpose(1, 0, 2)
    returned = lax.all_to_all(answers, "slab", split_axis=0, concat_axis=0, tiled=True)
    wall_displacement = returned[owners, :, slots].T
    return (pressure, new_displacement, wall_displacement)


def solution(mesh):
    in_specs = (
        P(None, ("groups", "slab"), None, None),
        P(("groups", "slab"), None, None),
        P(("groups", "slab"), None),
        P(("groups", "slab")),
        P(("groups", "slab")),
        P(None, ("groups", "slab"), None),
        P(("groups", "slab"), None),
        P(None, ("groups", "slab"), None),
        P(None, ("groups", "slab"), None),
        P(None, ("groups", "slab"), None),
        P(None, None, ("groups", "slab"), None),
        P(None, None, ("groups", "slab"), None),
    )
    out_specs = (
        P(("groups", "slab"), None, None),
        P(None, ("groups", "slab"), None),
        P(None, ("groups", "slab")),
    )
    return jax.shard_map(
        on_device, mesh=mesh, in_specs=in_specs, out_specs=out_specs, check_vma=False
    )
```

profile of v0, /device:TPU:0, one launch (start us, length us, event | category | flops | bytes accessed | tf_op | source)
XLA Modules:
  0.0 1320.2 jit_solution(18235905927680615599)
XLA Ops:
  54.7 50.5 %all-reduce.48 = (f32[]{:T(128)}, f32[]{:T(128)}) all-reduce(f32[]{:T(128)} %get-tuple-element.16, f32[]{:T(128)} %get-tuple-element.15), channel_id=1, replica_groups=mesh['groups'=1,'slab'=32] {'slab'}, use_global_device_ids=true, to_apply=%region_1.0 | all-reduce | flops 2 | bytes 16 | tf_op jit(solution)/shard_map/psum | solution.py:54
  107.2 39.9 %psum.198 = f32[]{:T(128)} all-reduce(f32[]{:T(128)} %multiply_reduce_fusion.6), channel_id=1, replica_groups=mesh['groups'=1,'slab'=32] {'slab'}, use_global_device_ids=true, to_apply=%region_5.0 | all-reduce | flops 1 | bytes 8 | tf_op jit(solution)/shard_map/psum | solution.py:54
  154.6 44.5 %psum.199 = f32[]{:T(128)} all-reduce(f32[]{:T(128)} %get-tuple-element.48), channel_id=1, replica_groups=mesh['groups'=1,'slab'=32] {'slab'}, use_global_device_ids=true, to_apply=%region_7.0 | all-reduce | flops 1 | bytes 8 | tf_op jit(solution)/shard_map/psum | solution.py:120
  201.2 40.0 %psum.200 = f32[]{:T(128)} all-reduce(f32[]{:T(128)} %get-tuple-element.46), channel_id=1, replica_groups=mesh['groups'=1,'slab'=32] {'slab'}, use_global_device_ids=true, to_apply=%region_9.0 | all-reduce | flops 1 | bytes 8 | tf_op jit(solution)/shard_map/psum | solution.py:54
  248.6 44.5 %psum.201 = f32[]{:T(128)} all-reduce(f32[]{:T(128)} %get-tuple-element.44), channel_id=1, replica_groups=mesh['groups'=1,'slab'=32] {'slab'}, use_global_device_ids=true, to_apply=%region_11.0 | all-reduce | flops 1 | bytes 8 | tf_op jit(solution)/shard_map/psum | solution.py:120
  295.2 39.5 %psum.202 = f32[]{:T(128)} all-reduce(f32[]{:T(128)} %get-tuple-element.42), channel_id=1, replica_groups=mesh['groups'=1,'slab'=32] {'slab'}, use_global_device_ids=true, to_apply=%region_13.0 | all-reduce | flops 1 | bytes 8 | tf_op jit(solution)/shard_map/psum | solution.py:54
  342.1 44.6 %psum.203 = f32[]{:T(128)} all-reduce(f32[]{:T(128)} %get-tuple-element.40), channel_id=1, replica_groups=mesh['groups'=1,'slab'=32] {'slab'}, use_global_device_ids=true, to_apply=%region_15.0 | all-reduce | flops 1 | bytes 8 | tf_op jit(solution)/shard_map/psum | solution.py:120
  388.8 39.7 %psum.204 = f32[]{:T(128)} all-reduce(f32[]{:T(128)} %multiply_reduce_fusion), channel_id=1, replica_groups=mesh['groups'=1,'slab'=32] {'slab'}, use_global_device_ids=true, to_apply=%region_17.0 | all-reduce | flops 1 | bytes 8 | tf_op jit(solution)/shard_map/psum | solution.py:54
  435.9 44.6 %psum.205 = f32[]{:T(128)} all-reduce(f32[]{:T(128)} %fusion.14), channel_id=1, replica_groups=mesh['groups'=1,'slab'=32] {'slab'}, use_global_device_ids=true, to_apply=%region_19.0 | all-reduce | flops 1 | bytes 8 | tf_op jit(solution)/shard_map/psum | solution.py:120
  526.0 43.1 %all-reduce.47 = (f32[]{:T(128)}, f32[]{:T(128)}) all-reduce(f32[]{:T(128)} %get-tuple-element.18, f32[]{:T(128)} %get-tuple-element.17), channel_id=1, replica_groups=mesh['groups'=1,'slab'=32] {'slab'}, use_global_device_ids=true, to_apply=%region_27.28 | all-reduce | flops 2 | bytes 16 | tf_op jit(solution)/shard_map/psum | solution.py:65
  571.0 39.6 %psum.208 = f32[]{:T(128)} all-reduce(f32[]{:T(128)} %multiply_reduce_fusion.21), channel_id=1, replica_groups=mesh['groups'=1,'slab'=32] {'slab'}, use_global_device_ids=true, to_apply=%region_31.32 | all-reduce | flops 1 | bytes 8 | tf_op jit(solution)/shard_map/psum | solution.py:65
  617.9 44.0 %psum.209 = f32[]{:T(128)} all-reduce(f32[]{:T(128)} %multiply_reduce_fusion.20), channel_id=1, replica_groups=mesh['groups'=1,'slab'=32] {'slab'}, use_global_device_ids=true, to_apply=%region_33.34 | all-reduce | flops 1 | bytes 8 | tf_op jit(solution)/shard_map/psum | solution.py:166
  664.0 39.4 %psum.210 = f32[]{:T(128)} all-reduce(f32[]{:T(128)} %get-tuple-element.37), channel_id=1, replica_groups=mesh['groups'=1,'slab'=32] {'slab'}, use_global_device_ids=true, to_apply=%region_35.36 | all-reduce | flops 1 | bytes 8 | tf_op jit(solution)/shard_map/psum | solution.py:65
  710.6 44.3 %psum.211 = f32[]{:T(128)} all-reduce(f32[]{:T(128)} %multiply_reduce_fusion.18), channel_id=1, replica_groups=mesh['groups'=1,'slab'=32] {'slab'}, use_global_device_ids=true, to_apply=%region_37.38 | all-reduce | flops 1 | bytes 8 | tf_op jit(solution)/shard_map/psum | solution.py:166
  803.6 44.1 %psum.213 = f32[]{:T(128)} all-reduce(f32[]{:T(128)} %multiply_reduce_fusion.16), channel_id=1, replica_groups=mesh['groups'=1,'slab'=32] {'slab'}, use_global_device_ids=true, to_apply=%region_41.42 | all-reduce | flops 1 | bytes 8 | tf_op jit(solution)/shard_map/psum | solution.py:166
  849.7 39.8 %psum.214 = f32[]{:T(128)} all-reduce(f32[]{:T(128)} %get-tuple-element.33), channel_id=1, replica_groups=mesh['groups'=1,'slab'=32] {'slab'}, use_global_device_ids=true, to_apply=%region_43.44 | all-reduce | flops 1 | bytes 8 | tf_op jit(solution)/shard_map/psum | solution.py:65
  896.7 44.0 %psum.215 = f32[]{:T(128)} all-reduce(f32[]{:T(128)} %multiply_reduce_fusion.14), channel_id=1, replica_groups=mesh['groups'=1,'slab'=32] {'slab'}, use_global_device_ids=true, to_apply=%region_45.46 | all-reduce | flops 1 | bytes 8 | tf_op jit(solution)/shard_map/psum | solution.py:166
  942.8 39.6 %psum.216 = f32[]{:T(128)} all-reduce(f32[]{:T(128)} %get-tuple-element.31), channel_id=1, replica_groups=mesh['groups'=1,'slab'=32] {'slab'}, use_global_device_ids=true, to_apply=%region_47.48 | all-reduce | flops 1 | bytes 8 | tf_op jit(solution)/shard_map/psum | solution.py:65
  990.1 44.1 %psum.217 = f32[]{:T(128)} all-reduce(f32[]{:T(128)} %multiply_reduce_fusion.12), channel_id=1, replica_groups=mesh['groups'=1,'slab'=32] {'slab'}, use_global_device_ids=true, to_apply=%region_49.50 | all-reduce | flops 1 | bytes 8 | tf_op jit(solution)/shard_map/psum | solution.py:166
  1036.2 40.0 %psum.218 = f32[]{:T(128)} all-reduce(f32[]{:T(128)} %get-tuple-element.29), channel_id=1, replica_groups=mesh['groups'=1,'slab'=32] {'slab'}, use_global_device_ids=true, to_apply=%region_51.52 | all-reduce | flops 1 | bytes 8 | tf_op jit(solution)/shard_map/psum | solution.py:65
  1083.5 44.1 %psum.219 = f32[]{:T(128)} all-reduce(f32[]{:T(128)} %get-tuple-element.27), channel_id=1, replica_groups=mesh['groups'=1,'slab'=32] {'slab'}, use_global_device_ids=true, to_apply=%region_53.54 | all-reduce | flops 1 | bytes 8 | tf_op jit(solution)/shard_map/psum | solution.py:166
  1129.6 39.4 %psum.220 = f32[]{:T(128)} all-reduce(f32[]{:T(128)} %multiply_reduce_fusion.9), channel_id=1, replica_groups=mesh['groups'=1,'slab'=32] {'slab'}, use_global_device_ids=true, to_apply=%region_55.56 | all-reduce | flops 1 | bytes 8 | tf_op jit(solution)/shard_map/psum | solution.py:65
  1176.3 44.0 %psum.221 = f32[]{:T(128)} all-reduce(f32[]{:T(128)} %fusion.42), channel_id=1, replica_groups=mesh['groups'=1,'slab'=32] {'slab'}, use_global_device_ids=true, to_apply=%region_57.58 | all-reduce | flops 1 | bytes 8 | tf_op jit(solution)/shard_map/psum | solution.py:166
  1225.5 39.5 %all-reduce.46 = (f32[5]{0:T(128)S(1)}, f32[5,5]{0,1:T(8,128)S(1)}) all-reduce(f32[5]{0:T(128)S(1)} %convolution_bitcast_fusion.1, f32[5,5]{0,1:T(8,128)S(1)} %convolution_bitcast_fusion), channel_id=1, replica_groups=mesh['groups'=1,'slab'=32] {'slab'}, use_global_device_ids=true, to_apply=%region_58.59 | all-reduce | flops 30 | bytes 240 | tf_op jit(solution)/shard_map/psum | solution.py:180
  (238 shorter events, 246.7 us)
Async XLA Ops:
  1.8 38.0 %collective-permute-start = (f32[3,1,64,256]{3,2,1,0:T(8,128)S(1)}, f32[3,1,64,256]{3,2,1,0:T(8,128)S(1)}, u32[]{:S(2)}, u32[]{:S(2)}) collective-permute-start(f32[3,1,64,256]{3,2,1,0:T(8,128)S(1)} %get-tuple-element.64), channel_id=1, source_target_pairs={{1,0},{2,1},{3,2},{4,3},{5,4},{6,5},{7,6},{8,7},{9,8},{10,9},{11,1... | collective-permute-start | bytes 589832 | tf_op jit(solution)/shard_map/ppermute | solution.py:26
  3.1 36.7 %collective-permute-start.1 = (f32[3,1,64,256]{3,2,1,0:T(8,128)S(1)}, f32[3,1,64,256]{3,2,1,0:T(8,128)S(1)}, u32[]{:S(2)}, u32[]{:S(2)}) collective-permute-start(f32[3,1,64,256]{3,2,1,0:T(8,128)S(1)} %get-tuple-element.65), channel_id=1, source_target_pairs={{0,1},{1,2},{2,3},{3,4},{4,5},{5,6},{6,7},{7,8},{8,9},{9,10},{10,1... | collective-permute-start | bytes 589832 | tf_op jit(solution)/shard_map/ppermute | solution.py:24
  23.7 462.8 %all-to-all-start = ((s32[32,1,32]{2,1,0:T(1,128)}), s32[32,1,32]{2,1,0:T(1,128)S(1)}, u32[]{:S(2)}, u32[]{:S(2)}) async-start(s32[32,1,32]{2,1,0:T(1,128)} %all_to_all.15), calls=%async_computation | async-start | bytes 32768 | tf_op jit(solution)/shard_map/all_to_all | solution.py:150
  33.5 486.5 %collective-permute-start.14 = (f32[3,1,1024]{2,1,0:T(1,128)S(1)}, f32[3,1,1024]{2,1,0:T(1,128)S(1)}, u32[]{:S(2)}, u32[]{:S(2)}) collective-permute-start(f32[3,1,1024]{2,1,0:T(1,128)S(1)} %get-tuple-element.136), channel_id=1, source_target_pairs={{1,0},{2,1},{3,2},{4,3},{5,4},{6,5},{7,6},{8,7},{9,8},{10,9},{11,1... | collective-permute-start | bytes 36872 | tf_op jit(solution)/shard_map/ppermute | solution.py:26
  34.8 485.2 %collective-permute-start.15 = (f32[3,1,1024]{2,1,0:T(1,128)S(1)}, f32[3,1,1024]{2,1,0:T(1,128)S(1)}, u32[]{:S(2)}, u32[]{:S(2)}) collective-permute-start(f32[3,1,1024]{2,1,0:T(1,128)S(1)} %get-tuple-element.137), channel_id=1, source_target_pairs={{0,1},{1,2},{2,3},{3,4},{4,5},{5,6},{6,7},{7,8},{8,9},{9,10},{10,1... | collective-permute-start | bytes 36872 | tf_op jit(solution)/shard_map/ppermute | solution.py:24
  40.5 5.5 collective-permute-start.2
  41.8 4.9 collective-permute-start.3
  47.0 6.1 collective-permute-start.4
  48.3 5.6 collective-permute-start.5
  148.6 4.5 collective-permute-start.6
  149.9 3.9 collective-permute-start.7
  242.6 4.5 collective-permute-start.8
  336.1 4.5 collective-permute-start.10
  429.9 4.5 collective-permute-start.12
  486.5 11.6 all-to-all-start.1
  520.1 4.4 collective-permute-start.16
  612.1 4.4 collective-permute-start.18
  704.8 4.4 collective-permute-start.20
  797.7 4.4 collective-permute-start.22
  890.9 4.4 collective-permute-start.24
  983.8 4.6 collective-permute-start.26
  985.1 4.0 collective-permute-start.27
  1077.7 4.4 collective-permute-start.28
  1170.4 4.7 collective-permute-start.30
  (23 other events, 1815.3 us)
where the time goes:
time: 1330 us; the launch traced here: 1320 us
  blocking collectives  1070 us (80%)
  starting transfers between devices  85.5 us (6%)
  between operations  56.6 us (4%)
  other arithmetic  51.2 us (4%)
  local copies, waits for them, and re-layouts  37.9 us (3%)
  waiting for transfers between devices  15.7 us (1%)
    psum x11, blocking collectives, on_device(): step_size = norm_now / lax.psum(jnp.sum(direction * image), 'slab')  487 us
    psum x8, blocking collectives, shell_total(): return lax.psum(value, 'slab')  320 us
    psum x5, blocking collectives, pressure_total(): return lax.psum(value, 'slab')  210 us
    ppermute x16, starting transfers between devices, with_halo(): lax.ppermute(tail, axis, [(i, (i + 1) % count) for i in range(ends)])  51.6 us
    psum x1, blocking collectives, on_device(): gram, target = lax.psum((gram_local, target_local), 'slab')  39.5 us
  transfers between devices with their start and end apart: 34, of which 15 were waited for; matrix products, arithmetic and copies ran while one was open for 4% of the time, Pallas kernels for 0%

commit v1 on v0

v1 whole, which is shorter than its diff:
```python
import jax
import jax.numpy as jnp
from jax import lax
from jax.experimental import pallas as pl
from jax.experimental.pallas import tpu as pltpu
from jax.sharding import PartitionSpec as P

CAP = 32
PITERS = 5
SITERS = 8

NU = 0.15
MU = 0.5
WALL = 4.0

P_SHIFT, P_BACK = (4.93, 7.29, 5.13, 7.05, 5.38), (10.17, 6.01, 8.86, 8.24)
S_SHIFT = (5.7, 5.09, 4.26, 4.26, 4.08, 4.17, 4.1, 4.18)
S_BACK = (2.53, 3.17, 4.07, 3.95, 4.22, 4.01, 4.14)
TINY = 1e-7

VMEM = pl.BlockSpec(memory_space=pltpu.VMEM)
F32 = jnp.float32
BF16 = jnp.bfloat16

H2_AT, ROW_AT, DISP_AT, HALO_ROWS = 128, 256, 264, 288
SHELL_AT, FIELD_ROWS = 512, 704


def call(kernel, outs, args, scratch=(), flops=1000000, limit=48):
    return pl.pallas_call(
        kernel,
        out_shape=outs,
        in_specs=[VMEM] * len(args),
        out_specs=jax.tree.map(lambda _: VMEM, outs),
        scratch_shapes=list(scratch),
        compiler_params=pltpu.CompilerParams(vmem_limit_bytes=limit * 1024 * 1024),
        cost_estimate=pl.CostEstimate(flops=flops, bytes_accessed=1000000, transcendentals=0),
    )(*args)


def shape(*dims, dtype=F32):
    return jax.ShapeDtypeStruct(dims, dtype)


def at(values, axis):
    return lax.broadcasted_iota(jnp.int32, values.shape, axis)


def ahead(values, axis):
    size = values.shape[axis]
    return jnp.where(at(values, axis) == size - 1, 0.0, pltpu.roll(values, size - 1, axis))


def behind(values, axis):
    return jnp.where(at(values, axis) == 0, 0.0, pltpu.roll(values, 1, axis))


def plane_sum(plane):
    return ahead(plane, 0) + behind(plane, 0) + ahead(plane, 1) + behind(plane, 1)


def difference(plane, axis):
    return ahead(plane, axis) - behind(plane, axis)


def halves(ref, start):
    return jnp.concatenate([ref[start : start + 64, :], ref[start + 64 : start + 128, :]], axis=1)


def put_halves(ref, start, plane):
    ref[start : start + 64, :] = plane[:, :128]
    ref[start + 64 : start + 128, :] = plane[:, 128:]


def parts(values, count):
    pieces = []
    for _ in range(count - 1):
        piece = values.astype(BF16)
        pieces.append(piece)
        values = values - piece.astype(F32)
    pieces.append(values.astype(BF16))
    return pieces


def dot(left, right, transposed=False):
    dims = (((1,), (1 if transposed else 0,)), ((), ()))
    return lax.dot_general(left, right, dims, preferred_element_type=F32)


def split_dot(left, right, count, transposed=False):
    rows = left.shape[0]
    product = dot(jnp.concatenate(parts(left, count), 0), right, transposed)
    return sum(product[i * rows : (i + 1) * rows] for i in range(count))


def fluid_kernel(velocity, displacement, to_left, to_right, source, wall):
    layers = velocity.shape[1]
    last = layers - 1
    field = [[velocity[c, x] for x in range(layers)] for c in range(3)]
    own = [[(1.0 - 6.0 * NU) * f + NU * plane_sum(f) for f in rows] for rows in field]
    spread = {
        x: NU * (difference(field[1][x], 0) + difference(field[2][x], 1)) for x in (0, last)
    }
    put_halves(to_left, 0, own[0][0] + NU * field[0][1] + spread[0])
    put_halves(to_left, H2_AT, NU * field[0][0])
    put_halves(to_right, 0, spread[last] - own[0][last] - NU * field[0][last - 1])
    put_halves(to_right, H2_AT, NU * field[0][last])
    for ref, x, row in ((to_left, 0, 0), (to_right, last, 7)):
        edge = (MU * NU) * (velocity[2, x, 1:2, :] - velocity[2, x, 0:1, :])
        ref[ROW_AT : DISP_AT, :] = jnp.zeros((8, 128), F32)
        ref[ROW_AT : ROW_AT + 1, :] = edge[:, :128]
        ref[ROW_AT + 1 : ROW_AT + 2, :] = edge[:, 128:]
        ref[ROW_AT + 2 : ROW_AT + 3, :] = jnp.ones((1, 128), F32)
        for c in range(3):
            for k in range(8):
                place = DISP_AT + c * 8 + k
                ref[place : place + 1, :] = displacement[c, row : row + 1, k * 128 : k * 128 + 128]
    zero = jnp.zeros_like(field[0][0])
    predicted = [
        [
            own[c][x]
            + NU
            * (
                (field[c][x + 1] if x < last else zero)
                + (field[c][x - 1] if x > 0 else zero)
            )
            for x in range(layers)
        ]
        for c in range(3)
    ]
    for x in range(layers):
        after = predicted[0][x + 1] if x < last else zero
        before = predicted[0][x - 1] if x > 0 else zero
        source[x] = -0.5 * (
            after - before + difference(predicted[1][x], 0) + difference(predicted[2][x], 1)
        )
        wall[x : x + 1, :] = MU * (predicted[0][x][1:2, :] - predicted[0][x][0:1, :])
        wall[4 + x : 5 + x, :] = MU * (predicted[2][x][1:2, :] - predicted[2][x][0:1, :])


def shell_beside(field):
    return ahead(field, 0) + behind(field, 0) + ahead(field, 1) + behind(field, 1)


def source_kernel(
    source, wall, to_left, to_right, from_left, from_right, displacement, load, stiffness, fields, first, wall_out
):
    layers = source.shape[0]
    last = layers - 1
    left1, left2 = halves(from_left, 0), halves(from_left, H2_AT)
    right1, right2 = halves(from_right, 0), halves(from_right, H2_AT)
    has_left = from_left[ROW_AT + 2 : ROW_AT + 3, 0:1]
    has_right = from_right[ROW_AT + 2 : ROW_AT + 3, 0:1]
    left1 = left1 - has_left * halves(to_left, H2_AT)
    right1 = right1 + has_right * halves(to_right, H2_AT)
    for x in range(layers):
        plane = source[x]
        if x == 0:
            plane = plane - 0.5 * left1
        if x == 1:
            plane = plane + 0.5 * left2
        if x == last - 1:
            plane = plane - 0.5 * right2
        if x == last:
            plane = plane - 0.5 * right1
        put_halves(fields, x * 128, plane)
        if x == 0:
            put_halves(first, 0, plane)
    wall_out[...] = wall[...]
    for x, ref, plane in ((0, from_left, left2), (last, from_right, right2)):
        edge = jnp.concatenate([ref[ROW_AT : ROW_AT + 1, :], ref[ROW_AT + 1 : ROW_AT + 2, :]], 1)
        wall_out[x : x + 1, :] = wall[x : x + 1, :] + MU * (plane[1:2, :] - plane[0:1, :])
        wall_out[4 + x : 5 + x, :] = wall[4 + x : 5 + x, :] + edge
    for c in range(3):
        field = displacement[c]
        above = jnp.concatenate(
            [from_left[DISP_AT + c * 8 + k : DISP_AT + c * 8 + k + 1, :] for k in range(8)], 1
        )
        below = jnp.concatenate(
            [from_right[DISP_AT + c * 8 + k : DISP_AT + c * 8 + k + 1, :] for k in range(8)], 1
        )
        row = at(field, 0)
        beside = jnp.where(row == 0, above, pltpu.roll(field, 1, 0))
        beside = beside + jnp.where(row == 7, below, pltpu.roll(field, 7, 0))
        beside = beside + ahead(field, 1) + behind(field, 1)
        start = load[c] - ((4.0 + stiffness[...]) * field - beside)
        for k in range(8):
            place = SHELL_AT + (c * 8 + k) * 8
            fields[place : place + 8, :] = start[:, k * 128 : k * 128 + 128]


def slots_kernel(owner, slots, *, ranks):
    width = owner.shape[1]
    down = lax.broadcasted_iota(jnp.int32, (width, width), 0)
    across = lax.broadcasted_iota(jnp.int32, (width, width), 1)
    earlier = jnp.where(down < across, 1.0, 0.0).astype(BF16)
    rank = lax.broadcasted_iota(jnp.int32, (ranks, width), 0)
    seen = jnp.zeros((ranks, 1), F32)
    for x in range(owner.shape[0]):
        member = jnp.where(rank == owner[x : x + 1, :], 1.0, 0.0)
        before = dot(member.astype(BF16), earlier) + seen
        slots[x : x + 1, :] = jnp.sum(before * member, 0, keepdims=True).astype(jnp.int32)
        seen = seen + jnp.sum(member, 1, keepdims=True)


def fold(product):
    rows, columns = product.shape
    tall = product[0:8]
    for a in range(1, rows // 8):
        tall = tall + product[a * 8 : a * 8 + 8]
    total = tall[:, :128]
    for b in range(1, columns // 128):
        total = total + tall[:, b * 128 : b * 128 + 128]
    return total


def whole(tile):
    return jnp.sum(jnp.sum(tile, 0, keepdims=True), 1, keepdims=True)


def place_pair(tile, i, j, value):
    row, lane = at(tile, 0), at(tile, 1)
    here = (row == i) & (lane == j[0])
    if j[1] is not None:
        here = here | ((row == j[1]) & (lane == j[2]))
    return jnp.where(here, value, tile)


def pressure_kernel(
    own, left, right, beyond, shift, shift_left, shift_right,
    wall, owner, slots, node, weight,
    payload, basis, work, diagonal, off, *, ranks,
):
    layers = shift.shape[0]
    for x in range(layers):
        work[0, x] = halves(left, x * 128)
        work[0, x + 4] = halves(own, x * 128)
        work[0, x + 8] = halves(right, x * 128)
    work[0, 12] = halves(beyond, 0)
    for x in range(1, 12):
        ref = (shift_left, shift, shift_right)[x // 4]
        values = ref[x % 4]
        inside = values > 0.0
        diagonal[x] = jnp.where(inside, values + 6.0, 0.0)
        off[x] = jnp.where(inside, 1.0, 0.0)
    for step in range(1, PITERS):
        for x in range(step, 13 - step):
            now = work[step - 1, x]
            beside = work[step - 1, x - 1] + work[step - 1, x + 1] + plane_sum(now)
            if x < 4 or x >= 8:
                beside = off[x] * beside
            value = (diagonal[x] - P_SHIFT[step - 1]) * now - beside
            if step > 1:
                value = value - P_BACK[step - 2] * work[step - 2, x]
            work[step, x] = value
    tile = jnp.zeros((8, 128), F32)
    for i in range(PITERS):
        for j in range(i, PITERS):
            total = sum(work[i, x] * work[j, x] for x in range(4, 8))
            value = whole(fold(total))
            tile = place_pair(tile, 3 + i, (96 + j, 3 + j, 96 + i), value)
    top = PITERS - 1
    total = 0.0
    for x in range(4, 8):
        now = work[top, x]
        image = (6.0 + shift[x - 4]) * now - plane_sum(now) - 2.0 * work[top, x + 1]
        total = total + now * image
    tile = place_pair(tile, 3 + top, (96 + PITERS, None, None), whole(fold(total)))
    for k in range(PITERS):
        for x in range(layers):
            basis[k, x] = work[k, x + 4]
    lanes = lax.broadcasted_iota(jnp.int32, (128, 256), 0)
    field_row = lax.broadcasted_iota(jnp.int32, (8, 256), 0)
    packed = jnp.zeros((ranks * 8, 128), F32)
    weights = jnp.zeros((ranks * 8, 128), F32)
    for x in range(layers):
        scale = weight[x : x + 1, :].astype(F32)
        rows = [wall[x : x + 1, :] * scale, wall[4 + x : 5 + x, :] * scale]
        rows.append(node[x : x + 1, :].astype(F32))
        rows += [work[k, x + 4][0:1, :] * scale for k in range(PITERS)]
        values = jnp.concatenate(rows, 0)
        who = owner[x : x + 1, :]
        here = jnp.where((lanes & 31) == slots[x : x + 1, :], 1.0, 0.0)
        place = jnp.where(lanes < 96, here, 0.0).astype(BF16)
        end = jnp.where(lanes >= 96, here, 0.0).astype(BF16)
        left_rows = jnp.concatenate([jnp.where(who == d, values, 0.0) for d in range(ranks)], 0)
        packed = packed + split_dot(left_rows, place, 3, True)
        weight_rows = jnp.concatenate(
            [
                jnp.where((who == d - 1 + field_row) & (field_row < 3), scale, 0.0)
                for d in range(ranks)
            ],
            0,
        )
        weights = weights + dot(weight_rows.astype(BF16), end, True)
    lane = lax.broadcasted_iota(jnp.int32, (8, 128), 1)
    zero = jnp.zeros((8, 128), F32)
    for d in range(ranks):
        mine = packed[d * 8 : d * 8 + 8]
        before = packed[d * 8 - 8 : d * 8] if d > 0 else zero
        after = packed[d * 8 + 8 : d * 8 + 16] if d < ranks - 1 else zero
        block = jnp.where(lane < 32, before, jnp.where(lane < 64, mine, after))
        block = jnp.where(lane < 96, block, 0.0) + weights[d * 8 : d * 8 + 8]
        payload[d] = block + tile


def row_of(matrix, k):
    return jnp.sum(jnp.where(at(matrix, 0) == k, matrix, 0.0), 0, keepdims=True)


def column_of(matrix, k):
    return jnp.sum(jnp.where(at(matrix, 1) == k, matrix, 0.0), 1, keepdims=True)


def as_column(row, matrix, shift):
    spread = jnp.broadcast_to(row, matrix.shape)
    return jnp.sum(jnp.where(at(matrix, 1) == at(matrix, 0) - shift, spread, 0.0), 1, keepdims=True)


def eliminate(matrix, first_row, first_lane, count):
    row_at = at(matrix, 0)
    start = matrix
    for k in range(count):
        row = row_of(matrix, first_row + k)
        column = column_of(matrix, first_lane + k)
        pivot = column_of(row, first_lane + k)
        scale = column_of(row_of(start, first_row + k), first_lane + k)
        good = pivot > TINY * scale
        inverse = jnp.where(good, 1.0 / jnp.where(good, pivot, 1.0), 0.0)
        row = row * inverse
        matrix = jnp.where(row_at == first_row + k, row, matrix - column * row)
    return matrix


def galerkin(gram, first_row, shifts, back, energy):
    count = len(shifts)
    lane, row = at(gram, 1), at(gram, 0)
    shift, prior = 0.0, 0.0
    for k in range(count):
        shift = jnp.where(lane == k, shifts[k], shift)
    for k in range(1, count):
        prior = jnp.where(lane == k, back[k - 1], prior)
    image = shift * gram + pltpu.roll(gram, 127, 1) + prior * pltpu.roll(gram, 1, 1)
    last = as_column(row_of(image, first_row + count - 1), gram, first_row)
    last = jnp.where(row == first_row + count - 1, energy, last)
    image = jnp.where(lane == count - 1, last, image)
    image = jnp.where(lane == count, column_of(gram, 0), image)
    inside = (row >= first_row) & (row < first_row + count) & (lane <= count)
    return jnp.where(inside, image, 0.0)


def shell_kernel(
    received, own, left, right, stiffness, stiffness_left, stiffness_right,
    displacement, residual_prev, solved_prev, residual_history, solved_history,
    payload, basis, factors, work, diagonal, off, table, *, ranks,
):
    lane8 = lax.broadcasted_iota(jnp.int32, (8, 128), 1)
    summed = received[0]
    for p in range(1, ranks):
        summed = summed + received[p]
    gram = pltpu.roll(jnp.where(lane8 >= 96, summed, 0.0), 32, 1)
    energy = jnp.sum(
        jnp.where((at(gram, 0) == 3 + PITERS - 1) & (lane8 == PITERS), gram, 0.0), keepdims=True
    )
    system = galerkin(gram, 3, P_SHIFT, P_BACK, energy)
    solved = column_of(eliminate(system, 3, 0, PITERS), PITERS)
    solved = jnp.where(lax.broadcasted_iota(jnp.int32, (8, 1), 0) >= 3, solved, 0.0)
    factors[...] = jnp.broadcast_to(solved, (8, 128))
    groups = [lane8 // 32 == q for q in range(4)]

    def gathered(j):
        chunks = []
        for k in range(ranks // 4):
            chunk = jnp.zeros((8, 128), F32)
            for q in range(4):
                chunk = jnp.where(
                    groups[q], pltpu.roll(received[4 * k + q], (32 * (q - j)) % 128, 1), chunk
                )
            chunks.append(chunk)
        return jnp.concatenate(chunks, 1)

    weights = gathered(3)
    entries = ranks * CAP
    target = lax.broadcasted_iota(jnp.int32, (64, entries), 0)
    low = lax.broadcasted_iota(jnp.int32, (128, entries), 0)
    node = None
    for j in range(3):
        values = gathered(j)
        numbers = values[2:3, :].astype(jnp.int32)
        if j == 1:
            node = numbers
        rows = (
            values[0:1, :],
            WALL * jnp.sum(values * solved, 0, keepdims=True),
            values[1:2, :],
        )
        code = ((numbers >> 7) & 7) * 8 + (numbers >> 10)
        spot = jnp.where(low == (numbers & 127), 1.0, 0.0).astype(BF16)
        match = target == code
        scattered = split_dot(
            jnp.concatenate([jnp.where(match, row, 0.0) for row in rows], 0), spot, 3, True
        )
        share = dot(jnp.where(match, weights[j : j + 1, :], 0.0).astype(BF16), spot, True)
        share = 1.0 / jnp.maximum(share, 1.0)
        ref = (left, own, right)[j]
        for c in range(3):
            force = scattered[c * 64 : c * 64 + 64] * share
            for k in range(8):
                place = SHELL_AT + (c * 8 + k) * 8
                work[0, c * 24 + j * 8 : c * 24 + j * 8 + 8, k * 128 : k * 128 + 128] = (
                    force[k * 8 : k * 8 + 8] + ref[place : place + 8, :]
                )
        stiff = (stiffness_left, stiffness, stiffness_right)[j][...]
        inside = stiff > 0.0
        main = jnp.where(inside, stiff + 4.0, 0.0)
        side = jnp.where(inside, 1.0, 0.0)
        for c in range(3):
            diagonal[c * 24 + j * 8 : c * 24 + j * 8 + 8, :] = main
            off[c * 24 + j * 8 : c * 24 + j * 8 + 8, :] = side
    for step in range(1, SITERS):
        now = work[step - 1]
        value = (diagonal[...] - S_SHIFT[step - 1]) * now - off[...] * shell_beside(now)
        if step > 1:
            value = value - S_BACK[step - 2] * work[step - 2]
        work[step] = value
    def basis_tile(k, c):
        return work[k, c * 24 + 8 : c * 24 + 16, :]

    vectors = [lambda c, k=k: basis_tile(k, c) for k in range(SITERS)]
    vectors.append(lambda c: residual_prev[c])
    vectors += [lambda c, k=k: residual_history[k, c] for k in range(residual_history.shape[0])]
    tile = jnp.zeros((16, 128), F32)
    for i in range(len(vectors)):
        for j in range(i, len(vectors)):
            total = sum(vectors[i](c) * vectors[j](c) for c in range(3))
            tile = place_pair(tile, i, (96 + j, j, 96 + i), whole(fold(total)))
    top = SITERS - 1
    total = 0.0
    for c in range(3):
        now = basis_tile(top, c)
        after = work[top, c * 24 + 9 : c * 24 + 17, :]
        image = (4.0 + stiffness[...]) * now - ahead(now, 1) - behind(now, 1) - 2.0 * after
        total = total + now * image
    tile = place_pair(tile, 13, (96 + 13, None, None), whole(fold(total)))
    for k in range(SITERS):
        for c in range(3):
            basis[k, c] = basis_tile(k, c)
    fields = vectors[:SITERS] + [lambda c: displacement[c]]
    fields += [lambda c, k=k: solved_history[k, c] for k in range(solved_history.shape[0])]
    fields.append(lambda c: solved_prev[c])
    for c in range(3):
        for f in range(16):
            value = fields[f](c) if f < len(fields) else jnp.zeros((8, 1024), F32)
            for k in range(8):
                table[k, pl.ds(c * 16 + f, 8, stride=48), :] = value[:, k * 128 : k * 128 + 128]
    column = lax.broadcasted_iota(jnp.int32, (1024, entries), 0)
    pick = jnp.where(column == (node & 1023), 1.0, 0.0).astype(BF16)
    found = split_dot(jnp.concatenate([table[k] for k in range(8)], 1), pick, 3)
    line = node >> 10
    answer = jnp.zeros((48, entries), F32)
    for r in range(8):
        answer = jnp.where(line == r, found[r * 48 : r * 48 + 48], answer)
    lane16 = lax.broadcasted_iota(jnp.int32, (16, 128), 1)
    for p in range(ranks):
        k = p // 4
        block = tile
        for c in range(3):
            piece = answer[c * 16 : c * 16 + 16, k * 128 : k * 128 + 128]
            block = jnp.where(
                lane16 // 32 == c, pltpu.roll(piece, (32 * (c - p % 4)) % 128, 1), block
            )
        payload[p] = block


def combine_kernel(basis, factors, pressure):
    for x in range(pressure.shape[0]):
        total = 0.0
        for k in range(PITERS):
            total = total + factors[3 + k : 4 + k, 0:1] * basis[k, x]
        pressure[x] = total


def update_kernel(
    received, basis, displacement, solved_prev, solved_history, owner, slots,
    new_displacement, wall, *, ranks,
):
    summed = received[0]
    for p in range(1, ranks):
        summed = summed + received[p]
    lane, row = at(summed, 1), at(summed, 0)
    gram = pltpu.roll(jnp.where(lane >= 96, summed, 0.0), 32, 1)
    energy = jnp.sum(jnp.where((row == 13) & (lane == 13), gram, 0.0), keepdims=True)
    system = galerkin(gram, 0, S_SHIFT, S_BACK, energy)
    steps = column_of(eliminate(system, 0, 0, SITERS), SITERS)
    down = lax.broadcasted_iota(jnp.int32, (16, 1), 0)
    steps = jnp.where(down < SITERS, steps, 0.0)
    base, count = SITERS, 1 + solved_history.shape[0]
    with_moved = jnp.sum(gram * steps, 0, keepdims=True)
    with_newest = with_moved - row_of(gram, base)
    steps_row = jnp.sum(jnp.where(row == lane, jnp.broadcast_to(steps, gram.shape), 0.0), 0, keepdims=True)
    newest_moved = jnp.sum(steps_row * with_newest, 1, keepdims=True)
    newest_newest = newest_moved - column_of(with_newest, base)
    block = jnp.where(row == base, with_newest, gram)
    block = jnp.where(lane == base, as_column(with_newest, gram, 0), block)
    block = jnp.where((row == base) & (lane == base), newest_newest, block)
    right = jnp.where(down == base, newest_moved, as_column(with_moved, gram, 0))
    block = jnp.where(lane == base + count, right, block)
    inside = (row >= base) & (row < base + count) & (lane >= base) & (lane <= base + count)
    block = jnp.where(inside, block, 0.0)
    coefficients = -column_of(eliminate(block, base, base, count), base + count)
    newest = row_of(coefficients, base)
    factors = jnp.where(
        down < base,
        (1.0 + newest) * steps,
        jnp.where(
            down == base,
            1.0 + newest,
            jnp.where(down < base + count, coefficients, jnp.where(down == base + count, -newest, 0.0)),
        ),
    )
    for c in range(3):
        total = row_of(factors, base) * displacement[c]
        for k in range(SITERS):
            total = total + row_of(factors, k) * basis[k, c]
        for k in range(count - 1):
            total = total + row_of(factors, base + 1 + k) * solved_history[k, c]
        total = total + row_of(factors, base + count) * solved_prev[c]
        new_displacement[c] = total
    answers = jnp.concatenate(
        [jnp.sum(received[p] * factors, 0, keepdims=True) for p in range(ranks)], 0
    )
    group = at(answers, 1) // 32
    stacked = jnp.concatenate([jnp.where(group == c, answers, 0.0) for c in range(3)], 0)
    slot_row = lax.broadcasted_iota(jnp.int32, (128, 256), 0) & 31
    rank = lax.broadcasted_iota(jnp.int32, (ranks, 256), 0)
    for x in range(owner.shape[0]):
        pick = jnp.where(slot_row == slots[x : x + 1, :], 1.0, 0.0).astype(BF16)
        spread = split_dot(stacked, pick, 3)
        mine = rank == owner[x : x + 1, :]
        for c in range(3):
            wall[c : c + 1, x * 256 : x * 256 + 256] = jnp.sum(
                jnp.where(mine, spread[c * ranks : (c + 1) * ranks], 0.0), 0, keepdims=True
            )


def on_device(
    velocity,
    pressure_shift,
    owner_rank,
    node_index,
    map_weight,
    shell_load,
    shell_stiffness,
    displacement,
    residual_prev,
    solved_prev,
    residual_history,
    solved_history,
):
    ranks = lax.axis_size("slab")
    layers = velocity.shape[1]
    kept = residual_history.shape[0]

    def leftward(values, by=1):
        return lax.ppermute(values, "slab", [(i, i - by) for i in range(by, ranks)])

    def rightward(values):
        return lax.ppermute(values, "slab", [(i, i + 1) for i in range(ranks - 1)])

    owner = owner_rank.reshape(layers, -1)
    node = node_index.reshape(layers, -1)
    weight = map_weight.reshape(layers, -1)

    to_left, to_right, source, wall = call(
        fluid_kernel,
        (shape(HALO_ROWS, 128), shape(HALO_ROWS, 128), shape(*velocity.shape[1:]), shape(8, 256)),
        (velocity, displacement),
    )
    from_right, from_left = leftward(to_left), rightward(to_right)
    shift_right, shift_left = leftward(pressure_shift), rightward(pressure_shift)
    stiffness_right, stiffness_left = leftward(shell_stiffness), rightward(shell_stiffness)
    (slots,) = call(
        lambda *refs: slots_kernel(*refs, ranks=ranks),
        (shape(layers, 256, dtype=jnp.int32),),
        (owner,),
    )
    fields, first, wall = call(
        source_kernel,
        (shape(FIELD_ROWS, 128), shape(128, 128), shape(8, 256)),
        (source, wall, to_left, to_right, from_left, from_right, displacement, shell_load, shell_stiffness),
    )
    fields_right, fields_left = leftward(fields), rightward(fields)
    beyond = leftward(first, 2)
    payload, pressure_basis = call(
        lambda *refs: pressure_kernel(*refs, ranks=ranks),
        (shape(ranks, 8, 128), shape(PITERS, *pressure_shift.shape)),
        (
            fields, fields_left, fields_right, beyond,
            pressure_shift, shift_left, shift_right,
            wall, owner, slots, node, weight,
        ),
        scratch=(
            pltpu.VMEM((PITERS, 13, 64, 256), F32),
            pltpu.VMEM((12, 64, 256), F32),
            pltpu.VMEM((12, 64, 256), F32),
        ),
    )
    received = lax.all_to_all(payload, "slab", split_axis=0, concat_axis=0, tiled=True)
    payload, shell_basis, factors = call(
        lambda *refs: shell_kernel(*refs, ranks=ranks),
        (shape(ranks, 16, 128), shape(SITERS, *displacement.shape), shape(8, 128)),
        (
            received, fields, fields_left, fields_right,
            shell_stiffness, stiffness_left, stiffness_right,
            displacement, residual_prev, solved_prev, residual_history, solved_history,
        ),
        scratch=(
            pltpu.VMEM((SITERS, 72, 1024), F32),
            pltpu.VMEM((72, 1024), F32),
            pltpu.VMEM((72, 1024), F32),
            pltpu.VMEM((8, 8 * 48, 128), F32),
        ),
    )
    answers = lax.all_to_all(payload, "slab", split_axis=0, concat_axis=0, tiled=True)
    (pressure,) = call(combine_kernel, (shape(*pressure_shift.shape),), (pressure_basis, factors))
    new_displacement, wall_displacement = call(
        lambda *refs: update_kernel(*refs, ranks=ranks),
        (shape(*displacement.shape), shape(3, owner_rank.shape[0])),
        (answers, shell_basis, displacement, solved_prev, solved_history, owner, slots),
    )
    return (pressure, new_displacement, wall_displacement)


def solution(mesh):
    in_specs = (
        P(None, ("groups", "slab"), None, None),
        P(("groups", "slab"), None, None),
        P(("groups", "slab"), None),
        P(("groups", "slab")),
        P(("groups", "slab")),
        P(None, ("groups", "slab"), None),
        P(("groups", "slab"), None),
        P(None, ("groups", "slab"), None),
        P(None, ("groups", "slab"), None),
        P(None, ("groups", "slab"), None),
        P(None, None, ("groups", "slab"), None),
        P(None, None, ("groups", "slab"), None),
    )
    out_specs = (
        P(("groups", "slab"), None, None),
        P(None, ("groups", "slab"), None),
        P(None, ("groups", "slab")),
    )
    return jax.shard_map(
        on_device, mesh=mesh, in_specs=in_specs, out_specs=out_specs, check_vma=False
    )
```

time: 1330 us -> 92.5 us (0.07)
  blocking collectives: 1070 us -> 0 us
  between operations: 56.6 us -> 0.93 us
  other arithmetic: 51.2 us -> 0.66 us
  starting transfers between devices: 85.5 us -> 37.5 us
  local copies, waits for them, and re-layouts: 37.9 us -> 15.2 us
  Pallas kernels: 0 us -> 14.7 us
    psum x25 -> x0, blocking collectives: 1060 us -> none  [the longest x11 487 us: on_device(): step_size = norm_now / lax.psum(jnp.sum(direction * image), 'slab')]
    ppermute x32 -> x9, starting transfers between devices: 72.2 us -> 23.9 us  [the longest x4 17.3 us: rightward(): return lax.ppermute(values, 'slab', [(i, i + 1) for i in range(ranks - 1)])]
    reduce_sum x25 -> x0, other arithmetic: 17.9 us -> none  [the longest x13 9.68 us: on_device(): step_size = norm_now / lax.psum(jnp.sum(direction * image), 'slab')]
    pallas_call x0 -> x7, Pallas kernels: none -> 14.7 us  [call(): pl.pallas_call(kernel, out_shape=outs, in_specs=[VMEM] * len(args), out_s...]
  transfers between devices with their start and end apart: 34 -> 11, of which waited for: 15 -> 5; matrix products, arithmetic and copies ran while one was open for 4% -> 1% of each run, Pallas kernels for 0% -> 1%
where the time goes in v1:
time: 92.5 us; the launch traced here: 91.6 us
  starting transfers between devices  37.5 us (41%)
  waiting for transfers between devices  22.5 us (24%)
  local copies, waits for them, and re-layouts  15.2 us (16%)
  Pallas kernels  14.7 us (16%)
  between operations  0.93 us (1%)
    ppermute x4, starting transfers between devices, rightward(): return lax.ppermute(values, 'slab', [(i, i + 1) for i in range(ranks - 1)])  17.3 us
    unnamed x57, local copies, waits for them, and re-layouts  15.2 us
    pallas_call x7, Pallas kernels, call(): pl.pallas_call(kernel, out_shape=outs, in_specs=[VMEM] * len(args), out_s...  14.7 us
    all_to_all x2, starting transfers between devices, on_device(): lax.all_to_all(payload, 'slab', split_axis=0, concat_axis=0, tiled=True)  13.7 us
    all_to_all x2, waiting for transfers between devices, on_device(): lax.all_to_all(payload, 'slab', split_axis=0, concat_axis=0, tiled=True)  11 us
    ppermute x5, waiting for transfers between devices, leftward(): return lax.ppermute(values, 'slab', [(i, i - by) for i in range(by, ranks)])  10.6 us
    ppermute x5, starting transfers between devices, leftward(): return lax.ppermute(values, 'slab', [(i, i - by) for i in range(by, ranks)])  6.59 us
  transfers between devices with their start and end apart: 11, of which 5 were waited for; matrix products, arithmetic and copies ran while one was open for 1% of the time, Pallas kernels for 1%

profile of v1, /device:TPU:0, one launch (start us, length us, event | category | flops | bytes accessed | tf_op | source)
XLA Modules:
  0.0 91.6 jit_solution(10743597907134602436)
XLA Ops:
  1.5 1.1 %copy-done.4 = f32[3,4,64,256]{3,2,1,0:T(8,128)S(1)} copy-done((f32[3,4,64,256]{3,2,1,0:T(8,128)S(1)}, f32[3,4,64,256]{3,2,1,0:T(8,128)}, u32[]{:S(2)}) %copy-start.4) | copy-done | bytes 786456
  3.4 1.3 %collective-permute-start.1 = (f32[288,128]{1,0:T(8,128)S(1)}, f32[288,128]{1,0:T(8,128)S(1)}, u32[]{:S(2)}, u32[]{:S(2)}) collective-permute-start(f32[288,128]{1,0:T(8,128)S(1)} %get-tuple-element.19.to_left), channel_id=1, source_target_pairs={{1,0},{2,1},{3,2},{4,3},{5,4},{6,5},{7,6},{8,7},{9,8},{10,9},{11,1... | collective-permute-start | bytes 442376 | tf_op jit(solution)/shard_map/ppermute | solution.py:565
  4.7 3.0 %collective-permute-start = (f32[288,128]{1,0:T(8,128)S(1)}, f32[288,128]{1,0:T(8,128)S(1)}, u32[]{:S(2)}, u32[]{:S(2)}) collective-permute-start(f32[288,128]{1,0:T(8,128)S(1)} %get-tuple-element.20.to_right), channel_id=1, source_target_pairs={{0,1},{1,2},{2,3},{3,4},{4,5},{5,6},{6,7},{7,8},{8,9},{9,10},{10,1... | collective-permute-start | bytes 442376 | tf_op jit(solution)/shard_map/ppermute | solution.py:568
  7.8 1.0 %collective-permute-done.from_left = f32[288,128]{1,0:T(8,128)S(1)} collective-permute-done((f32[288,128]{1,0:T(8,128)S(1)}, f32[288,128]{1,0:T(8,128)S(1)}, u32[]{:S(2)}, u32[]{:S(2)}) %collective-permute-start) | collective-permute-done | bytes 147488 | tf_op jit(solution)/shard_map/ppermute | solution.py:568
  11.5 1.4 %collective-permute-start.3 = (f32[704,128]{1,0:T(8,128)S(1)}, f32[704,128]{1,0:T(8,128)S(1)}, u32[]{:S(2)}, u32[]{:S(2)}) collective-permute-start(f32[704,128]{1,0:T(8,128)S(1)} %get-tuple-element.21.refs_0_.refs_1_), channel_id=1, source_target_pairs={{1,0},{2,1},{3,2},{4,3},{5,4},{6,5},{7,6},{8,7},{9,8},{10,9},{11,1... | collective-permute-start | bytes 1081352 | tf_op jit(solution)/shard_map/ppermute | solution.py:565
  12.9 7.7 %collective-permute-start.2 = (f32[704,128]{1,0:T(8,128)S(1)}, f32[704,128]{1,0:T(8,128)S(1)}, u32[]{:S(2)}, u32[]{:S(2)}) collective-permute-start(f32[704,128]{1,0:T(8,128)S(1)} %get-tuple-element.21.refs_0_.refs_1_), channel_id=1, source_target_pairs={{0,1},{1,2},{2,3},{3,4},{4,5},{5,6},{6,7},{7,8},{8,9},{9,10},{10,1... | collective-permute-start | bytes 1081352 | tf_op jit(solution)/shard_map/ppermute | solution.py:568
  20.7 4.4 %collective-permute-start.5 = (f32[4,64,256]{2,1,0:T(8,128)S(1)}, f32[4,64,256]{2,1,0:T(8,128)S(1)}, u32[]{:S(2)}, u32[]{:S(2)}) collective-permute-start(f32[4,64,256]{2,1,0:T(8,128)S(1)} %copy-done.10), channel_id=1, source_target_pairs={{0,1},{1,2},{2,3},{3,4},{4,5},{5,6},{6,7},{7,8},{8,9},{9,10},{10,1... | collective-permute-start | bytes 786440 | tf_op jit(solution)/shard_map/ppermute | solution.py:568
  25.0 1.3 %collective-permute-start.6 = (f32[4,64,256]{2,1,0:T(8,128)S(1)}, f32[4,64,256]{2,1,0:T(8,128)S(1)}, u32[]{:S(2)}, u32[]{:S(2)}) collective-permute-start(f32[4,64,256]{2,1,0:T(8,128)S(1)} %copy-done.10), channel_id=1, source_target_pairs={{1,0},{2,1},{3,2},{4,3},{5,4},{6,5},{7,6},{8,7},{9,8},{10,9},{11,1... | collective-permute-start | bytes 786440 | tf_op jit(solution)/shard_map/ppermute | solution.py:565
  26.3 1.3 %collective-permute-start.4 = (f32[128,128]{1,0:T(8,128)S(1)}, f32[128,128]{1,0:T(8,128)S(1)}, u32[]{:S(2)}, u32[]{:S(2)}) collective-permute-start(f32[128,128]{1,0:T(8,128)S(1)} %get-tuple-element.22), channel_id=1, source_target_pairs={{2,0},{3,1},{4,2},{5,3},{6,4},{7,5},{8,6},{9,7},{10,8},{11,9},{12,... | collective-permute-start | bytes 196616 | tf_op jit(solution)/shard_map/ppermute | solution.py:565
  29.1 8.2 %collective-permute-done.4.refs_3_ = f32[128,128]{1,0:T(8,128)S(1)} collective-permute-done((f32[128,128]{1,0:T(8,128)S(1)}, f32[128,128]{1,0:T(8,128)S(1)}, u32[]{:S(2)}, u32[]{:S(2)}) %collective-permute-start.4) | collective-permute-done | bytes 65568 | tf_op jit(solution)/shard_map/ppermute | solution.py:565
  38.8 0.9 %copy-done.11 = f32[4,64,256]{2,1,0:T(8,128)S(1)} copy-done((f32[4,64,256]{2,1,0:T(8,128)S(1)}, f32[4,64,256]{2,1,0:T(8,128)}, u32[]{:S(2)}) %copy-start.11) | copy-done | bytes 262168
  39.7 0.9 %copy-done.13 = f32[4,64,256]{2,1,0:T(8,128)S(1)} copy-done((f32[4,64,256]{2,1,0:T(8,128)S(1)}, f32[4,64,256]{2,1,0:T(8,128)}, u32[]{:S(2)}) %copy-start.13) | copy-done | bytes 262168
  40.7 0.9 %copy-done.15 = f32[4,64,256]{2,1,0:T(8,128)S(1)} copy-done((f32[4,64,256]{2,1,0:T(8,128)S(1)}, f32[4,64,256]{2,1,0:T(8,128)}, u32[]{:S(2)}) %copy-start.15) | copy-done | bytes 262168
  41.6 2.6 %shard_map.142 = (f32[32,8,128]{2,1,0:T(8,128)S(1)}, f32[5,4,64,256]{3,2,1,0:T(8,128)S(1)}) custom-call(f32[704,128]{1,0:T(8,128)S(1)} %get-tuple-element.21.refs_0_.refs_1_, f32[704,128]{1,0:T(8,128)S(1)} %collective-permute-done.2.refs_1_.refs_2_, f32[704,128]{1,0:T(8,128)S(1)} %collective-permute-done.3.refs_2_.refs_3_, ...), custom_call_target="tpu_custom_call" | custom-call | flops 1000000 | bytes 1000000 | tf_op jit(solution)/shard_map/pallas_call | solution.py:30
  44.9 6.2 %all-to-all-start = ((f32[32,8,128]{2,1,0:T(8,128)}), f32[32,8,128]{2,1,0:T(8,128)S(1)}, u32[]{:S(2)}, u32[]{:S(2)}) async-start(f32[32,8,128]{2,1,0:T(8,128)} %copy-done.18), calls=%async_computation | async-start | bytes 262144 | tf_op jit(solution)/shard_map/all_to_all | solution.py:608
  51.1 2.2 %collective-permute-start.7 = (f32[8,1024]{1,0:T(8,128)S(1)}, f32[8,1024]{1,0:T(8,128)S(1)}, u32[]{:S(2)}, u32[]{:S(2)}) collective-permute-start(f32[8,1024]{1,0:T(8,128)S(1)} %copy-done.17), channel_id=1, source_target_pairs={{0,1},{1,2},{2,3},{3,4},{4,5},{5,6},{6,7},{7,8},{8,9},{9,10},{10,1... | collective-permute-start | bytes 98312 | tf_op jit(solution)/shard_map/ppermute | solution.py:568
  53.3 1.3 %collective-permute-start.8 = (f32[8,1024]{1,0:T(8,128)S(1)}, f32[8,1024]{1,0:T(8,128)S(1)}, u32[]{:S(2)}, u32[]{:S(2)}) collective-permute-start(f32[8,1024]{1,0:T(8,128)S(1)} %copy-done.17), channel_id=1, source_target_pairs={{1,0},{2,1},{3,2},{4,3},{5,4},{6,5},{7,6},{8,7},{9,8},{10,9},{11,1... | collective-permute-start | bytes 98312 | tf_op jit(solution)/shard_map/ppermute | solution.py:565
  55.2 2.3 %collective-permute-done.8.refs_6_ = f32[8,1024]{1,0:T(8,128)S(1)} collective-permute-done((f32[8,1024]{1,0:T(8,128)S(1)}, f32[8,1024]{1,0:T(8,128)S(1)}, u32[]{:S(2)}, u32[]{:S(2)}) %collective-permute-start.8) | collective-permute-done | bytes 32800 | tf_op jit(solution)/shard_map/ppermute | solution.py:565
  58.1 1.2 %all-to-all-done.refs_0_ = f32[32,8,128]{2,1,0:T(8,128)S(1)} async-done(((f32[32,8,128]{2,1,0:T(8,128)}), f32[32,8,128]{2,1,0:T(8,128)S(1)}, u32[]{:S(2)}, u32[]{:S(2)}) %all-to-all-start) | async-done | bytes 131104 | tf_op jit(solution)/shard_map/all_to_all | solution.py:608
  61.8 7.5 %shard_map.143 = (f32[32,16,128]{2,1,0:T(8,128)S(1)}, f32[8,3,8,1024]{3,2,1,0:T(8,128)S(1)}, f32[8,128]{1,0:T(8,128)S(1)}) custom-call(f32[32,8,128]{2,1,0:T(8,128)S(1)} %all-to-all-done.refs_0_, f32[704,128]{1,0:T(8,128)S(1)} %get-tuple-element.21.refs_0_.refs_1_, f32[704,128]{1,0:T(8,128)S(1)} %collective-permute-done.2.refs_1_.refs_2_, ...), custom_call_target="tpu_custom_call" | custom-call | flops 1000000 | bytes 1000000 | tf_op jit(solution)/shard_map/pallas_call | solution.py:30
  69.3 0.9 copy-done.5
  70.9 7.4 %all-to-all-start.1 = ((f32[32,16,128]{2,1,0:T(8,128)}), f32[32,16,128]{2,1,0:T(8,128)S(1)}, u32[]{:S(2)}, u32[]{:S(2)}) async-start(f32[32,16,128]{2,1,0:T(8,128)} %copy-done.9), calls=%async_computation.1 | async-start | bytes 524288 | tf_op jit(solution)/shard_map/all_to_all | solution.py:624
  79.1 9.8 %all-to-all-done.1.refs_0_ = f32[32,16,128]{2,1,0:T(8,128)S(1)} async-done(((f32[32,16,128]{2,1,0:T(8,128)}), f32[32,16,128]{2,1,0:T(8,128)S(1)}, u32[]{:S(2)}, u32[]{:S(2)}) %all-to-all-start.1) | async-done | bytes 262176 | tf_op jit(solution)/shard_map/all_to_all | solution.py:624
  88.9 2.7 %shard_map.145 = (f32[3,8,1024]{2,1,0:T(8,128)}, f32[3,1024]{1,0:T(4,128)}) custom-call(f32[32,16,128]{2,1,0:T(8,128)S(1)} %all-to-all-done.1.refs_0_, f32[8,3,8,1024]{3,2,1,0:T(8,128)S(1)} %copy-done.6, f32[3,8,1024]{2,1,0:T(8,128)S(1)} %copy-done.2, f32[3,8,1024]{2,1,0:T(8,128)S(1)} %copy-done.7, f32[4,3,8,1024]{3,2,1,0:T(8,128)S(1)} %copy-done.3, ...), custom_call_target="tpu_custom_call" | custom-call | flops 1000000 | bytes 1000000 | tf_op jit(solution)/shard_map/pallas_call | solution.py:30
  (66 shorter events, 13.0 us)
Async XLA Ops:
  1.5 1.1 %copy-start.4 = (f32[3,4,64,256]{3,2,1,0:T(8,128)S(1)}, f32[3,4,64,256]{3,2,1,0:T(8,128)}, u32[]{:S(2)}) copy-start(f32[3,4,64,256]{3,2,1,0:T(8,128)} %velocity.1) | copy-start | bytes 2359300
  2.7 18.0 %copy-start.10 = (f32[4,64,256]{2,1,0:T(8,128)S(1)}, f32[4,64,256]{2,1,0:T(8,128)}, u32[]{:S(2)}) copy-start(f32[4,64,256]{2,1,0:T(8,128)} %refs_4_.3) | copy-start | bytes 786436
  2.7 25.5 %copy-start.25 = (s32[1024,1]{0,1:T(1,128)S(1)}, s32[1024,1]{0,1:T(1,128)}, u32[]{:S(2)}) copy-start(s32[1024,1]{0,1:T(1,128)} %param.14) | copy-start | bytes 12292
  2.7 26.2 %copy-start.26 = (s32[1024]{0:T(1024)S(1)}, s32[1024]{0:T(1024)}, u32[]{:S(2)}) copy-start(s32[1024]{0:T(1024)} %param.15) | copy-start | bytes 12292
  2.7 26.2 %copy-start.27 = (s32[1024]{0:T(1024)S(1)}, s32[1024]{0:T(1024)}, u32[]{:S(2)}) copy-start(s32[1024]{0:T(1024)} %param.16) | copy-start | bytes 12292
  3.4 4.3 %collective-permute-start.1 = (f32[288,128]{1,0:T(8,128)S(1)}, f32[288,128]{1,0:T(8,128)S(1)}, u32[]{:S(2)}, u32[]{:S(2)}) collective-permute-start(f32[288,128]{1,0:T(8,128)S(1)} %get-tuple-element.19.to_left), channel_id=1, source_target_pairs={{1,0},{2,1},{3,2},{4,3},{5,4},{6,5},{7,6},{8,7},{9,8},{10,9},{11,1... | collective-permute-start | bytes 442376 | tf_op jit(solution)/shard_map/ppermute | solution.py:565
  4.7 4.0 %collective-permute-start = (f32[288,128]{1,0:T(8,128)S(1)}, f32[288,128]{1,0:T(8,128)S(1)}, u32[]{:S(2)}, u32[]{:S(2)}) collective-permute-start(f32[288,128]{1,0:T(8,128)S(1)} %get-tuple-element.20.to_right), channel_id=1, source_target_pairs={{0,1},{1,2},{2,3},{3,4},{4,5},{5,6},{6,7},{7,8},{8,9},{9,10},{10,1... | collective-permute-start | bytes 442376 | tf_op jit(solution)/shard_map/ppermute | solution.py:568
  11.3 39.8 %copy-start.17 = (f32[8,1024]{1,0:T(8,128)S(1)}, f32[8,1024]{1,0:T(8,128)}, u32[]{:S(2)}) copy-start(f32[8,1024]{1,0:T(8,128)} %refs_4_.4) | copy-start | bytes 98308
  11.4 47.9 %copy-start.2 = (f32[3,8,1024]{2,1,0:T(8,128)S(1)}, f32[3,8,1024]{2,1,0:T(8,128)}, u32[]{:S(2)}) copy-start(f32[3,8,1024]{2,1,0:T(8,128)} %refs_2_.1) | copy-start | bytes 294916
  11.5 47.9 %copy-start.3 = (f32[4,3,8,1024]{3,2,1,0:T(8,128)S(1)}, f32[4,3,8,1024]{3,2,1,0:T(8,128)}, u32[]{:S(2)}) copy-start(f32[4,3,8,1024]{3,2,1,0:T(8,128)} %refs_4_.5) | copy-start | bytes 1179652
  11.5 47.9 %copy-start.7 = (f32[3,8,1024]{2,1,0:T(8,128)S(1)}, f32[3,8,1024]{2,1,0:T(8,128)}, u32[]{:S(2)}) copy-start(f32[3,8,1024]{2,1,0:T(8,128)} %refs_3_.1) | copy-start | bytes 294916
  11.5 47.9 %copy-start.8 = (f32[4,3,8,1024]{3,2,1,0:T(8,128)S(1)}, f32[4,3,8,1024]{3,2,1,0:T(8,128)}, u32[]{:S(2)}) copy-start(f32[4,3,8,1024]{3,2,1,0:T(8,128)} %refs_10_.1) | copy-start | bytes 1179652
  11.5 27.3 %collective-permute-start.3 = (f32[704,128]{1,0:T(8,128)S(1)}, f32[704,128]{1,0:T(8,128)S(1)}, u32[]{:S(2)}, u32[]{:S(2)}) collective-permute-start(f32[704,128]{1,0:T(8,128)S(1)} %get-tuple-element.21.refs_0_.refs_1_), channel_id=1, source_target_pairs={{1,0},{2,1},{3,2},{4,3},{5,4},{6,5},{7,6},{8,7},{9,8},{10,9},{11,1... | collective-permute-start | bytes 1081352 | tf_op jit(solution)/shard_map/ppermute | solution.py:565
  12.9 25.8 %collective-permute-start.2 = (f32[704,128]{1,0:T(8,128)S(1)}, f32[704,128]{1,0:T(8,128)S(1)}, u32[]{:S(2)}, u32[]{:S(2)}) collective-permute-start(f32[704,128]{1,0:T(8,128)S(1)} %get-tuple-element.21.refs_0_.refs_1_), channel_id=1, source_target_pairs={{0,1},{1,2},{2,3},{3,4},{4,5},{5,6},{6,7},{7,8},{8,9},{9,10},{10,1... | collective-permute-start | bytes 1081352 | tf_op jit(solution)/shard_map/ppermute | solution.py:568
  20.7 16.7 %collective-permute-start.5 = (f32[4,64,256]{2,1,0:T(8,128)S(1)}, f32[4,64,256]{2,1,0:T(8,128)S(1)}, u32[]{:S(2)}, u32[]{:S(2)}) collective-permute-start(f32[4,64,256]{2,1,0:T(8,128)S(1)} %copy-done.10), channel_id=1, source_target_pairs={{0,1},{1,2},{2,3},{3,4},{4,5},{5,6},{6,7},{7,8},{8,9},{9,10},{10,1... | collective-permute-start | bytes 786440 | tf_op jit(solution)/shard_map/ppermute | solution.py:568
  25.0 13.0 %collective-permute-start.6 = (f32[4,64,256]{2,1,0:T(8,128)S(1)}, f32[4,64,256]{2,1,0:T(8,128)S(1)}, u32[]{:S(2)}, u32[]{:S(2)}) collective-permute-start(f32[4,64,256]{2,1,0:T(8,128)S(1)} %copy-done.10), channel_id=1, source_target_pairs={{1,0},{2,1},{3,2},{4,3},{5,4},{6,5},{7,6},{8,7},{9,8},{10,9},{11,1... | collective-permute-start | bytes 786440 | tf_op jit(solution)/shard_map/ppermute | solution.py:565
  26.3 11.0 %collective-permute-start.4 = (f32[128,128]{1,0:T(8,128)S(1)}, f32[128,128]{1,0:T(8,128)S(1)}, u32[]{:S(2)}, u32[]{:S(2)}) collective-permute-start(f32[128,128]{1,0:T(8,128)S(1)} %get-tuple-element.22), channel_id=1, source_target_pairs={{2,0},{3,1},{4,2},{5,3},{6,4},{7,5},{8,6},{9,7},{10,8},{11,9},{12,... | collective-permute-start | bytes 196616 | tf_op jit(solution)/shard_map/ppermute | solution.py:565
  38.8 1.0 %copy-start.11 = (f32[4,64,256]{2,1,0:T(8,128)S(1)}, f32[4,64,256]{2,1,0:T(8,128)}, u32[]{:S(2)}) copy-start(f32[4,64,256]{2,1,0:T(8,128)} %refs_4_.3) | copy-start | bytes 786436
  39.7 0.9 %copy-start.13 = (f32[4,64,256]{2,1,0:T(8,128)S(1)}, f32[4,64,256]{2,1,0:T(8,128)}, u32[]{:S(2)}) copy-start(f32[4,64,256]{2,1,0:T(8,128)} %copy-done.12) | copy-start | bytes 786436
  44.9 14.5 %all-to-all-start = ((f32[32,8,128]{2,1,0:T(8,128)}), f32[32,8,128]{2,1,0:T(8,128)S(1)}, u32[]{:S(2)}, u32[]{:S(2)}) async-start(f32[32,8,128]{2,1,0:T(8,128)} %copy-done.18), calls=%async_computation | async-start | bytes 262144 | tf_op jit(solution)/shard_map/all_to_all | solution.py:608
  51.1 3.5 %collective-permute-start.7 = (f32[8,1024]{1,0:T(8,128)S(1)}, f32[8,1024]{1,0:T(8,128)S(1)}, u32[]{:S(2)}, u32[]{:S(2)}) collective-permute-start(f32[8,1024]{1,0:T(8,128)S(1)} %copy-done.17), channel_id=1, source_target_pairs={{0,1},{1,2},{2,3},{3,4},{4,5},{5,6},{6,7},{7,8},{8,9},{9,10},{10,1... | collective-permute-start | bytes 98312 | tf_op jit(solution)/shard_map/ppermute | solution.py:568
  53.3 4.2 %collective-permute-start.8 = (f32[8,1024]{1,0:T(8,128)S(1)}, f32[8,1024]{1,0:T(8,128)S(1)}, u32[]{:S(2)}, u32[]{:S(2)}) collective-permute-start(f32[8,1024]{1,0:T(8,128)S(1)} %copy-done.17), channel_id=1, source_target_pairs={{1,0},{2,1},{3,2},{4,3},{5,4},{6,5},{7,6},{8,7},{9,8},{10,9},{11,1... | collective-permute-start | bytes 98312 | tf_op jit(solution)/shard_map/ppermute | solution.py:565
  70.9 18.0 %copy-start.6 = (f32[8,3,8,1024]{3,2,1,0:T(8,128)S(1)}, f32[8,3,8,1024]{3,2,1,0:T(8,128)}, u32[]{:S(2)}) copy-start(f32[8,3,8,1024]{3,2,1,0:T(8,128)} %copy-done.5) | copy-start | bytes 2359300
  70.9 18.0 %all-to-all-start.1 = ((f32[32,16,128]{2,1,0:T(8,128)}), f32[32,16,128]{2,1,0:T(8,128)S(1)}, u32[]{:S(2)}, u32[]{:S(2)}) async-start(f32[32,16,128]{2,1,0:T(8,128)} %copy-done.9), calls=%async_computation.1 | async-start | bytes 524288 | tf_op jit(solution)/shard_map/all_to_all | solution.py:624
  (15 other events, 11.7 us)

commit v2 on v1

--- a/solution.py
+++ b/solution.py
@@ -23,18 +23,99 @@
 BF16 = jnp.bfloat16
 
 H2_AT, ROW_AT, DISP_AT, HALO_ROWS = 128, 256, 264, 288
-SHELL_AT, FIELD_ROWS = 512, 704
-
-
-def call(kernel, outs, args, scratch=(), flops=1000000, limit=48):
+FIELD_ROWS, STIFF_AT, SHELL_ROWS = 512, 192, 256
+
+
+def even_device():
+    return lax.rem(lax.axis_index("slab"), 2) == 0
+
+
+class Late:
+    def __init__(self, source, place, semaphore):
+        self.place = place
+        self.copy = pltpu.make_async_copy(source, place, semaphore)
+        self.copy.start()
+        self.pending = True
+
+    def __call__(self):
+        if self.pending:
+            self.copy.wait()
+            self.pending = False
+        return self.place
+
+
+class Sides:
+    def __init__(self, to_mate, to_other, left, right, semaphores):
+        even = even_device()
+        self.copies = [
+            pltpu.make_async_copy(to_mate, left, semaphores.at[0]),
+            pltpu.make_async_copy(to_other, right, semaphores.at[1]),
+        ]
+        self.places = (left, right)
+
+        @pl.when(even)
+        def _():
+            pltpu.make_async_copy(to_other, left, semaphores.at[0]).start()
+            pltpu.make_async_copy(to_mate, right, semaphores.at[1]).start()
+
+        @pl.when(jnp.logical_not(even))
+        def _():
+            for copy in self.copies:
+                copy.start()
+
+        self.pending = True
+
+    def __call__(self):
+        if self.pending:
+            for copy in self.copies:
+                copy.wait()
+            self.pending = False
+        return self.places
+
+
+def call(
+    kernel, outs, args, late=(), pairs=(), direct=(), stored=(), scratch=(),
+    flops=1000000000, limit=48.0,
+):
+    count, made = len(args), len(outs)
+
+    def body(*refs):
+        operands = list(refs[:count])
+        at_end = count + made + len(scratch)
+        places = iter(refs[at_end:-1])
+        wanted = []
+        used = 0
+        for i in late:
+            operands[i] = Late(operands[i], next(places), refs[-1].at[used])
+            wanted.append(operands[i])
+            used += 1
+        for i in pairs:
+            operands[i] = Sides(
+                operands[i], operands[i + 1], next(places), next(places), refs[-1].at[pl.ds(used, 2)]
+            )
+            wanted.append(operands[i])
+            used += 2
+        operands = [value for i, value in enumerate(operands) if i - 1 not in pairs]
+        kernel(*operands, *refs[count:at_end])
+        for value in wanted:
+            value()
+
+    outside = [i for i in late] + [i + k for i in pairs for k in (0, 1)]
+    extra = [pltpu.VMEM(args[i].shape, args[i].dtype) for i in outside]
+    extra.append(pltpu.SemaphoreType.DMA((max(1, len(outside)),)))
+    args = [
+        pltpu.with_memory_space_constraint(value, pltpu.HBM) if i in stored else value
+        for i, value in enumerate(args)
+    ]
+    any_space = pl.BlockSpec(memory_space=pl.ANY)
     return pl.pallas_call(
-        kernel,
+        body,
         out_shape=outs,
-        in_specs=[VMEM] * len(args),
-        out_specs=jax.tree.map(lambda _: VMEM, outs),
-        scratch_shapes=list(scratch),
-        compiler_params=pltpu.CompilerParams(vmem_limit_bytes=limit * 1024 * 1024),
-        cost_estimate=pl.CostEstimate(flops=flops, bytes_accessed=1000000, transcendentals=0),
+        in_specs=[any_space if i in outside else VMEM for i in range(count)],
+        out_specs=tuple(any_space if i in direct else VMEM for i in range(made)),
+        scratch_shapes=list(scratch) + extra,
+        compiler_params=pltpu.CompilerParams(vmem_limit_bytes=int(limit * 1024 * 1024)),
+        cost_estimate=pl.CostEstimate(flops=flops, bytes_accessed=0, transcendentals=0),
     )(*args)
 
 
@@ -87,13 +168,30 @@
     return lax.dot_general(left, right, dims, preferred_element_type=F32)
 
 
+def pieces_of(values, count):
+    pieces = []
+    for _ in range(count):
+        pieces.append(values.astype(BF16).astype(F32))
+        values = values - pieces[-1]
+    return pieces
+
+
+def added(product, count):
+    rows = product.shape[0] // count
+    return sum(product[i * rows : (i + 1) * rows] for i in range(count))
+
+
 def split_dot(left, right, count, transposed=False):
     rows = left.shape[0]
     product = dot(jnp.concatenate(parts(left, count), 0), right, transposed)
     return sum(product[i * rows : (i + 1) * rows] for i in range(count))
 
 
-def fluid_kernel(velocity, displacement, to_left, to_right, source, wall):
+def fluid_kernel(
+    velocity, displacement, to_mate, to_other, own_left, own_right, source, wall
+):
+    velocity, displacement = velocity(), displacement()
+    even = even_device()
     layers = velocity.shape[1]
     last = layers - 1
     field = [[velocity[c, x] for x in range(layers)] for c in range(3)]
@@ -101,20 +199,27 @@
     spread = {
         x: NU * (difference(field[1][x], 0) + difference(field[2][x], 1)) for x in (0, last)
     }
-    put_halves(to_left, 0, own[0][0] + NU * field[0][1] + spread[0])
-    put_halves(to_left, H2_AT, NU * field[0][0])
-    put_halves(to_right, 0, spread[last] - own[0][last] - NU * field[0][last - 1])
-    put_halves(to_right, H2_AT, NU * field[0][last])
-    for ref, x, row in ((to_left, 0, 0), (to_right, last, 7)):
-        edge = (MU * NU) * (velocity[2, x, 1:2, :] - velocity[2, x, 0:1, :])
+    lefts = (own[0][0] + NU * field[0][1] + spread[0], NU * field[0][0])
+    rights = (spread[last] - own[0][last] - NU * field[0][last - 1], NU * field[0][last])
+    own_left[...] = lefts[1]
+    own_right[...] = rights[1]
+    edges = [
+        (MU * NU) * (velocity[2, x, 1:2, :] - velocity[2, x, 0:1, :]) for x in (0, last)
+    ]
+    for ref, first, second in ((to_mate, rights, lefts), (to_other, lefts, rights)):
+        put_halves(ref, 0, jnp.where(even, first[0], second[0]))
+        put_halves(ref, H2_AT, jnp.where(even, first[1], second[1]))
         ref[ROW_AT : DISP_AT, :] = jnp.zeros((8, 128), F32)
+        ref[ROW_AT + 2 : ROW_AT + 3, :] = jnp.ones((1, 128), F32)
+        edge = jnp.where(even, edges[int(first is rights)], edges[int(second is rights)])
         ref[ROW_AT : ROW_AT + 1, :] = edge[:, :128]
         ref[ROW_AT + 1 : ROW_AT + 2, :] = edge[:, 128:]
-        ref[ROW_AT + 2 : ROW_AT + 3, :] = jnp.ones((1, 128), F32)
         for c in range(3):
+            rows = (displacement[c, 0:1, :], displacement[c, 7:8, :])
+            row = jnp.where(even, rows[int(first is rights)], rows[int(second is rights)])
             for k in range(8):
                 place = DISP_AT + c * 8 + k
-                ref[place : place + 1, :] = displacement[c, row : row + 1, k * 128 : k * 128 + 128]
+                ref[place : place + 1, :] = row[:, k * 128 : k * 128 + 128]
     zero = jnp.zeros_like(field[0][0])
     predicted = [
         [
@@ -143,16 +248,19 @@
 
 
 def source_kernel(
-    source, wall, to_left, to_right, from_left, from_right, displacement, load, stiffness, fields, first, wall_out
+    source, wall, own_left, own_right, halo, displacement, load, stiffness,
+    fields, first, shell, wall_out,
 ):
+    from_left, from_right = halo()
+    displacement, load, stiffness = displacement(), load(), stiffness()
     layers = source.shape[0]
     last = layers - 1
     left1, left2 = halves(from_left, 0), halves(from_left, H2_AT)
     right1, right2 = halves(from_right, 0), halves(from_right, H2_AT)
     has_left = from_left[ROW_AT + 2 : ROW_AT + 3, 0:1]
     has_right = from_right[ROW_AT + 2 : ROW_AT + 3, 0:1]
-    left1 = left1 - has_left * halves(to_left, H2_AT)
-    right1 = right1 + has_right * halves(to_right, H2_AT)
+    left1 = left1 - has_left * own_left[...]
+    right1 = right1 + has_right * own_right[...]
     for x in range(layers):
         plane = source[x]
         if x == 0:
@@ -185,8 +293,11 @@
         beside = beside + ahead(field, 1) + behind(field, 1)
         start = load[c] - ((4.0 + stiffness[...]) * field - beside)
         for k in range(8):
-            place = SHELL_AT + (c * 8 + k) * 8
-            fields[place : place + 8, :] = start[:, k * 128 : k * 128 + 128]
+            place = (c * 8 + k) * 8
+            shell[place : place + 8, :] = start[:, k * 128 : k * 128 + 128]
+    for k in range(8):
+        place = STIFF_AT + k * 8
+        shell[place : place + 8, :] = stiffness[:, k * 128 : k * 128 + 128]
 
 
 def slots_kernel(owner, slots, *, ranks):
@@ -227,10 +338,13 @@
 
 
 def pressure_kernel(
-    own, left, right, beyond, shift, shift_left, shift_right,
+    own, halo, beyond, shift, shift_halo,
     wall, owner, slots, node, weight,
-    payload, basis, work, diagonal, off, *, ranks,
+    payload, basis, work, diagonal, off, sent, *, ranks,
 ):
+    left, right = halo()
+    beyond, shift = beyond(), shift()
+    shift_left, shift_right = shift_halo()
     layers = shift.shape[0]
     for x in range(layers):
         work[0, x] = halves(left, x * 128)
@@ -238,8 +352,7 @@
         work[0, x + 8] = halves(right, x * 128)
     work[0, 12] = halves(beyond, 0)
     for x in range(1, 12):
-        ref = (shift_left, shift, shift_right)[x // 4]
-        values = ref[x % 4]
+        values = (shift_left, shift, shift_right)[x // 4][x % 4]
         inside = values > 0.0
         diagonal[x] = jnp.where(inside, values + 6.0, 0.0)
         off[x] = jnp.where(inside, 1.0, 0.0)
@@ -253,6 +366,12 @@
             if step > 1:
                 value = value - P_BACK[step - 2] * work[step - 2, x]
             work[step, x] = value
+    copies = [
+        pltpu.make_async_copy(work.at[k, pl.ds(4, layers)], basis.at[k], sent.at[k])
+        for k in range(PITERS)
+    ]
+    for copy in copies:
+        copy.start()
     tile = jnp.zeros((8, 128), F32)
     for i in range(PITERS):
         for j in range(i, PITERS):
@@ -266,9 +385,6 @@
         image = (6.0 + shift[x - 4]) * now - plane_sum(now) - 2.0 * work[top, x + 1]
         total = total + now * image
     tile = place_pair(tile, 3 + top, (96 + PITERS, None, None), whole(fold(total)))
-    for k in range(PITERS):
-        for x in range(layers):
-            basis[k, x] = work[k, x + 4]
     lanes = lax.broadcasted_iota(jnp.int32, (128, 256), 0)
     field_row = lax.broadcasted_iota(jnp.int32, (8, 256), 0)
     packed = jnp.zeros((ranks * 8, 128), F32)
@@ -283,8 +399,10 @@
         here = jnp.where((lanes & 31) == slots[x : x + 1, :], 1.0, 0.0)
         place = jnp.where(lanes < 96, here, 0.0).astype(BF16)
         end = jnp.where(lanes >= 96, here, 0.0).astype(BF16)
-        left_rows = jnp.concatenate([jnp.where(who == d, values, 0.0) for d in range(ranks)], 0)
-        packed = packed + split_dot(left_rows, place, 3, True)
+        left_rows = jnp.concatenate(
+            [jnp.where(who == d, piece, 0.0) for piece in pieces_of(values, 3) for d in range(ranks)], 0
+        )
+        packed = packed + added(dot(left_rows.astype(BF16), place, True), 3)
         weight_rows = jnp.concatenate(
             [
                 jnp.where((who == d - 1 + field_row) & (field_row < 3), scale, 0.0)
@@ -302,6 +420,8 @@
         block = jnp.where(lane < 32, before, jnp.where(lane < 64, mine, after))
         block = jnp.where(lane < 96, block, 0.0) + weights[d * 8 : d * 8 + 8]
         payload[d] = block + tile
+    for copy in copies:
+        copy.wait()
 
 
 def row_of(matrix, k):
@@ -312,58 +432,61 @@
     return jnp.sum(jnp.where(at(matrix, 1) == k, matrix, 0.0), 1, keepdims=True)
 
 
-def as_column(row, matrix, shift):
-    spread = jnp.broadcast_to(row, matrix.shape)
-    return jnp.sum(jnp.where(at(matrix, 1) == at(matrix, 0) - shift, spread, 0.0), 1, keepdims=True)
-
-
-def eliminate(matrix, first_row, first_lane, count):
-    row_at = at(matrix, 0)
-    start = matrix
-    for k in range(count):
-        row = row_of(matrix, first_row + k)
-        column = column_of(matrix, first_lane + k)
-        pivot = column_of(row, first_lane + k)
-        scale = column_of(row_of(start, first_row + k), first_lane + k)
-        good = pivot > TINY * scale
+def eliminate(columns, right, first):
+    row = at(right, 0)
+    lengths = [TINY * column[first + k : first + k + 1] for k, column in enumerate(columns)]
+    for k in range(len(columns)):
+        column = columns[k]
+        here = first + k
+        pivot = column[here : here + 1]
+        good = pivot > lengths[k]
         inverse = jnp.where(good, 1.0 / jnp.where(good, pivot, 1.0), 0.0)
-        row = row * inverse
-        matrix = jnp.where(row_at == first_row + k, row, matrix - column * row)
-    return matrix
-
-
-def galerkin(gram, first_row, shifts, back, energy):
+        factor = column * inverse
+
+        def reduced(values):
+            mine = values[here : here + 1]
+            return jnp.where(row == here, mine * inverse, values - factor * mine)
+
+        columns = columns[: k + 1] + [reduced(values) for values in columns[k + 1 :]]
+        right = reduced(right)
+    return right
+
+
+def galerkin(gram, first, shifts, back, energy):
     count = len(shifts)
-    lane, row = at(gram, 1), at(gram, 0)
+    images = []
+    for k in range(count - 1):
+        image = shifts[k] * gram[k] + gram[k + 1]
+        if k > 0:
+            image = image + back[k - 1] * gram[k - 1]
+        images.append(image)
+    last = jnp.broadcast_to(gram[count - 1], (gram[0].shape[0], 128))
+    row = at(last, 0)
     shift, prior = 0.0, 0.0
     for k in range(count):
-        shift = jnp.where(lane == k, shifts[k], shift)
+        shift = jnp.where(row == first + k, shifts[k], shift)
     for k in range(1, count):
-        prior = jnp.where(lane == k, back[k - 1], prior)
-    image = shift * gram + pltpu.roll(gram, 127, 1) + prior * pltpu.roll(gram, 1, 1)
-    last = as_column(row_of(image, first_row + count - 1), gram, first_row)
-    last = jnp.where(row == first_row + count - 1, energy, last)
-    image = jnp.where(lane == count - 1, last, image)
-    image = jnp.where(lane == count, column_of(gram, 0), image)
-    inside = (row >= first_row) & (row < first_row + count) & (lane <= count)
-    return jnp.where(inside, image, 0.0)
+        prior = jnp.where(row == first + k, back[k - 1], prior)
+    size = last.shape[0]
+    image = shift * last + pltpu.roll(last, size - 1, 0) + prior * pltpu.roll(last, 1, 0)
+    image = jnp.where(row == first + count - 1, energy, image)
+    images.append(image[:, 0:1])
+    return images
 
 
 def shell_kernel(
-    received, own, left, right, stiffness, stiffness_left, stiffness_right,
+    received, own, halo,
     displacement, residual_prev, solved_prev, residual_history, solved_history,
-    payload, basis, factors, work, diagonal, off, table, *, ranks,
+    payload, basis, factors, work, diagonal, off, table, sent, *, ranks,
 ):
+    received = received()
     lane8 = lax.broadcasted_iota(jnp.int32, (8, 128), 1)
     summed = received[0]
     for p in range(1, ranks):
         summed = summed + received[p]
-    gram = pltpu.roll(jnp.where(lane8 >= 96, summed, 0.0), 32, 1)
-    energy = jnp.sum(
-        jnp.where((at(gram, 0) == 3 + PITERS - 1) & (lane8 == PITERS), gram, 0.0), keepdims=True
-    )
-    system = galerkin(gram, 3, P_SHIFT, P_BACK, energy)
-    solved = column_of(eliminate(system, 3, 0, PITERS), PITERS)
+    gram = [column_of(summed, 96 + k) for k in range(PITERS + 1)]
+    system = galerkin(gram[:PITERS], 3, P_SHIFT, P_BACK, gram[PITERS][7:8])
+    solved = eliminate(system, gram[0], 3)
     solved = jnp.where(lax.broadcasted_iota(jnp.int32, (8, 1), 0) >= 3, solved, 0.0)
     factors[...] = jnp.broadcast_to(solved, (8, 128))
     groups = [lane8 // 32 == q for q in range(4)]
@@ -379,6 +502,7 @@
             chunks.append(chunk)
         return jnp.concatenate(chunks, 1)
 
+    left, right = halo()
     weights = gathered(3)
     entries = ranks * CAP
     target = lax.broadcasted_iota(jnp.int32, (64, entries), 0)
@@ -397,20 +521,26 @@
         code = ((numbers >> 7) & 7) * 8 + (numbers >> 10)
         spot = jnp.where(low == (numbers & 127), 1.0, 0.0).astype(BF16)
         match = target == code
-        scattered = split_dot(
-            jnp.concatenate([jnp.where(match, row, 0.0) for row in rows], 0), spot, 3, True
+        pieces = pieces_of(jnp.concatenate(rows, 0), 3)
+        left_rows = jnp.concatenate(
+            [jnp.where(match, piece[c : c + 1], 0.0) for piece in pieces for c in range(3)], 0
         )
+        scattered = added(dot(left_rows.astype(BF16), spot, True), 3)
         share = dot(jnp.where(match, weights[j : j + 1, :], 0.0).astype(BF16), spot, True)
         share = 1.0 / jnp.maximum(share, 1.0)
         ref = (left, own, right)[j]
         for c in range(3):
             force = scattered[c * 64 : c * 64 + 64] * share
             for k in range(8):
-                place = SHELL_AT + (c * 8 + k) * 8
+                place = (c * 8 + k) * 8
                 work[0, c * 24 + j * 8 : c * 24 + j * 8 + 8, k * 128 : k * 128 + 128] = (
                     force[k * 8 : k * 8 + 8] + ref[place : place + 8, :]
                 )
-        stiff = (stiffness_left, stiffness, stiffness_right)[j][...]
+        stiff = jnp.concatenate(
+            [ref[STIFF_AT + k * 8 : STIFF_AT + k * 8 + 8, :] for k in range(8)], 1
+        )
+        if j == 1:
+            stiffness = stiff
         inside = stiff > 0.0
         main = jnp.where(inside, stiff + 4.0, 0.0)
         side = jnp.where(inside, 1.0, 0.0)
@@ -423,6 +553,15 @@
         if step > 1:
             value = value - S_BACK[step - 2] * work[step - 2]
         work[step] = value
+    copies = [
+        pltpu.make_async_copy(work.at[k, pl.ds(c * 24 + 8, 8)], basis.at[k, c], sent.at[k, c])
+        for k in range(SITERS)
+        for c in range(3)
+    ]
+    for copy in copies:
+        copy.start()
+    displacement, residual_prev, solved_prev = displacement(), residual_prev(), solved_prev()
+    residual_history, solved_history = residual_history(), solved_history()
     def basis_tile(k, c):
         return work[k, c * 24 + 8 : c * 24 + 16, :]
 
@@ -439,12 +578,9 @@
     for c in range(3):
         now = basis_tile(top, c)
         after = work[top, c * 24 + 9 : c * 24 + 17, :]
-        image = (4.0 + stiffness[...]) * now - ahead(now, 1) - behind(now, 1) - 2.0 * after
+        image = (4.0 + stiffness) * now - ahead(now, 1) - behind(now, 1) - 2.0 * after
         total = total + now * image
     tile = place_pair(tile, 13, (96 + 13, None, None), whole(fold(total)))
-    for k in range(SITERS):
-        for c in range(3):
-            basis[k, c] = basis_tile(k, c)
     fields = vectors[:SITERS] + [lambda c: displacement[c]]
     fields += [lambda c, k=k: solved_history[k, c] for k in range(solved_history.shape[0])]
     fields.append(lambda c: solved_prev[c])
@@ -455,7 +591,7 @@
                 table[k, pl.ds(c * 16 + f, 8, stride=48), :] = value[:, k * 128 : k * 128 + 128]
     column = lax.broadcasted_iota(jnp.int32, (1024, entries), 0)
     pick = jnp.where(column == (node & 1023), 1.0, 0.0).astype(BF16)
-    found = split_dot(jnp.concatenate([table[k] for k in range(8)], 1), pick, 3)
+    found = split_dot(jnp.concatenate([table[k] for k in range(8)], 1), pick, 2)
     line = node >> 10
     answer = jnp.zeros((48, entries), F32)
     for r in range(8):
@@ -470,9 +606,12 @@
                 lane16 // 32 == c, pltpu.roll(piece, (32 * (c - p % 4)) % 128, 1), block
             )
         payload[p] = block
+    for copy in copies:
+        copy.wait()
 
 
 def combine_kernel(basis, factors, pressure):
+    basis = basis()
     for x in range(pressure.shape[0]):
         total = 0.0
         for k in range(PITERS):
@@ -484,30 +623,25 @@
     received, basis, displacement, solved_prev, solved_history, owner, slots,
     new_displacement, wall, *, ranks,
 ):
+    received = received()
     summed = received[0]
     for p in range(1, ranks):
         summed = summed + received[p]
-    lane, row = at(summed, 1), at(summed, 0)
-    gram = pltpu.roll(jnp.where(lane >= 96, summed, 0.0), 32, 1)
-    energy = jnp.sum(jnp.where((row == 13) & (lane == 13), gram, 0.0), keepdims=True)
-    system = galerkin(gram, 0, S_SHIFT, S_BACK, energy)
-    steps = column_of(eliminate(system, 0, 0, SITERS), SITERS)
+    gram = [column_of(summed, 96 + k) for k in range(14)]
+    system = galerkin(gram[:SITERS], 0, S_SHIFT, S_BACK, gram[13][13:14])
+    steps = eliminate(system, gram[0], 0)
     down = lax.broadcasted_iota(jnp.int32, (16, 1), 0)
     steps = jnp.where(down < SITERS, steps, 0.0)
-    base, count = SITERS, 1 + solved_history.shape[0]
-    with_moved = jnp.sum(gram * steps, 0, keepdims=True)
-    with_newest = with_moved - row_of(gram, base)
-    steps_row = jnp.sum(jnp.where(row == lane, jnp.broadcast_to(steps, gram.shape), 0.0), 0, keepdims=True)
-    newest_moved = jnp.sum(steps_row * with_newest, 1, keepdims=True)
-    newest_newest = newest_moved - column_of(with_newest, base)
-    block = jnp.where(row == base, with_newest, gram)
-    block = jnp.where(lane == base, as_column(with_newest, gram, 0), block)
-    block = jnp.where((row == base) & (lane == base), newest_newest, block)
-    right = jnp.where(down == base, newest_moved, as_column(with_moved, gram, 0))
-    block = jnp.where(lane == base + count, right, block)
-    inside = (row >= base) & (row < base + count) & (lane >= base) & (lane <= base + count)
-    block = jnp.where(inside, block, 0.0)
-    coefficients = -column_of(eliminate(block, base, base, count), base + count)
+    base, count = SITERS, 1 + solved_history.place.shape[0]
+    with_moved = sum(steps[k : k + 1] * gram[k] for k in range(SITERS))
+    with_newest = with_moved - gram[base]
+    newest_moved = jnp.sum(steps * with_newest, 0, keepdims=True)
+    newest_newest = newest_moved - with_newest[base : base + 1]
+    columns = [jnp.where(down == base, newest_newest, with_newest)]
+    for k in range(1, count):
+        columns.append(jnp.where(down == base, with_newest[base + k : base + k + 1], gram[base + k]))
+    right = jnp.where(down == base, newest_moved, with_moved)
+    coefficients = -eliminate(columns, right, base)
     newest = row_of(coefficients, base)
     factors = jnp.where(
         down < base,
@@ -518,6 +652,8 @@
             jnp.where(down < base + count, coefficients, jnp.where(down == base + count, -newest, 0.0)),
         ),
     )
+    basis = basis()
+    displacement, solved_prev, solved_history = displacement(), solved_prev(), solved_history()
     for c in range(3):
         total = row_of(factors, base) * displacement[c]
         for k in range(SITERS):
@@ -561,72 +697,101 @@
     layers = velocity.shape[1]
     kept = residual_history.shape[0]
 
-    def leftward(values, by=1):
-        return lax.ppermute(values, "slab", [(i, i - by) for i in range(by, ranks)])
-
-    def rightward(values):
-        return lax.ppermute(values, "slab", [(i, i + 1) for i in range(ranks - 1)])
+    def with_mate(values):
+        return lax.ppermute(values, "slab", [(i, i ^ 1) for i in range(ranks)])
+
+    def with_other(values):
+        pairs = [(i, i + 1) for i in range(1, ranks - 1, 2)]
+        return lax.ppermute(values, "slab", pairs + [(j, i) for i, j in pairs])
 
     owner = owner_rank.reshape(layers, -1)
     node = node_index.reshape(layers, -1)
     weight = map_weight.reshape(layers, -1)
-
-    to_left, to_right, source, wall = call(
+    plane = shape(*velocity.shape[2:])
+
+    to_mate, to_other, own_left, own_right, source, wall = call(
         fluid_kernel,
-        (shape(HALO_ROWS, 128), shape(HALO_ROWS, 128), shape(*velocity.shape[1:]), shape(8, 256)),
+        (
+            shape(HALO_ROWS, 128), shape(HALO_ROWS, 128), plane, plane,
+            shape(*velocity.shape[1:]), shape(8, 256),
+        ),
         (velocity, displacement),
-    )
-    from_right, from_left = leftward(to_left), rightward(to_right)
-    shift_right, shift_left = leftward(pressure_shift), rightward(pressure_shift)
-    stiffness_right, stiffness_left = leftward(shell_stiffness), rightward(shell_stiffness)
+        late=(0, 1),
+        stored=(0, 1),
+    )
+    halo_other, halo_mate = with_other(to_other), with_mate(to_mate)
+    shift_other, shift_mate = with_other(pressure_shift), with_mate(pressure_shift)
     (slots,) = call(
-        lambda *refs: slots_kernel(*refs, ranks=ranks),
+        lambda *refs: slots_kernel(*refs[:2], ranks=ranks),
         (shape(layers, 256, dtype=jnp.int32),),
         (owner,),
     )
-    fields, first, wall = call(
-        source_kernel,
-        (shape(FIELD_ROWS, 128), shape(128, 128), shape(8, 256)),
-        (source, wall, to_left, to_right, from_left, from_right, displacement, shell_load, shell_stiffness),
-    )
-    fields_right, fields_left = leftward(fields), rightward(fields)
-    beyond = leftward(first, 2)
+    fields, first, shell, wall = call(
+        lambda *refs: source_kernel(*refs),
+        (shape(FIELD_ROWS, 128), shape(128, 128), shape(SHELL_ROWS, 128), shape(8, 256)),
+        (
+            source, wall, own_left, own_right, halo_mate, halo_other,
+            displacement, shell_load, shell_stiffness,
+        ),
+        late=(6, 7, 8),
+        stored=(6, 7, 8),
+        pairs=(4,),
+    )
+    beyond = lax.ppermute(first, "slab", [(i, i - 2) for i in range(2, ranks)])
+    fields_other, fields_mate = with_other(fields), with_mate(fields)
+    shell_other, shell_mate = with_other(shell), with_mate(shell)
     payload, pressure_basis = call(
         lambda *refs: pressure_kernel(*refs, ranks=ranks),
-        (shape(ranks, 8, 128), shape(PITERS, *pressure_shift.shape)),
+        (shape(ranks, 8, 128), pltpu.HBM((PITERS, *pressure_shift.shape), F32)),
         (
-            fields, fields_left, fields_right, beyond,
-            pressure_shift, shift_left, shift_right,
+            fields, fields_mate, fields_other, beyond, pressure_shift, shift_mate, shift_other,
             wall, owner, slots, node, weight,
         ),
+        late=(3, 4),
+        stored=(4,),
+        pairs=(1, 5),
+        direct=(1,),
         scratch=(
             pltpu.VMEM((PITERS, 13, 64, 256), F32),
             pltpu.VMEM((12, 64, 256), F32),
             pltpu.VMEM((12, 64, 256), F32),
+            pltpu.SemaphoreType.DMA((PITERS,)),
         ),
     )
     received = lax.all_to_all(payload, "slab", split_axis=0, concat_axis=0, tiled=True)
     payload, shell_basis, factors = call(
         lambda *refs: shell_kernel(*refs, ranks=ranks),
-        (shape(ranks, 16, 128), shape(SITERS, *displacement.shape), shape(8, 128)),
+        (shape(ranks, 16, 128), pltpu.HBM((SITERS, *displacement.shape), F32), shape(8, 128)),
         (
-            received, fields, fields_left, fields_right,
-            shell_stiffness, stiffness_left, stiffness_right,
+            received, shell, shell_mate, shell_other,
             displacement, residual_prev, solved_prev, residual_history, solved_history,
         ),
+        late=(0, 4, 5, 6, 7, 8),
+        stored=(4, 5, 6, 7, 8),
+        pairs=(2,),
+        direct=(1,),
         scratch=(
             pltpu.VMEM((SITERS, 72, 1024), F32),
             pltpu.VMEM((72, 1024), F32),
             pltpu.VMEM((72, 1024), F32),
             pltpu.VMEM((8, 8 * 48, 128), F32),
+            pltpu.SemaphoreType.DMA((SITERS, 3)),
         ),
     )
     answers = lax.all_to_all(payload, "slab", split_axis=0, concat_axis=0, tiled=True)
-    (pressure,) = call(combine_kernel, (shape(*pressure_shift.shape),), (pressure_basis, factors))
+    (pressure,) = call(
+        combine_kernel,
+        (shape(*pressure_shift.shape),),
+        (pressure_basis, factors),
+        late=(0,),
+        stored=(0,),
+    )
     new_displacement, wall_displacement = call(
         lambda *refs: update_kernel(*refs, ranks=ranks),
         (shape(*displacement.shape), shape(3, owner_rank.shape[0])),
         (answers, shell_basis, displacement, solved_prev, solved_history, owner, slots),
+        late=(0, 1, 2, 3, 4),
+        stored=(1, 2, 3, 4),
     )
     return (pressure, new_displacement, wall_displacement)
 

time: 92.5 us -> 71.2 us (0.77)
  starting transfers between devices: 37.5 us -> 22.2 us
  local copies, waits for them, and re-layouts: 15.2 us -> 0.57 us
  Pallas kernels: 14.7 us -> 20.7 us
  waiting for transfers between devices: 22.5 us -> 25.7 us
    unnamed x57 -> x9, local copies, waits for them, and re-layouts: 15.2 us -> 0.54 us
    ppermute x9, starting transfers between devices: 23.9 us -> 11.6 us  [the longest x4 7.67 us: with_mate(): return lax.ppermute(values, 'slab', [(i, i ^ 1) for i in range(ranks)])]
    pallas_call x7, Pallas kernels: 14.7 us -> 20.7 us  [call(): pl.pallas_call(body, out_shape=outs, in_specs=[any_space if i in outside...]
    all_to_all x2, waiting for transfers between devices: 11 us -> 15.3 us  [on_device(): lax.all_to_all(payload, 'slab', split_axis=0, concat_axis=0, tiled=True)]
    all_to_all x2, starting transfers between devices: 13.7 us -> 10.6 us  [on_device(): lax.all_to_all(payload, 'slab', split_axis=0, concat_axis=0, tiled=True)]
    ppermute x9, waiting for transfers between devices: 11.5 us -> 10.5 us  [the longest x1 10 us: on_device(): beyond = lax.ppermute(first, 'slab', [(i, i - 2) for i in range(2, ranks)])]
  transfers between devices with their start and end apart: 11 -> 11, of which waited for: 5 -> 4; matrix products, arithmetic and copies ran while one was open for 1% -> 2% of each run, Pallas kernels for 1% -> 5%
where the time goes in v2:
time: 71.2 us; the launch traced here: 70.7 us
  waiting for transfers between devices  25.7 us (36%)
  starting transfers between devices  22.2 us (31%)
  Pallas kernels  20.7 us (29%)
  between operations  0.84 us (1%)
    pallas_call x7, Pallas kernels, call(): pl.pallas_call(body, out_shape=outs, in_specs=[any_space if i in outside...  20.7 us
    all_to_all x2, waiting for transfers between devices, on_device(): lax.all_to_all(payload, 'slab', split_axis=0, concat_axis=0, tiled=True)  15.3 us
    all_to_all x2, starting transfers between devices, on_device(): lax.all_to_all(payload, 'slab', split_axis=0, concat_axis=0, tiled=True)  10.6 us
    ppermute x1, waiting for transfers between devices, on_device(): beyond = lax.ppermute(first, 'slab', [(i, i - 2) for i in range(2, ranks)])  10 us
    ppermute x4, starting transfers between devices, with_mate(): return lax.ppermute(values, 'slab', [(i, i ^ 1) for i in range(ranks)])  7.67 us
    ppermute x4, starting transfers between devices, with_other(): return lax.ppermute(values, 'slab', pairs + [(j, i) for i, j in pairs])  2.65 us
  transfers between devices with their start and end apart: 11, of which 4 were waited for; matrix products, arithmetic and copies ran while one was open for 2% of the time, Pallas kernels for 5%

profile of v2, /device:TPU:0, one launch (start us, length us, event | category | flops | bytes accessed | tf_op | source)
XLA Modules:
  0.0 70.7 jit_solution(15638394888897282379)
XLA Ops:
  0.6 1.9 %shard_map.139 = (f32[288,128]{1,0:T(8,128)S(1)}, f32[288,128]{1,0:T(8,128)S(1)}, f32[64,256]{1,0:T(8,128)S(1)}, f32[64,256]{1,0:T(8,128)S(1)}, f32[4,64,256]{2,1,0:T(8,128)S(1)}, /*index=5*/f32[8,256]{1,0:T(8,128)S(1)}) custom-call(f32[3,4,64,256]{3,2,1,0:T(8,128)} %refs_0_.1, f32[3,8,1024]{2,1,0:T(8,128)} %refs_2_.1), custom_call_target="tpu_custom_call" | custom-call | flops 1000000000 | tf_op jit(solution)/shard_map/pallas_call | solution.py:111
  2.6 0.5 collective-permute-start
  3.1 0.7 collective-permute-start.1
  3.8 3.9 %collective-permute-start.5 = (f32[4,64,256]{2,1,0:T(8,128)S(1)}, f32[4,64,256]{2,1,0:T(8,128)S(1)}, u32[]{:S(2)}, u32[]{:S(2)}) collective-permute-start(f32[4,64,256]{2,1,0:T(8,128)S(1)} %copy-done.3), channel_id=1, source_target_pairs={{0,1},{1,0},{2,3},{3,2},{4,5},{5,4},{6,7},{7,6},{8,9},{9,8},{10,11... | collective-permute-start | bytes 786440 | tf_op jit(solution)/shard_map/ppermute | solution.py:701
  7.7 0.7 collective-permute-start.6
  8.4 1.1 %shard_map.140 = (f32[512,128]{1,0:T(8,128)S(1)}, f32[128,128]{1,0:T(8,128)S(1)}, f32[256,128]{1,0:T(8,128)S(1)}, f32[8,256]{1,0:T(8,128)S(1)}) custom-call(f32[4,64,256]{2,1,0:T(8,128)S(1)} %get-tuple-element.20.refs_0_, f32[8,256]{1,0:T(8,128)S(1)} %get-tuple-element.21.refs_1_, f32[64,256]{1,0:T(8,128)S(1)} %get-tuple-element.22.refs_2_, ...), custom_call_target="tpu_custom_call" | custom-call | flops 1000000000 | tf_op jit(solution)/shard_map/pallas_call | solution.py:111
  9.6 2.9 %collective-permute-start.2 = (f32[512,128]{1,0:T(8,128)S(1)}, f32[512,128]{1,0:T(8,128)S(1)}, u32[]{:S(2)}, u32[]{:S(2)}) collective-permute-start(f32[512,128]{1,0:T(8,128)S(1)} %get-tuple-element.26.refs_0_), channel_id=1, source_target_pairs={{0,1},{1,0},{2,3},{3,2},{4,5},{5,4},{6,7},{7,6},{8,9},{9,8},{10,11... | collective-permute-start | bytes 786440 | tf_op jit(solution)/shard_map/ppermute | solution.py:701
  12.5 0.7 collective-permute-start.3
  13.2 0.5 broadcast.3
  13.7 0.7 reduce.3
  14.4 1.3 %collective-permute-start.4 = (f32[128,128]{1,0:T(8,128)S(1)}, f32[128,128]{1,0:T(8,128)S(1)}, u32[]{:S(2)}, u32[]{:S(2)}) collective-permute-start(f32[128,128]{1,0:T(8,128)S(1)} %get-tuple-element.27), channel_id=1, source_target_pairs={{2,0},{3,1},{4,2},{5,3},{6,4},{7,5},{8,6},{9,7},{10,8},{11,9},{12,... | collective-permute-start | bytes 196616 | tf_op jit(solution)/shard_map/ppermute | solution.py:740
  15.7 0.2 shard_map.141.refs_9_.refs_6_
  15.9 10.0 %collective-permute-done.4.refs_3_ = f32[128,128]{1,0:T(8,128)S(1)} collective-permute-done((f32[128,128]{1,0:T(8,128)S(1)}, f32[128,128]{1,0:T(8,128)S(1)}, u32[]{:S(2)}, u32[]{:S(2)}) %collective-permute-start.4) | collective-permute-done | bytes 65568 | tf_op jit(solution)/shard_map/ppermute | solution.py:740
  26.0 5.1 %shard_map.142 = (f32[32,8,128]{2,1,0:T(8,128)}, f32[5,4,64,256]{3,2,1,0:T(8,128)}) custom-call(f32[512,128]{1,0:T(8,128)S(1)} %get-tuple-element.26.refs_0_, f32[512,128]{1,0:T(8,128)S(1)} %collective-permute-done.2.refs_1_, f32[512,128]{1,0:T(8,128)S(1)} %collective-permute-done.3.refs_2_, f32[128,128]{1,0:T(8,128)S(1)} %collective-permute-done.4.refs_3_, ...), custom_call_target="tpu_custom_call" | custom-call | flops 1000000000 | tf_op jit(solution)/shard_map/pallas_call | solution.py:111
  31.1 5.5 %all-to-all-start = ((f32[32,8,128]{2,1,0:T(8,128)}), f32[32,8,128]{2,1,0:T(8,128)S(1)}, u32[]{:S(2)}, u32[]{:S(2)}) async-start(f32[32,8,128]{2,1,0:T(8,128)} %get-tuple-element.30), calls=%async_computation | async-start | bytes 262144 | tf_op jit(solution)/shard_map/all_to_all | solution.py:761
  36.6 0.3 collective-permute-start.7
  36.9 0.7 collective-permute-start.8
  37.6 0.4 collective-permute-done.7.refs_2_
  38.0 6.8 %all-to-all-done.refs_0_ = f32[32,8,128]{2,1,0:T(8,128)S(1)} async-done(((f32[32,8,128]{2,1,0:T(8,128)}), f32[32,8,128]{2,1,0:T(8,128)S(1)}, u32[]{:S(2)}, u32[]{:S(2)}) %all-to-all-start) | async-done | bytes 131104 | tf_op jit(solution)/shard_map/all_to_all | solution.py:761
  44.8 7.7 %shard_map.143 = (f32[32,16,128]{2,1,0:T(8,128)}, f32[8,3,8,1024]{3,2,1,0:T(8,128)}, f32[8,128]{1,0:T(8,128)S(1)}) custom-call(f32[32,8,128]{2,1,0:T(8,128)S(1)} %all-to-all-done.refs_0_, f32[256,128]{1,0:T(8,128)S(1)} %get-tuple-element.31.refs_1_, f32[256,128]{1,0:T(8,128)S(1)} %collective-permute-done.7.refs_2_, ...), custom_call_target="tpu_custom_call" | custom-call | flops 1000000000 | tf_op jit(solution)/shard_map/pallas_call | solution.py:111
  52.5 5.1 %all-to-all-start.1 = ((f32[32,16,128]{2,1,0:T(8,128)}), f32[32,16,128]{2,1,0:T(8,128)S(1)}, u32[]{:S(2)}, u32[]{:S(2)}) async-start(f32[32,16,128]{2,1,0:T(8,128)} %get-tuple-element.33), calls=%async_computation.1 | async-start | bytes 524288 | tf_op jit(solution)/shard_map/all_to_all | solution.py:781
  57.6 2.1 %shard_map.144 = f32[4,64,256]{2,1,0:T(8,128)} custom-call(f32[5,4,64,256]{3,2,1,0:T(8,128)} %get-tuple-element.29.refs_0_, f32[8,128]{1,0:T(8,128)S(1)} %get-tuple-element.32.refs_1_), custom_call_target="tpu_custom_call" | custom-call | flops 1000000000 | tf_op jit(solution)/shard_map/pallas_call | solution.py:111
  59.8 8.4 %all-to-all-done.1.refs_0_ = f32[32,16,128]{2,1,0:T(8,128)S(1)} async-done(((f32[32,16,128]{2,1,0:T(8,128)}), f32[32,16,128]{2,1,0:T(8,128)S(1)}, u32[]{:S(2)}, u32[]{:S(2)}) %all-to-all-start.1) | async-done | bytes 262176 | tf_op jit(solution)/shard_map/all_to_all | solution.py:781
  68.2 2.5 %shard_map.145 = (f32[3,8,1024]{2,1,0:T(8,128)}, f32[3,1024]{1,0:T(4,128)}) custom-call(f32[32,16,128]{2,1,0:T(8,128)S(1)} %all-to-all-done.1.refs_0_, f32[8,3,8,1024]{3,2,1,0:T(8,128)} %get-tuple-element.34.refs_1_, f32[3,8,1024]{2,1,0:T(8,128)} %refs_2_.1, f32[3,8,1024]{2,1,0:T(8,128)} %refs_3_.1, f32[4,3,8,1024]{3,2,1,0:T(8,128)} %refs_4_.5, ...), custom_call_target="tpu_custom_call" | custom-call | flops 1000000000 | tf_op jit(solution)/shard_map/pallas_call | solution.py:111
  (18 shorter events, 0.1 us)
Async XLA Ops:
  0.6 3.1 %copy-start.3 = (f32[4,64,256]{2,1,0:T(8,128)S(1)}, f32[4,64,256]{2,1,0:T(8,128)}, u32[]{:S(2)}) copy-start(f32[4,64,256]{2,1,0:T(8,128)} %refs_4_.3) | copy-start | bytes 786436
  2.6 5.8 %collective-permute-start = (f32[288,128]{1,0:T(8,128)S(1)}, f32[288,128]{1,0:T(8,128)S(1)}, u32[]{:S(2)}, u32[]{:S(2)}) collective-permute-start(f32[288,128]{1,0:T(8,128)S(1)} %get-tuple-element.24), channel_id=1, source_target_pairs={{0,1},{1,0},{2,3},{3,2},{4,5},{5,4},{6,7},{7,6},{8,9},{9,8},{10,11... | collective-permute-start | bytes 442376 | tf_op jit(solution)/shard_map/ppermute | solution.py:701
  3.1 5.3 %collective-permute-start.1 = (f32[288,128]{1,0:T(8,128)S(1)}, f32[288,128]{1,0:T(8,128)S(1)}, u32[]{:S(2)}, u32[]{:S(2)}) collective-permute-start(f32[288,128]{1,0:T(8,128)S(1)} %get-tuple-element.25), channel_id=1, source_target_pairs={{1,2},{3,4},{5,6},{7,8},{9,10},{11,12},{13,14},{15,16},{17,18},{19... | collective-permute-start | bytes 442376 | tf_op jit(solution)/shard_map/ppermute | solution.py:705
  3.8 22.2 %collective-permute-start.5 = (f32[4,64,256]{2,1,0:T(8,128)S(1)}, f32[4,64,256]{2,1,0:T(8,128)S(1)}, u32[]{:S(2)}, u32[]{:S(2)}) collective-permute-start(f32[4,64,256]{2,1,0:T(8,128)S(1)} %copy-done.3), channel_id=1, source_target_pairs={{0,1},{1,0},{2,3},{3,2},{4,5},{5,4},{6,7},{7,6},{8,9},{9,8},{10,11... | collective-permute-start | bytes 786440 | tf_op jit(solution)/shard_map/ppermute | solution.py:701
  7.7 18.3 %collective-permute-start.6 = (f32[4,64,256]{2,1,0:T(8,128)S(1)}, f32[4,64,256]{2,1,0:T(8,128)S(1)}, u32[]{:S(2)}, u32[]{:S(2)}) collective-permute-start(f32[4,64,256]{2,1,0:T(8,128)S(1)} %copy-done.3), channel_id=1, source_target_pairs={{1,2},{3,4},{5,6},{7,8},{9,10},{11,12},{13,14},{15,16},{17,18},{19... | collective-permute-start | bytes 786440 | tf_op jit(solution)/shard_map/ppermute | solution.py:705
  8.4 5.3 %copy-start = (s32[1024,1]{0,1:T(1,128)S(1)}, s32[1024,1]{0,1:T(1,128)}, u32[]{:S(2)}) copy-start(s32[1024,1]{0,1:T(1,128)} %param.14) | copy-start | bytes 12292
  8.4 5.9 %copy-start.1 = (s32[1024]{0:T(1024)S(1)}, s32[1024]{0:T(1024)}, u32[]{:S(2)}) copy-start(s32[1024]{0:T(1024)} %param.15) | copy-start | bytes 12292
  8.4 6.0 %copy-start.2 = (s32[1024]{0:T(1024)S(1)}, s32[1024]{0:T(1024)}, u32[]{:S(2)}) copy-start(s32[1024]{0:T(1024)} %param.16) | copy-start | bytes 12292
  9.6 16.4 %collective-permute-start.2 = (f32[512,128]{1,0:T(8,128)S(1)}, f32[512,128]{1,0:T(8,128)S(1)}, u32[]{:S(2)}, u32[]{:S(2)}) collective-permute-start(f32[512,128]{1,0:T(8,128)S(1)} %get-tuple-element.26.refs_0_), channel_id=1, source_target_pairs={{0,1},{1,0},{2,3},{3,2},{4,5},{5,4},{6,7},{7,6},{8,9},{9,8},{10,11... | collective-permute-start | bytes 786440 | tf_op jit(solution)/shard_map/ppermute | solution.py:701
  12.5 13.5 %collective-permute-start.3 = (f32[512,128]{1,0:T(8,128)S(1)}, f32[512,128]{1,0:T(8,128)S(1)}, u32[]{:S(2)}, u32[]{:S(2)}) collective-permute-start(f32[512,128]{1,0:T(8,128)S(1)} %get-tuple-element.26.refs_0_), channel_id=1, source_target_pairs={{1,2},{3,4},{5,6},{7,8},{9,10},{11,12},{13,14},{15,16},{17,18},{19... | collective-permute-start | bytes 786440 | tf_op jit(solution)/shard_map/ppermute | solution.py:705
  14.4 11.6 %collective-permute-start.4 = (f32[128,128]{1,0:T(8,128)S(1)}, f32[128,128]{1,0:T(8,128)S(1)}, u32[]{:S(2)}, u32[]{:S(2)}) collective-permute-start(f32[128,128]{1,0:T(8,128)S(1)} %get-tuple-element.27), channel_id=1, source_target_pairs={{2,0},{3,1},{4,2},{5,3},{6,4},{7,5},{8,6},{9,7},{10,8},{11,9},{12,... | collective-permute-start | bytes 196616 | tf_op jit(solution)/shard_map/ppermute | solution.py:740
  31.1 13.7 %all-to-all-start = ((f32[32,8,128]{2,1,0:T(8,128)}), f32[32,8,128]{2,1,0:T(8,128)S(1)}, u32[]{:S(2)}, u32[]{:S(2)}) async-start(f32[32,8,128]{2,1,0:T(8,128)} %get-tuple-element.30), calls=%async_computation | async-start | bytes 262144 | tf_op jit(solution)/shard_map/all_to_all | solution.py:761
  36.6 1.4 %collective-permute-start.7 = (f32[256,128]{1,0:T(8,128)S(1)}, f32[256,128]{1,0:T(8,128)S(1)}, u32[]{:S(2)}, u32[]{:S(2)}) collective-permute-start(f32[256,128]{1,0:T(8,128)S(1)} %get-tuple-element.31.refs_1_), channel_id=1, source_target_pairs={{0,1},{1,0},{2,3},{3,2},{4,5},{5,4},{6,7},{7,6},{8,9},{9,8},{10,11... | collective-permute-start | bytes 393224 | tf_op jit(solution)/shard_map/ppermute | solution.py:701
  36.9 1.1 %collective-permute-start.8 = (f32[256,128]{1,0:T(8,128)S(1)}, f32[256,128]{1,0:T(8,128)S(1)}, u32[]{:S(2)}, u32[]{:S(2)}) collective-permute-start(f32[256,128]{1,0:T(8,128)S(1)} %get-tuple-element.31.refs_1_), channel_id=1, source_target_pairs={{1,2},{3,4},{5,6},{7,8},{9,10},{11,12},{13,14},{15,16},{17,18},{19... | collective-permute-start | bytes 393224 | tf_op jit(solution)/shard_map/ppermute | solution.py:705
  52.5 15.7 %all-to-all-start.1 = ((f32[32,16,128]{2,1,0:T(8,128)}), f32[32,16,128]{2,1,0:T(8,128)S(1)}, u32[]{:S(2)}, u32[]{:S(2)}) async-start(f32[32,16,128]{2,1,0:T(8,128)} %get-tuple-element.33), calls=%async_computation.1 | async-start | bytes 524288 | tf_op jit(solution)/shard_map/all_to_all | solution.py:781

commit v3 on v2

--- a/solution.py
+++ b/solution.py
@@ -73,8 +73,21 @@
         return self.places
 
 
+class Either:
+    def __init__(self, which, first, second):
+        self.which, self.first, self.second = which, first, second
+
+    def __getitem__(self, index):
+        return jnp.where(self.which, self.first[index], self.second[index])
+
+
+def sides(to_mate, to_other):
+    even = even_device()
+    return Either(even, to_other, to_mate), Either(even, to_mate, to_other)
+
+
 def call(
-    kernel, outs, args, late=(), pairs=(), direct=(), stored=(), scratch=(),
+    kernel, outs, args, late=(), outer=(), pairs=(), direct=(), stored=(), scratch=(),
     flops=1000000000, limit=48.0,
 ):
     count, made = len(args), len(outs)
@@ -111,7 +124,7 @@
     return pl.pallas_call(
         body,
         out_shape=outs,
-        in_specs=[any_space if i in outside else VMEM for i in range(count)],
+        in_specs=[any_space if i in outside or i in outer else VMEM for i in range(count)],
         out_specs=tuple(any_space if i in direct else VMEM for i in range(made)),
         scratch_shapes=list(scratch) + extra,
         compiler_params=pltpu.CompilerParams(vmem_limit_bytes=int(limit * 1024 * 1024)),
@@ -188,9 +201,15 @@
 
 
 def fluid_kernel(
-    velocity, displacement, to_mate, to_other, own_left, own_right, source, wall
+    velocity_in, displacement_in, to_mate, to_other, own_left, own_right, source, wall,
+    velocity, displacement, arrived,
 ):
-    velocity, displacement = velocity(), displacement()
+    copies = [pltpu.make_async_copy(velocity_in, velocity, arrived.at[0, 0])]
+    copies.append(pltpu.make_async_copy(displacement_in, displacement, arrived.at[3, 0]))
+    for copy in copies:
+        copy.start()
+    for copy in copies:
+        copy.wait()
     even = even_device()
     layers = velocity.shape[1]
     last = layers - 1
@@ -244,7 +263,9 @@
 
 
 def shell_beside(field):
-    return ahead(field, 0) + behind(field, 0) + ahead(field, 1) + behind(field, 1)
+    rows = field.shape[0]
+    beside = pltpu.roll(field, rows - 1, 0) + pltpu.roll(field, 1, 0)
+    return beside + ahead(field, 1) + behind(field, 1)
 
 
 def source_kernel(
@@ -252,7 +273,6 @@
     fields, first, shell, wall_out,
 ):
     from_left, from_right = halo()
-    displacement, load, stiffness = displacement(), load(), stiffness()
     layers = source.shape[0]
     last = layers - 1
     left1, left2 = halves(from_left, 0), halves(from_left, H2_AT)
@@ -338,13 +358,12 @@
 
 
 def pressure_kernel(
-    own, halo, beyond, shift, shift_halo,
+    own, mate, other, beyond, shift, shift_mate, shift_other,
     wall, owner, slots, node, weight,
     payload, basis, work, diagonal, off, sent, *, ranks,
 ):
-    left, right = halo()
-    beyond, shift = beyond(), shift()
-    shift_left, shift_right = shift_halo()
+    left, right = sides(mate, other)
+    shift_left, shift_right = sides(shift_mate, shift_other)
     layers = shift.shape[0]
     for x in range(layers):
         work[0, x] = halves(left, x * 128)
@@ -356,6 +375,11 @@
         inside = values > 0.0
         diagonal[x] = jnp.where(inside, values + 6.0, 0.0)
         off[x] = jnp.where(inside, 1.0, 0.0)
+    copies = [
+        pltpu.make_async_copy(work.at[k, pl.ds(4, layers)], basis.at[k], sent.at[k])
+        for k in range(PITERS)
+    ]
+    copies[0].start()
     for step in range(1, PITERS):
         for x in range(step, 13 - step):
             now = work[step - 1, x]
@@ -366,12 +390,7 @@
             if step > 1:
                 value = value - P_BACK[step - 2] * work[step - 2, x]
             work[step, x] = value
-    copies = [
-        pltpu.make_async_copy(work.at[k, pl.ds(4, layers)], basis.at[k], sent.at[k])
-        for k in range(PITERS)
-    ]
-    for copy in copies:
-        copy.start()
+        copies[step].start()
     tile = jnp.zeros((8, 128), F32)
     for i in range(PITERS):
         for j in range(i, PITERS):
@@ -475,7 +494,7 @@
 
 
 def shell_kernel(
-    received, own, halo,
+    received, own, mate, other,
     displacement, residual_prev, solved_prev, residual_history, solved_history,
     payload, basis, factors, work, diagonal, off, table, sent, *, ranks,
 ):
@@ -502,7 +521,7 @@
             chunks.append(chunk)
         return jnp.concatenate(chunks, 1)
 
-    left, right = halo()
+    left, right = sides(mate, other)
     weights = gathered(3)
     entries = ranks * CAP
     target = lax.broadcasted_iota(jnp.int32, (64, entries), 0)
@@ -521,11 +540,11 @@
         code = ((numbers >> 7) & 7) * 8 + (numbers >> 10)
         spot = jnp.where(low == (numbers & 127), 1.0, 0.0).astype(BF16)
         match = target == code
-        pieces = pieces_of(jnp.concatenate(rows, 0), 3)
+        pieces = pieces_of(jnp.concatenate(rows, 0), 2)
         left_rows = jnp.concatenate(
             [jnp.where(match, piece[c : c + 1], 0.0) for piece in pieces for c in range(3)], 0
         )
-        scattered = added(dot(left_rows.astype(BF16), spot, True), 3)
+        scattered = added(dot(left_rows.astype(BF16), spot, True), 2)
         share = dot(jnp.where(match, weights[j : j + 1, :], 0.0).astype(BF16), spot, True)
         share = 1.0 / jnp.maximum(share, 1.0)
         ref = (left, own, right)[j]
@@ -547,32 +566,41 @@
         for c in range(3):
             diagonal[c * 24 + j * 8 : c * 24 + j * 8 + 8, :] = main
             off[c * 24 + j * 8 : c * 24 + j * 8 + 8, :] = side
+    copies = [
+        pltpu.make_async_copy(work.at[k, pl.ds(c * 24 + 8, 8)], basis.at[k, c], sent.at[k, c])
+        for k in range(SITERS)
+        for c in range(3)
+    ]
     for step in range(1, SITERS):
         now = work[step - 1]
         value = (diagonal[...] - S_SHIFT[step - 1]) * now - off[...] * shell_beside(now)
         if step > 1:
             value = value - S_BACK[step - 2] * work[step - 2]
         work[step] = value
-    copies = [
-        pltpu.make_async_copy(work.at[k, pl.ds(c * 24 + 8, 8)], basis.at[k, c], sent.at[k, c])
-        for k in range(SITERS)
-        for c in range(3)
-    ]
-    for copy in copies:
+        for copy in copies[step * 3 - 3 : step * 3]:
+            copy.start()
+    for copy in copies[-3:]:
         copy.start()
-    displacement, residual_prev, solved_prev = displacement(), residual_prev(), solved_prev()
-    residual_history, solved_history = residual_history(), solved_history()
-    def basis_tile(k, c):
-        return work[k, c * 24 + 8 : c * 24 + 16, :]
-
-    vectors = [lambda c, k=k: basis_tile(k, c) for k in range(SITERS)]
-    vectors.append(lambda c: residual_prev[c])
-    vectors += [lambda c, k=k: residual_history[k, c] for k in range(residual_history.shape[0])]
+    def basis_tile(k, c, columns=slice(None)):
+        return work[k, c * 24 + 8 : c * 24 + 16, columns]
+
+    def tile_of(ref):
+        return lambda c, columns=slice(None): ref[c, :, columns]
+
+    vectors = [lambda c, columns=slice(None), k=k: basis_tile(k, c, columns) for k in range(SITERS)]
+    vectors.append(tile_of(residual_prev))
+    vectors += [tile_of(residual_history.at[k]) for k in range(residual_history.shape[0])]
     tile = jnp.zeros((16, 128), F32)
-    for i in range(len(vectors)):
-        for j in range(i, len(vectors)):
-            total = sum(vectors[i](c) * vectors[j](c) for c in range(3))
-            tile = place_pair(tile, i, (96 + j, j, 96 + i), whole(fold(total)))
+    pairs = [(i, j) for i in range(len(vectors)) for j in range(i, len(vectors))]
+    for some in (pairs[:46], pairs[46:]):
+        totals = [0.0] * len(some)
+        used = sorted({v for pair in some for v in pair})
+        for c in range(3):
+            for k in range(8):
+                tiles = {v: vectors[v](c, slice(k * 128, k * 128 + 128)) for v in used}
+                totals = [total + tiles[i] * tiles[j] for total, (i, j) in zip(totals, some)]
+        for total, (i, j) in zip(totals, some):
+            tile = place_pair(tile, i, (96 + j, j, 96 + i), whole(total))
     top = SITERS - 1
     total = 0.0
     for c in range(3):
@@ -632,7 +660,7 @@
     steps = eliminate(system, gram[0], 0)
     down = lax.broadcasted_iota(jnp.int32, (16, 1), 0)
     steps = jnp.where(down < SITERS, steps, 0.0)
-    base, count = SITERS, 1 + solved_history.place.shape[0]
+    base, count = SITERS, 1 + solved_history.shape[0]
     with_moved = sum(steps[k : k + 1] * gram[k] for k in range(SITERS))
     with_newest = with_moved - gram[base]
     newest_moved = jnp.sum(steps * with_newest, 0, keepdims=True)
@@ -652,8 +680,6 @@
             jnp.where(down < base + count, coefficients, jnp.where(down == base + count, -newest, 0.0)),
         ),
     )
-    basis = basis()
-    displacement, solved_prev, solved_history = displacement(), solved_prev(), solved_history()
     for c in range(3):
         total = row_of(factors, base) * displacement[c]
         for k in range(SITERS):
@@ -716,8 +742,13 @@
             shape(*velocity.shape[1:]), shape(8, 256),
         ),
         (velocity, displacement),
-        late=(0, 1),
+        outer=(0, 1),
         stored=(0, 1),
+        scratch=(
+            pltpu.VMEM(velocity.shape, F32),
+            pltpu.VMEM(displacement.shape, F32),
+            pltpu.SemaphoreType.DMA((4, max(layers, 1))),
+        ),
     )
     halo_other, halo_mate = with_other(to_other), with_mate(to_mate)
     shift_other, shift_mate = with_other(pressure_shift), with_mate(pressure_shift)
@@ -733,8 +764,6 @@
             source, wall, own_left, own_right, halo_mate, halo_other,
             displacement, shell_load, shell_stiffness,
         ),
-        late=(6, 7, 8),
-        stored=(6, 7, 8),
         pairs=(4,),
     )
     beyond = lax.ppermute(first, "slab", [(i, i - 2) for i in range(2, ranks)])
@@ -747,9 +776,6 @@
             fields, fields_mate, fields_other, beyond, pressure_shift, shift_mate, shift_other,
             wall, owner, slots, node, weight,
         ),
-        late=(3, 4),
-        stored=(4,),
-        pairs=(1, 5),
         direct=(1,),
         scratch=(
             pltpu.VMEM((PITERS, 13, 64, 256), F32),
@@ -766,9 +792,7 @@
             received, shell, shell_mate, shell_other,
             displacement, residual_prev, solved_prev, residual_history, solved_history,
         ),
-        late=(0, 4, 5, 6, 7, 8),
-        stored=(4, 5, 6, 7, 8),
-        pairs=(2,),
+        late=(0,),
         direct=(1,),
         scratch=(
             pltpu.VMEM((SITERS, 72, 1024), F32),
@@ -790,8 +814,7 @@
         lambda *refs: update_kernel(*refs, ranks=ranks),
         (shape(*displacement.shape), shape(3, owner_rank.shape[0])),
         (answers, shell_basis, displacement, solved_prev, solved_history, owner, slots),
-        late=(0, 1, 2, 3, 4),
-        stored=(1, 2, 3, 4),
+        late=(0,),
     )
     return (pressure, new_displacement, wall_displacement)
 

time: 71.2 us -> 67.8 us (0.952)
  Pallas kernels: 20.7 us -> 17.4 us
    pallas_call x7, Pallas kernels: 20.7 us -> 17.4 us  [call(): pl.pallas_call(body, out_shape=outs, in_specs=[any_space if i in outside...]
  transfers between devices with their start and end apart: 11 -> 11, of which waited for: 4 -> 4; matrix products, arithmetic and copies ran while one was open for 2% -> 2% of each run, Pallas kernels for 5% -> 4%
where the time goes in v3:
time: 67.8 us; the launch traced here: 67.4 us
  waiting for transfers between devices  25.6 us (38%)
  starting transfers between devices  22.2 us (33%)
  Pallas kernels  17.4 us (26%)
  between operations  0.94 us (1%)
    pallas_call x7, Pallas kernels, call(): pl.pallas_call(body, out_shape=outs, in_specs=[any_space if i in outside...  17.4 us
    all_to_all x2, waiting for transfers between devices, on_device(): lax.all_to_all(payload, 'slab', split_axis=0, concat_axis=0, tiled=True)  15.2 us
    all_to_all x2, starting transfers between devices, on_device(): lax.all_to_all(payload, 'slab', split_axis=0, concat_axis=0, tiled=True)  10.6 us
    ppermute x1, waiting for transfers between devices, on_device(): beyond = lax.ppermute(first, 'slab', [(i, i - 2) for i in range(2, ranks)])  10 us
    ppermute x4, starting transfers between devices, with_mate(): return lax.ppermute(values, 'slab', [(i, i ^ 1) for i in range(ranks)])  7.67 us
    ppermute x4, starting transfers between devices, with_other(): return lax.ppermute(values, 'slab', pairs + [(j, i) for i, j in pairs])  2.65 us
  transfers between devices with their start and end apart: 11, of which 4 were waited for; matrix products, arithmetic and copies ran while one was open for 2% of the time, Pallas kernels for 4%

profile of v3, /device:TPU:0, one launch (start us, length us, event | category | flops | bytes accessed | tf_op | source)
XLA Modules:
  0.0 67.4 jit_solution(10082136867334679774)
XLA Ops:
  0.7 2.1 %shard_map.139 = (f32[288,128]{1,0:T(8,128)S(1)}, f32[288,128]{1,0:T(8,128)S(1)}, f32[64,256]{1,0:T(8,128)S(1)}, f32[64,256]{1,0:T(8,128)S(1)}, f32[4,64,256]{2,1,0:T(8,128)S(1)}, /*index=5*/f32[8,256]{1,0:T(8,128)S(1)}) custom-call(f32[3,4,64,256]{3,2,1,0:T(8,128)} %refs_0_.1, f32[3,8,1024]{2,1,0:T(8,128)} %refs_2_.1), custom_call_target="tpu_custom_call" | custom-call | flops 1000000000 | tf_op jit(solution)/shard_map/pallas_call | solution.py:124
  2.8 0.5 collective-permute-start
  3.3 0.7 collective-permute-start.1
  3.9 3.9 %collective-permute-start.5 = (f32[4,64,256]{2,1,0:T(8,128)S(1)}, f32[4,64,256]{2,1,0:T(8,128)S(1)}, u32[]{:S(2)}, u32[]{:S(2)}) collective-permute-start(f32[4,64,256]{2,1,0:T(8,128)S(1)} %copy-done.2), channel_id=1, source_target_pairs={{0,1},{1,0},{2,3},{3,2},{4,5},{5,4},{6,7},{7,6},{8,9},{9,8},{10,11... | collective-permute-start | bytes 786440 | tf_op jit(solution)/shard_map/ppermute | solution.py:727
  7.9 0.7 collective-permute-start.6
  8.6 0.6 shard_map.140
  9.2 2.9 %collective-permute-start.2 = (f32[512,128]{1,0:T(8,128)S(1)}, f32[512,128]{1,0:T(8,128)S(1)}, u32[]{:S(2)}, u32[]{:S(2)}) collective-permute-start(f32[512,128]{1,0:T(8,128)S(1)} %get-tuple-element.26.refs_0_), channel_id=1, source_target_pairs={{0,1},{1,0},{2,3},{3,2},{4,5},{5,4},{6,7},{7,6},{8,9},{9,8},{10,11... | collective-permute-start | bytes 786440 | tf_op jit(solution)/shard_map/ppermute | solution.py:727
  12.1 0.7 collective-permute-start.3
  12.8 0.5 broadcast.3
  13.3 0.7 reduce.3
  14.0 1.3 %collective-permute-start.4 = (f32[128,128]{1,0:T(8,128)S(1)}, f32[128,128]{1,0:T(8,128)S(1)}, u32[]{:S(2)}, u32[]{:S(2)}) collective-permute-start(f32[128,128]{1,0:T(8,128)S(1)} %get-tuple-element.27), channel_id=1, source_target_pairs={{2,0},{3,1},{4,2},{5,3},{6,4},{7,5},{8,6},{9,7},{10,8},{11,9},{12,... | collective-permute-start | bytes 196616 | tf_op jit(solution)/shard_map/ppermute | solution.py:769
  15.3 0.2 shard_map.141.refs_9_.refs_6_
  15.6 10.0 %collective-permute-done.4.refs_3_ = f32[128,128]{1,0:T(8,128)S(1)} collective-permute-done((f32[128,128]{1,0:T(8,128)S(1)}, f32[128,128]{1,0:T(8,128)S(1)}, u32[]{:S(2)}, u32[]{:S(2)}) %collective-permute-start.4) | collective-permute-done | bytes 65568 | tf_op jit(solution)/shard_map/ppermute | solution.py:769
  25.7 3.5 %shard_map.142 = (f32[32,8,128]{2,1,0:T(8,128)}, f32[5,4,64,256]{3,2,1,0:T(8,128)}) custom-call(f32[512,128]{1,0:T(8,128)S(1)} %get-tuple-element.26.refs_0_, f32[512,128]{1,0:T(8,128)S(1)} %collective-permute-done.2.refs_1_, f32[512,128]{1,0:T(8,128)S(1)} %collective-permute-done.3.refs_2_, f32[128,128]{1,0:T(8,128)S(1)} %collective-permute-done.4.refs_3_, ...), custom_call_target="tpu_custom_call" | custom-call | flops 1000000000 | tf_op jit(solution)/shard_map/pallas_call | solution.py:124
  29.1 5.5 %all-to-all-start = ((f32[32,8,128]{2,1,0:T(8,128)}), f32[32,8,128]{2,1,0:T(8,128)S(1)}, u32[]{:S(2)}, u32[]{:S(2)}) async-start(f32[32,8,128]{2,1,0:T(8,128)} %get-tuple-element.30), calls=%async_computation | async-start | bytes 262144 | tf_op jit(solution)/shard_map/all_to_all | solution.py:787
  34.6 0.3 collective-permute-start.7
  34.9 0.7 collective-permute-start.8
  35.6 0.4 collective-permute-done.7.refs_2_
  36.0 6.8 %all-to-all-done.refs_0_ = f32[32,8,128]{2,1,0:T(8,128)S(1)} async-done(((f32[32,8,128]{2,1,0:T(8,128)}), f32[32,8,128]{2,1,0:T(8,128)S(1)}, u32[]{:S(2)}, u32[]{:S(2)}) %all-to-all-start) | async-done | bytes 131104 | tf_op jit(solution)/shard_map/all_to_all | solution.py:787
  42.9 7.4 %shard_map.143 = (f32[32,16,128]{2,1,0:T(8,128)}, f32[8,3,8,1024]{3,2,1,0:T(8,128)}, f32[8,128]{1,0:T(8,128)S(1)}) custom-call(f32[32,8,128]{2,1,0:T(8,128)S(1)} %all-to-all-done.refs_0_, f32[256,128]{1,0:T(8,128)S(1)} %get-tuple-element.31.refs_1_, f32[256,128]{1,0:T(8,128)S(1)} %collective-permute-done.7.refs_2_, ...), custom_call_target="tpu_custom_call" | custom-call | flops 1000000000 | tf_op jit(solution)/shard_map/pallas_call | solution.py:124
  50.2 5.1 %all-to-all-start.1 = ((f32[32,16,128]{2,1,0:T(8,128)}), f32[32,16,128]{2,1,0:T(8,128)S(1)}, u32[]{:S(2)}, u32[]{:S(2)}) async-start(f32[32,16,128]{2,1,0:T(8,128)} %get-tuple-element.33), calls=%async_computation.1 | async-start | bytes 524288 | tf_op jit(solution)/shard_map/all_to_all | solution.py:805
  55.4 2.2 %shard_map.144 = f32[4,64,256]{2,1,0:T(8,128)} custom-call(f32[5,4,64,256]{3,2,1,0:T(8,128)} %get-tuple-element.29.refs_0_, f32[8,128]{1,0:T(8,128)S(1)} %get-tuple-element.32.refs_1_), custom_call_target="tpu_custom_call" | custom-call | flops 1000000000 | tf_op jit(solution)/shard_map/pallas_call | solution.py:124
  57.6 8.4 %all-to-all-done.1.refs_0_ = f32[32,16,128]{2,1,0:T(8,128)S(1)} async-done(((f32[32,16,128]{2,1,0:T(8,128)}), f32[32,16,128]{2,1,0:T(8,128)S(1)}, u32[]{:S(2)}, u32[]{:S(2)}) %all-to-all-start.1) | async-done | bytes 262176 | tf_op jit(solution)/shard_map/all_to_all | solution.py:805
  65.9 1.4 %shard_map.145 = (f32[3,8,1024]{2,1,0:T(8,128)}, f32[3,1024]{1,0:T(4,128)}) custom-call(f32[32,16,128]{2,1,0:T(8,128)S(1)} %all-to-all-done.1.refs_0_, f32[8,3,8,1024]{3,2,1,0:T(8,128)S(1)} %copy-done.8, f32[3,8,1024]{2,1,0:T(8,128)S(1)} %copy-done.5, f32[3,8,1024]{2,1,0:T(8,128)S(1)} %copy-done.6, f32[4,3,8,1024]{3,2,1,0:T(8,128)S(1)} %copy-done.1, ...), custom_call_target="tpu_custom_call" | custom-call | flops 1000000000 | tf_op jit(solution)/shard_map/pallas_call | solution.py:124
  (34 shorter events, 0.1 us)
Async XLA Ops:
  0.6 7.9 %copy-start.5 = (f32[3,8,1024]{2,1,0:T(8,128)S(1)}, f32[3,8,1024]{2,1,0:T(8,128)}, u32[]{:S(2)}) copy-start(f32[3,8,1024]{2,1,0:T(8,128)} %refs_2_.1) | copy-start | bytes 294916
  0.6 3.3 %copy-start.2 = (f32[4,64,256]{2,1,0:T(8,128)S(1)}, f32[4,64,256]{2,1,0:T(8,128)}, u32[]{:S(2)}) copy-start(f32[4,64,256]{2,1,0:T(8,128)} %refs_4_.3) | copy-start | bytes 786436
  0.7 7.9 %copy-start.3 = (f32[3,8,1024]{2,1,0:T(8,128)S(1)}, f32[3,8,1024]{2,1,0:T(8,128)}, u32[]{:S(2)}) copy-start(f32[3,8,1024]{2,1,0:T(8,128)} %refs_7_.2) | copy-start | bytes 294916
  0.7 7.9 %copy-start.7 = (f32[8,1024]{1,0:T(8,128)S(1)}, f32[8,1024]{1,0:T(8,128)}, u32[]{:S(2)}) copy-start(f32[8,1024]{1,0:T(8,128)} %refs_8_.2) | copy-start | bytes 98308
  2.8 5.8 %collective-permute-start = (f32[288,128]{1,0:T(8,128)S(1)}, f32[288,128]{1,0:T(8,128)S(1)}, u32[]{:S(2)}, u32[]{:S(2)}) collective-permute-start(f32[288,128]{1,0:T(8,128)S(1)} %get-tuple-element.24), channel_id=1, source_target_pairs={{0,1},{1,0},{2,3},{3,2},{4,5},{5,4},{6,7},{7,6},{8,9},{9,8},{10,11... | collective-permute-start | bytes 442376 | tf_op jit(solution)/shard_map/ppermute | solution.py:727
  3.3 5.3 %collective-permute-start.1 = (f32[288,128]{1,0:T(8,128)S(1)}, f32[288,128]{1,0:T(8,128)S(1)}, u32[]{:S(2)}, u32[]{:S(2)}) collective-permute-start(f32[288,128]{1,0:T(8,128)S(1)} %get-tuple-element.25), channel_id=1, source_target_pairs={{1,2},{3,4},{5,6},{7,8},{9,10},{11,12},{13,14},{15,16},{17,18},{19... | collective-permute-start | bytes 442376 | tf_op jit(solution)/shard_map/ppermute | solution.py:731
  3.9 21.6 %collective-permute-start.5 = (f32[4,64,256]{2,1,0:T(8,128)S(1)}, f32[4,64,256]{2,1,0:T(8,128)S(1)}, u32[]{:S(2)}, u32[]{:S(2)}) collective-permute-start(f32[4,64,256]{2,1,0:T(8,128)S(1)} %copy-done.2), channel_id=1, source_target_pairs={{0,1},{1,0},{2,3},{3,2},{4,5},{5,4},{6,7},{7,6},{8,9},{9,8},{10,11... | collective-permute-start | bytes 786440 | tf_op jit(solution)/shard_map/ppermute | solution.py:727
  7.9 17.7 %collective-permute-start.6 = (f32[4,64,256]{2,1,0:T(8,128)S(1)}, f32[4,64,256]{2,1,0:T(8,128)S(1)}, u32[]{:S(2)}, u32[]{:S(2)}) collective-permute-start(f32[4,64,256]{2,1,0:T(8,128)S(1)} %copy-done.2), channel_id=1, source_target_pairs={{1,2},{3,4},{5,6},{7,8},{9,10},{11,12},{13,14},{15,16},{17,18},{19... | collective-permute-start | bytes 786440 | tf_op jit(solution)/shard_map/ppermute | solution.py:731
  8.6 4.7 %copy-start.9 = (s32[1024,1]{0,1:T(1,128)S(1)}, s32[1024,1]{0,1:T(1,128)}, u32[]{:S(2)}) copy-start(s32[1024,1]{0,1:T(1,128)} %param.14) | copy-start | bytes 12292
  8.6 5.4 %copy-start.10 = (s32[1024]{0:T(1024)S(1)}, s32[1024]{0:T(1024)}, u32[]{:S(2)}) copy-start(s32[1024]{0:T(1024)} %param.15) | copy-start | bytes 12292
  8.6 5.4 %copy-start.11 = (s32[1024]{0:T(1024)S(1)}, s32[1024]{0:T(1024)}, u32[]{:S(2)}) copy-start(s32[1024]{0:T(1024)} %param.16) | copy-start | bytes 12292
  9.2 16.4 %collective-permute-start.2 = (f32[512,128]{1,0:T(8,128)S(1)}, f32[512,128]{1,0:T(8,128)S(1)}, u32[]{:S(2)}, u32[]{:S(2)}) collective-permute-start(f32[512,128]{1,0:T(8,128)S(1)} %get-tuple-element.26.refs_0_), channel_id=1, source_target_pairs={{0,1},{1,0},{2,3},{3,2},{4,5},{5,4},{6,7},{7,6},{8,9},{9,8},{10,11... | collective-permute-start | bytes 786440 | tf_op jit(solution)/shard_map/ppermute | solution.py:727
  12.1 13.5 %collective-permute-start.3 = (f32[512,128]{1,0:T(8,128)S(1)}, f32[512,128]{1,0:T(8,128)S(1)}, u32[]{:S(2)}, u32[]{:S(2)}) collective-permute-start(f32[512,128]{1,0:T(8,128)S(1)} %get-tuple-element.26.refs_0_), channel_id=1, source_target_pairs={{1,2},{3,4},{5,6},{7,8},{9,10},{11,12},{13,14},{15,16},{17,18},{19... | collective-permute-start | bytes 786440 | tf_op jit(solution)/shard_map/ppermute | solution.py:731
  14.0 11.6 %collective-permute-start.4 = (f32[128,128]{1,0:T(8,128)S(1)}, f32[128,128]{1,0:T(8,128)S(1)}, u32[]{:S(2)}, u32[]{:S(2)}) collective-permute-start(f32[128,128]{1,0:T(8,128)S(1)} %get-tuple-element.27), channel_id=1, source_target_pairs={{2,0},{3,1},{4,2},{5,3},{6,4},{7,5},{8,6},{9,7},{10,8},{11,9},{12,... | collective-permute-start | bytes 196616 | tf_op jit(solution)/shard_map/ppermute | solution.py:769
  25.6 17.2 %copy-start = (f32[4,3,8,1024]{3,2,1,0:T(8,128)S(1)}, f32[4,3,8,1024]{3,2,1,0:T(8,128)}, u32[]{:S(2)}) copy-start(f32[4,3,8,1024]{3,2,1,0:T(8,128)} %refs_7_.3) | copy-start | bytes 1179652
  25.6 17.2 %copy-start.1 = (f32[4,3,8,1024]{3,2,1,0:T(8,128)S(1)}, f32[4,3,8,1024]{3,2,1,0:T(8,128)}, u32[]{:S(2)}) copy-start(f32[4,3,8,1024]{3,2,1,0:T(8,128)} %refs_4_.5) | copy-start | bytes 1179652
  25.6 17.2 %copy-start.4 = (f32[3,8,1024]{2,1,0:T(8,128)S(1)}, f32[3,8,1024]{2,1,0:T(8,128)}, u32[]{:S(2)}) copy-start(f32[3,8,1024]{2,1,0:T(8,128)} %refs_5_.1) | copy-start | bytes 294916
  25.6 17.2 %copy-start.6 = (f32[3,8,1024]{2,1,0:T(8,128)S(1)}, f32[3,8,1024]{2,1,0:T(8,128)}, u32[]{:S(2)}) copy-start(f32[3,8,1024]{2,1,0:T(8,128)} %refs_3_.1) | copy-start | bytes 294916
  29.1 13.7 %all-to-all-start = ((f32[32,8,128]{2,1,0:T(8,128)}), f32[32,8,128]{2,1,0:T(8,128)S(1)}, u32[]{:S(2)}, u32[]{:S(2)}) async-start(f32[32,8,128]{2,1,0:T(8,128)} %get-tuple-element.30), calls=%async_computation | async-start | bytes 262144 | tf_op jit(solution)/shard_map/all_to_all | solution.py:787
  34.6 1.4 %collective-permute-start.7 = (f32[256,128]{1,0:T(8,128)S(1)}, f32[256,128]{1,0:T(8,128)S(1)}, u32[]{:S(2)}, u32[]{:S(2)}) collective-permute-start(f32[256,128]{1,0:T(8,128)S(1)} %get-tuple-element.31.refs_1_), channel_id=1, source_target_pairs={{0,1},{1,0},{2,3},{3,2},{4,5},{5,4},{6,7},{7,6},{8,9},{9,8},{10,11... | collective-permute-start | bytes 393224 | tf_op jit(solution)/shard_map/ppermute | solution.py:727
  34.9 1.1 %collective-permute-start.8 = (f32[256,128]{1,0:T(8,128)S(1)}, f32[256,128]{1,0:T(8,128)S(1)}, u32[]{:S(2)}, u32[]{:S(2)}) collective-permute-start(f32[256,128]{1,0:T(8,128)S(1)} %get-tuple-element.31.refs_1_), channel_id=1, source_target_pairs={{1,2},{3,4},{5,6},{7,8},{9,10},{11,12},{13,14},{15,16},{17,18},{19... | collective-permute-start | bytes 393224 | tf_op jit(solution)/shard_map/ppermute | solution.py:731
  50.2 15.7 %all-to-all-start.1 = ((f32[32,16,128]{2,1,0:T(8,128)}), f32[32,16,128]{2,1,0:T(8,128)S(1)}, u32[]{:S(2)}, u32[]{:S(2)}) async-start(f32[32,16,128]{2,1,0:T(8,128)} %get-tuple-element.33), calls=%async_computation.1 | async-start | bytes 524288 | tf_op jit(solution)/shard_map/all_to_all | solution.py:805
  55.3 10.6 %copy-start.8 = (f32[8,3,8,1024]{3,2,1,0:T(8,128)S(1)}, f32[8,3,8,1024]{3,2,1,0:T(8,128)}, u32[]{:S(2)}) copy-start(f32[8,3,8,1024]{3,2,1,0:T(8,128)} %get-tuple-element.34.refs_1_) | copy-start | bytes 2359300

commit v4 on v3

--- a/solution.py
+++ b/solution.py
@@ -140,13 +140,25 @@
     return lax.broadcasted_iota(jnp.int32, values.shape, axis)
 
 
+def without_edge(values, axis, index):
+    width = (8, 128)[axis]
+    size = values.shape[axis]
+    edge = 0 if index == 0 else size - width
+    tile = lax.slice_in_dim(values, edge, edge + width, axis=axis)
+    tile = jnp.where(at(tile, axis) == index - edge, 0.0, tile)
+    if index == 0:
+        rest = lax.slice_in_dim(values, width, size, axis=axis)
+        return jnp.concatenate([tile, rest], axis)
+    return jnp.concatenate([lax.slice_in_dim(values, 0, edge, axis=axis), tile], axis)
+
+
 def ahead(values, axis):
     size = values.shape[axis]
-    return jnp.where(at(values, axis) == size - 1, 0.0, pltpu.roll(values, size - 1, axis))
+    return without_edge(pltpu.roll(values, size - 1, axis), axis, size - 1)
 
 
 def behind(values, axis):
-    return jnp.where(at(values, axis) == 0, 0.0, pltpu.roll(values, 1, axis))
+    return without_edge(pltpu.roll(values, 1, axis), axis, 0)
 
 
 def plane_sum(plane):
@@ -360,7 +372,7 @@
 def pressure_kernel(
     own, mate, other, beyond, shift, shift_mate, shift_other,
     wall, owner, slots, node, weight,
-    payload, basis, work, diagonal, off, sent, *, ranks,
+    payload, basis, work, sent, *, ranks,
 ):
     left, right = sides(mate, other)
     shift_left, shift_right = sides(shift_mate, shift_other)
@@ -370,11 +382,7 @@
         work[0, x + 4] = halves(own, x * 128)
         work[0, x + 8] = halves(right, x * 128)
     work[0, 12] = halves(beyond, 0)
-    for x in range(1, 12):
-        values = (shift_left, shift, shift_right)[x // 4][x % 4]
-        inside = values > 0.0
-        diagonal[x] = jnp.where(inside, values + 6.0, 0.0)
-        off[x] = jnp.where(inside, 1.0, 0.0)
+    inside = [jnp.where(side[3 * end][0:1, 0:1] > 0.0, 1.0, 0.0) for side, end in ((shift_left, 1), (shift_right, 0))]
     copies = [
         pltpu.make_async_copy(work.at[k, pl.ds(4, layers)], basis.at[k], sent.at[k])
         for k in range(PITERS)
@@ -385,8 +393,9 @@
             now = work[step - 1, x]
             beside = work[step - 1, x - 1] + work[step - 1, x + 1] + plane_sum(now)
             if x < 4 or x >= 8:
-                beside = off[x] * beside
-            value = (diagonal[x] - P_SHIFT[step - 1]) * now - beside
+                beside = inside[x // 8] * beside
+            diagonal = (shift_left, shift, shift_right)[x // 4][x % 4] + (6.0 - P_SHIFT[step - 1])
+            value = diagonal * now - beside
             if step > 1:
                 value = value - P_BACK[step - 2] * work[step - 2, x]
             work[step, x] = value
@@ -443,6 +452,36 @@
         copy.wait()
 
 
+def second_spot(i, j):
+    if i < SITERS:
+        return 6 + i % 4, 96 + 16 * (i // 4) + j
+    return 10 + (i - SITERS) // 4, 96 + 8 * ((i - SITERS) % 4) + j - SITERS
+
+
+ENERGY_AT = (11, 112)
+
+
+def place_second(tile, i, j, value):
+    row, lane = second_spot(i, j)
+    if i < SITERS <= j:
+        return place_pair(tile, row, (lane, None, None), value)
+    return place_pair(tile, row, (lane, *second_spot(j, i)), value)
+
+
+def second_gram(summed):
+    row, lane = at(summed, 0), at(summed, 1)
+    first = pltpu.roll(pltpu.roll(summed, 32, 1), 10, 0)
+    second = pltpu.roll(pltpu.roll(summed, 16, 1), 14, 0)
+    gram = jnp.where(row < 4, first, second)
+    gram = jnp.where((row < SITERS) & (lane < 16), gram, 0.0)
+    for k in range(5):
+        source, start = second_spot(SITERS + k, SITERS)
+        moved = pltpu.roll(summed, (SITERS - start) % 128, 1)[source : source + 1]
+        here = (row == SITERS + k) & (lane >= SITERS) & (lane < SITERS + 5)
+        gram = jnp.where(here, jnp.broadcast_to(moved, gram.shape), gram)
+    return gram
+
+
 def row_of(matrix, k):
     return jnp.sum(jnp.where(at(matrix, 0) == k, matrix, 0.0), 0, keepdims=True)
 
@@ -496,9 +535,8 @@
 def shell_kernel(
     received, own, mate, other,
     displacement, residual_prev, solved_prev, residual_history, solved_history,
-    payload, basis, factors, work, diagonal, off, table, sent, *, ranks,
+    payload, basis, factors, work, diagonal, table, sent, *, ranks,
 ):
-    received = received()
     lane8 = lax.broadcasted_iota(jnp.int32, (8, 128), 1)
     summed = received[0]
     for p in range(1, ranks):
@@ -527,6 +565,7 @@
     target = lax.broadcasted_iota(jnp.int32, (64, entries), 0)
     low = lax.broadcasted_iota(jnp.int32, (128, entries), 0)
     node = None
+    inside = []
     for j in range(3):
         values = gathered(j)
         numbers = values[2:3, :].astype(jnp.int32)
@@ -552,7 +591,7 @@
             force = scattered[c * 64 : c * 64 + 64] * share
             for k in range(8):
                 place = (c * 8 + k) * 8
-                work[0, c * 24 + j * 8 : c * 24 + j * 8 + 8, k * 128 : k * 128 + 128] = (
+                work[0, c, j * 8 : j * 8 + 8, k * 128 : k * 128 + 128] = (
                     force[k * 8 : k * 8 + 8] + ref[place : place + 8, :]
                 )
         stiff = jnp.concatenate(
@@ -560,29 +599,24 @@
         )
         if j == 1:
             stiffness = stiff
-        inside = stiff > 0.0
-        main = jnp.where(inside, stiff + 4.0, 0.0)
-        side = jnp.where(inside, 1.0, 0.0)
         for c in range(3):
-            diagonal[c * 24 + j * 8 : c * 24 + j * 8 + 8, :] = main
-            off[c * 24 + j * 8 : c * 24 + j * 8 + 8, :] = side
+            diagonal[c * 24 + j * 8 : c * 24 + j * 8 + 8, :] = stiff
+        inside.append(jnp.where(stiff[:, 0:1] > 0.0, 1.0, 0.0))
+    inside = jnp.concatenate(inside * 3, 0)
     copies = [
-        pltpu.make_async_copy(work.at[k, pl.ds(c * 24 + 8, 8)], basis.at[k, c], sent.at[k, c])
+        pltpu.make_async_copy(work.at[k, :, pl.ds(8, 8)], basis.at[k], sent.at[k])
         for k in range(SITERS)
-        for c in range(3)
     ]
     for step in range(1, SITERS):
-        now = work[step - 1]
-        value = (diagonal[...] - S_SHIFT[step - 1]) * now - off[...] * shell_beside(now)
+        now = work[step - 1].reshape(72, 1024)
+        value = (diagonal[...] + (4.0 - S_SHIFT[step - 1])) * now - inside * shell_beside(now)
         if step > 1:
-            value = value - S_BACK[step - 2] * work[step - 2]
-        work[step] = value
-        for copy in copies[step * 3 - 3 : step * 3]:
-            copy.start()
-    for copy in copies[-3:]:
-        copy.start()
+            value = value - S_BACK[step - 2] * work[step - 2].reshape(72, 1024)
+        work[step] = value.reshape(3, 24, 1024)
+        copies[step - 1].start()
+    copies[-1].start()
     def basis_tile(k, c, columns=slice(None)):
-        return work[k, c * 24 + 8 : c * 24 + 16, columns]
+        return work[k, c, 8:16, columns]
 
     def tile_of(ref):
         return lambda c, columns=slice(None): ref[c, :, columns]
@@ -600,15 +634,15 @@
                 tiles = {v: vectors[v](c, slice(k * 128, k * 128 + 128)) for v in used}
                 totals = [total + tiles[i] * tiles[j] for total, (i, j) in zip(totals, some)]
         for total, (i, j) in zip(totals, some):
-            tile = place_pair(tile, i, (96 + j, j, 96 + i), whole(total))
+            tile = place_second(tile, i, j, whole(total))
     top = SITERS - 1
     total = 0.0
     for c in range(3):
         now = basis_tile(top, c)
-        after = work[top, c * 24 + 9 : c * 24 + 17, :]
+        after = work[top, c, 9:17, :]
         image = (4.0 + stiffness) * now - ahead(now, 1) - behind(now, 1) - 2.0 * after
         total = total + now * image
-    tile = place_pair(tile, 13, (96 + 13, None, None), whole(fold(total)))
+    tile = place_pair(tile, ENERGY_AT[0], (ENERGY_AT[1], None, None), whole(fold(total)))
     fields = vectors[:SITERS] + [lambda c: displacement[c]]
     fields += [lambda c, k=k: solved_history[k, c] for k in range(solved_history.shape[0])]
     fields.append(lambda c: solved_prev[c])
@@ -625,15 +659,20 @@
     for r in range(8):
         answer = jnp.where(line == r, found[r * 48 : r * 48 + 48], answer)
     lane16 = lax.broadcasted_iota(jnp.int32, (16, 128), 1)
+    row16 = lax.broadcasted_iota(jnp.int32, (16, 128), 0)
+    extra = jnp.concatenate(
+        [answer[c * 16 + 12 : c * 16 + 14] for c in range(3)] + [jnp.zeros((10, entries), F32)], 0
+    )
     for p in range(ranks):
-        k = p // 4
-        block = tile
+        columns = slice(p // 4 * 128, p // 4 * 128 + 128)
+        block = jnp.where(row16 < 6, pltpu.roll(extra[:, columns], (32 * (3 - p % 4)) % 128, 1), tile)
         for c in range(3):
-            piece = answer[c * 16 : c * 16 + 16, k * 128 : k * 128 + 128]
+            piece = answer[c * 16 : c * 16 + 16, columns]
             block = jnp.where(
                 lane16 // 32 == c, pltpu.roll(piece, (32 * (c - p % 4)) % 128, 1), block
             )
-        payload[p] = block
+        for t in range(3):
+            payload[p, t] = block[t * 4 : t * 4 + 4]
     for copy in copies:
         copy.wait()
 
@@ -651,17 +690,24 @@
     received, basis, displacement, solved_prev, solved_history, owner, slots,
     new_displacement, wall, *, ranks,
 ):
-    received = received()
-    summed = received[0]
-    for p in range(1, ranks):
-        summed = summed + received[p]
-    gram = [column_of(summed, 96 + k) for k in range(14)]
-    system = galerkin(gram[:SITERS], 0, S_SHIFT, S_BACK, gram[13][13:14])
+    blocks = [
+        jnp.concatenate([received[p, t] for t in range(3)] + [jnp.zeros((4, 128), F32)], 0)
+        for p in range(ranks)
+    ]
+    summed = sum(blocks)
+    matrix = second_gram(summed)
+    gram = [column_of(matrix, k) for k in range(SITERS + 5)]
+    energy = summed[ENERGY_AT[0] : ENERGY_AT[0] + 1, ENERGY_AT[1] : ENERGY_AT[1] + 1]
+    system = galerkin(gram[:SITERS], 0, S_SHIFT, S_BACK, energy)
     steps = eliminate(system, gram[0], 0)
     down = lax.broadcasted_iota(jnp.int32, (16, 1), 0)
     steps = jnp.where(down < SITERS, steps, 0.0)
     base, count = SITERS, 1 + solved_history.shape[0]
-    with_moved = sum(steps[k : k + 1] * gram[k] for k in range(SITERS))
+    with_moved = jnp.sum(matrix * steps, 0, keepdims=True)
+    diagonal = at(matrix, 0) == at(matrix, 1)
+    with_moved = jnp.sum(
+        jnp.where(diagonal, jnp.broadcast_to(with_moved, matrix.shape), 0.0), 1, keepdims=True
+    )
     with_newest = with_moved - gram[base]
     newest_moved = jnp.sum(steps * with_newest, 0, keepdims=True)
     newest_newest = newest_moved - with_newest[base : base + 1]
@@ -688,11 +734,13 @@
             total = total + row_of(factors, base + 1 + k) * solved_history[k, c]
         total = total + row_of(factors, base + count) * solved_prev[c]
         new_displacement[c] = total
-    answers = jnp.concatenate(
-        [jnp.sum(received[p] * factors, 0, keepdims=True) for p in range(ranks)], 0
-    )
-    group = at(answers, 1) // 32
-    stacked = jnp.concatenate([jnp.where(group == c, answers, 0.0) for c in range(3)], 0)
+    row, group = at(summed, 0), at(summed, 1) // 32
+    spare = jnp.where(row % 2 == 0, factors[12:13], factors[13:14])
+    stacked = []
+    for c in range(3):
+        scales = jnp.where(group == c, factors, jnp.where((group == 3) & (row // 2 == c), spare, 0.0))
+        stacked += [jnp.sum(block * scales, 0, keepdims=True) for block in blocks]
+    stacked = jnp.concatenate(stacked, 0)
     slot_row = lax.broadcasted_iota(jnp.int32, (128, 256), 0) & 31
     rank = lax.broadcasted_iota(jnp.int32, (ranks, 256), 0)
     for x in range(owner.shape[0]):
@@ -779,27 +827,23 @@
         direct=(1,),
         scratch=(
             pltpu.VMEM((PITERS, 13, 64, 256), F32),
-            pltpu.VMEM((12, 64, 256), F32),
-            pltpu.VMEM((12, 64, 256), F32),
             pltpu.SemaphoreType.DMA((PITERS,)),
         ),
     )
     received = lax.all_to_all(payload, "slab", split_axis=0, concat_axis=0, tiled=True)
     payload, shell_basis, factors = call(
         lambda *refs: shell_kernel(*refs, ranks=ranks),
-        (shape(ranks, 16, 128), pltpu.HBM((SITERS, *displacement.shape), F32), shape(8, 128)),
+        (shape(ranks, 3, 4, 128), pltpu.HBM((SITERS, *displacement.shape), F32), shape(8, 128)),
         (
             received, shell, shell_mate, shell_other,
             displacement, residual_prev, solved_prev, residual_history, solved_history,
         ),
-        late=(0,),
         direct=(1,),
         scratch=(
-            pltpu.VMEM((SITERS, 72, 1024), F32),
-            pltpu.VMEM((72, 1024), F32),
+            pltpu.VMEM((SITERS, 3, 24, 1024), F32),
             pltpu.VMEM((72, 1024), F32),
             pltpu.VMEM((8, 8 * 48, 128), F32),
-            pltpu.SemaphoreType.DMA((SITERS, 3)),
+            pltpu.SemaphoreType.DMA((SITERS,)),
         ),
     )
     answers = lax.all_to_all(payload, "slab", split_axis=0, concat_axis=0, tiled=True)
@@ -814,7 +858,6 @@
         lambda *refs: update_kernel(*refs, ranks=ranks),
         (shape(*displacement.shape), shape(3, owner_rank.shape[0])),
         (answers, shell_basis, displacement, solved_prev, solved_history, owner, slots),
-        late=(0,),
     )
     return (pressure, new_displacement, wall_displacement)
 

time: 67.8 us -> 66.2 us (0.976)
  waiting for transfers between devices: 25.6 us -> 23.9 us
    all_to_all x2, waiting for transfers between devices: 15.2 us -> 13.5 us  [on_device(): lax.all_to_all(payload, 'slab', split_axis=0, concat_axis=0, tiled=True)]
  transfers between devices with their start and end apart: 11 -> 11, of which waited for: 4 -> 4; matrix products, arithmetic and copies ran while one was open for 2% -> 2% of each run, Pallas kernels for 4% -> 5%
where the time goes in v4:
time: 66.2 us; the launch traced here: 65.7 us
  waiting for transfers between devices  23.9 us (36%)
  starting transfers between devices  22.2 us (34%)
  Pallas kernels  17.4 us (26%)
  between operations  0.94 us (1%)
    pallas_call x7, Pallas kernels, call(): pl.pallas_call(body, out_shape=outs, in_specs=[any_space if i in outside...  17.4 us
    all_to_all x2, waiting for transfers between devices, on_device(): lax.all_to_all(payload, 'slab', split_axis=0, concat_axis=0, tiled=True)  13.5 us
    all_to_all x2, starting transfers between devices, on_device(): lax.all_to_all(payload, 'slab', split_axis=0, concat_axis=0, tiled=True)  10.6 us
    ppermute x1, waiting for transfers between devices, on_device(): beyond = lax.ppermute(first, 'slab', [(i, i - 2) for i in range(2, ranks)])  10 us
    ppermute x4, starting transfers between devices, with_mate(): return lax.ppermute(values, 'slab', [(i, i ^ 1) for i in range(ranks)])  7.67 us
    ppermute x4, starting transfers between devices, with_other(): return lax.ppermute(values, 'slab', pairs + [(j, i) for i, j in pairs])  2.65 us
  transfers between devices with their start and end apart: 11, of which 4 were waited for; matrix products, arithmetic and copies ran while one was open for 2% of the time, Pallas kernels for 5%

profile of v4, /device:TPU:0, one launch (start us, length us, event | category | flops | bytes accessed | tf_op | source)
XLA Modules:
  0.0 65.7 jit_solution(2014753198253456774)
XLA Ops:
  0.7 2.1 %shard_map.139 = (f32[288,128]{1,0:T(8,128)S(1)}, f32[288,128]{1,0:T(8,128)S(1)}, f32[64,256]{1,0:T(8,128)S(1)}, f32[64,256]{1,0:T(8,128)S(1)}, f32[4,64,256]{2,1,0:T(8,128)S(1)}, /*index=5*/f32[8,256]{1,0:T(8,128)S(1)}) custom-call(f32[3,4,64,256]{3,2,1,0:T(8,128)} %refs_0_.1, f32[3,8,1024]{2,1,0:T(8,128)} %refs_2_.1), custom_call_target="tpu_custom_call" | custom-call | flops 1000000000 | tf_op jit(solution)/shard_map/pallas_call | solution.py:124
  2.8 0.5 collective-permute-start
  3.3 0.7 %collective-permute-start.1 = (f32[288,128]{1,0:T(8,128)S(1)}, f32[288,128]{1,0:T(8,128)S(1)}, u32[]{:S(2)}, u32[]{:S(2)}) collective-permute-start(f32[288,128]{1,0:T(8,128)S(1)} %get-tuple-element.25), channel_id=1, source_target_pairs={{1,2},{3,4},{5,6},{7,8},{9,10},{11,12},{13,14},{15,16},{17,18},{19... | collective-permute-start | bytes 442376 | tf_op jit(solution)/shard_map/ppermute | solution.py:779
  3.9 3.9 %collective-permute-start.5 = (f32[4,64,256]{2,1,0:T(8,128)S(1)}, f32[4,64,256]{2,1,0:T(8,128)S(1)}, u32[]{:S(2)}, u32[]{:S(2)}) collective-permute-start(f32[4,64,256]{2,1,0:T(8,128)S(1)} %copy-done.2), channel_id=1, source_target_pairs={{0,1},{1,0},{2,3},{3,2},{4,5},{5,4},{6,7},{7,6},{8,9},{9,8},{10,11... | collective-permute-start | bytes 786440 | tf_op jit(solution)/shard_map/ppermute | solution.py:775
  7.9 0.7 %collective-permute-start.6 = (f32[4,64,256]{2,1,0:T(8,128)S(1)}, f32[4,64,256]{2,1,0:T(8,128)S(1)}, u32[]{:S(2)}, u32[]{:S(2)}) collective-permute-start(f32[4,64,256]{2,1,0:T(8,128)S(1)} %copy-done.2), channel_id=1, source_target_pairs={{1,2},{3,4},{5,6},{7,8},{9,10},{11,12},{13,14},{15,16},{17,18},{19... | collective-permute-start | bytes 786440 | tf_op jit(solution)/shard_map/ppermute | solution.py:779
  8.6 0.6 shard_map.140
  9.2 2.9 %collective-permute-start.2 = (f32[512,128]{1,0:T(8,128)S(1)}, f32[512,128]{1,0:T(8,128)S(1)}, u32[]{:S(2)}, u32[]{:S(2)}) collective-permute-start(f32[512,128]{1,0:T(8,128)S(1)} %get-tuple-element.26.refs_0_), channel_id=1, source_target_pairs={{0,1},{1,0},{2,3},{3,2},{4,5},{5,4},{6,7},{7,6},{8,9},{9,8},{10,11... | collective-permute-start | bytes 786440 | tf_op jit(solution)/shard_map/ppermute | solution.py:775
  12.1 0.7 %collective-permute-start.3 = (f32[512,128]{1,0:T(8,128)S(1)}, f32[512,128]{1,0:T(8,128)S(1)}, u32[]{:S(2)}, u32[]{:S(2)}) collective-permute-start(f32[512,128]{1,0:T(8,128)S(1)} %get-tuple-element.26.refs_0_), channel_id=1, source_target_pairs={{1,2},{3,4},{5,6},{7,8},{9,10},{11,12},{13,14},{15,16},{17,18},{19... | collective-permute-start | bytes 786440 | tf_op jit(solution)/shard_map/ppermute | solution.py:779
  12.8 0.5 broadcast.3
  13.3 0.7 %reduce.3 = s32[1024]{0:T(1024)S(1)} reduce(s32[1024,1]{0,1:T(1,128)S(1)} %copy-done.9, s32[]{:T(128)} %broadcast.3), dimensions={1}, to_apply=%param.14.reduce_sub_computation.3 | reduce | bytes 8196 | tf_op args[2]
  14.0 1.3 %collective-permute-start.4 = (f32[128,128]{1,0:T(8,128)S(1)}, f32[128,128]{1,0:T(8,128)S(1)}, u32[]{:S(2)}, u32[]{:S(2)}) collective-permute-start(f32[128,128]{1,0:T(8,128)S(1)} %get-tuple-element.27), channel_id=1, source_target_pairs={{2,0},{3,1},{4,2},{5,3},{6,4},{7,5},{8,6},{9,7},{10,8},{11,9},{12,... | collective-permute-start | bytes 196616 | tf_op jit(solution)/shard_map/ppermute | solution.py:817
  15.3 0.2 shard_map.141.refs_9_.refs_6_
  15.6 10.0 %collective-permute-done.4.refs_3_ = f32[128,128]{1,0:T(8,128)S(1)} collective-permute-done((f32[128,128]{1,0:T(8,128)S(1)}, f32[128,128]{1,0:T(8,128)S(1)}, u32[]{:S(2)}, u32[]{:S(2)}) %collective-permute-start.4) | collective-permute-done | bytes 65568 | tf_op jit(solution)/shard_map/ppermute | solution.py:817
  25.7 3.5 %shard_map.142 = (f32[32,8,128]{2,1,0:T(8,128)}, f32[5,4,64,256]{3,2,1,0:T(8,128)}) custom-call(f32[512,128]{1,0:T(8,128)S(1)} %get-tuple-element.26.refs_0_, f32[512,128]{1,0:T(8,128)S(1)} %collective-permute-done.2.refs_1_, f32[512,128]{1,0:T(8,128)S(1)} %collective-permute-done.3.refs_2_, f32[128,128]{1,0:T(8,128)S(1)} %collective-permute-done.4.refs_3_, ...), custom_call_target="tpu_custom_call" | custom-call | flops 1000000000 | tf_op jit(solution)/shard_map/pallas_call | solution.py:124
  29.2 5.5 %all-to-all-start = ((f32[32,8,128]{2,1,0:T(8,128)}), f32[32,8,128]{2,1,0:T(8,128)S(1)}, u32[]{:S(2)}, u32[]{:S(2)}) async-start(f32[32,8,128]{2,1,0:T(8,128)} %get-tuple-element.30), calls=%async_computation | async-start | bytes 262144 | tf_op jit(solution)/shard_map/all_to_all | solution.py:833
  34.7 0.3 collective-permute-start.7
  35.0 0.7 collective-permute-start.8
  35.6 0.4 collective-permute-done.7.refs_2_
  36.1 6.8 %all-to-all-done.refs_0_ = f32[32,8,128]{2,1,0:T(8,128)S(1)} async-done(((f32[32,8,128]{2,1,0:T(8,128)}), f32[32,8,128]{2,1,0:T(8,128)S(1)}, u32[]{:S(2)}, u32[]{:S(2)}) %all-to-all-start) | async-done | bytes 131104 | tf_op jit(solution)/shard_map/all_to_all | solution.py:833
  42.9 7.0 %shard_map.143 = (f32[32,3,4,128]{3,2,1,0:T(4,128)}, f32[8,3,8,1024]{3,2,1,0:T(8,128)}, f32[8,128]{1,0:T(8,128)S(1)}) custom-call(f32[32,8,128]{2,1,0:T(8,128)S(1)} %all-to-all-done.refs_0_, f32[256,128]{1,0:T(8,128)S(1)} %get-tuple-element.31.refs_1_, f32[256,128]{1,0:T(8,128)S(1)} %collective-permute-done.7.refs_2_, ...), custom_call_target="tpu_custom_call" | custom-call | flops 1000000000 | tf_op jit(solution)/shard_map/pallas_call | solution.py:124
  49.9 5.1 %all-to-all-start.1 = ((f32[32,3,4,128]{3,2,1,0:T(4,128)}), f32[32,3,4,128]{3,2,1,0:T(4,128)S(1)}, u32[]{:S(2)}, u32[]{:S(2)}) async-start(f32[32,3,4,128]{3,2,1,0:T(4,128)} %get-tuple-element.33), calls=%async_computation.1 | async-start | bytes 393216 | tf_op jit(solution)/shard_map/all_to_all | solution.py:849
  55.0 2.2 %shard_map.144 = f32[4,64,256]{2,1,0:T(8,128)} custom-call(f32[5,4,64,256]{3,2,1,0:T(8,128)} %get-tuple-element.29.refs_0_, f32[8,128]{1,0:T(8,128)S(1)} %get-tuple-element.32.refs_1_), custom_call_target="tpu_custom_call" | custom-call | flops 1000000000 | tf_op jit(solution)/shard_map/pallas_call | solution.py:124
  57.3 6.7 %all-to-all-done.1.refs_0_ = f32[32,3,4,128]{3,2,1,0:T(4,128)S(1)} async-done(((f32[32,3,4,128]{3,2,1,0:T(4,128)}), f32[32,3,4,128]{3,2,1,0:T(4,128)S(1)}, u32[]{:S(2)}, u32[]{:S(2)}) %all-to-all-start.1) | async-done | bytes 196640 | tf_op jit(solution)/shard_map/all_to_all | solution.py:849
  63.9 1.8 %shard_map.145 = (f32[3,8,1024]{2,1,0:T(8,128)}, f32[3,1024]{1,0:T(4,128)}) custom-call(f32[32,3,4,128]{3,2,1,0:T(4,128)S(1)} %all-to-all-done.1.refs_0_, f32[8,3,8,1024]{3,2,1,0:T(8,128)S(1)} %copy-done.8, f32[3,8,1024]{2,1,0:T(8,128)S(1)} %copy-done.5, f32[3,8,1024]{2,1,0:T(8,128)S(1)} %copy-done.6, f32[4,3,8,1024]{3,2,1,0:T(8,128)S(1)} %copy-done.1, ...), custom_call_target="tpu_custom_call" | custom-call | flops 1000000000 | tf_op jit(solution)/shard_map/pallas_call | solution.py:124
  (34 shorter events, 0.1 us)
Async XLA Ops:
  0.6 7.9 %copy-start.5 = (f32[3,8,1024]{2,1,0:T(8,128)S(1)}, f32[3,8,1024]{2,1,0:T(8,128)}, u32[]{:S(2)}) copy-start(f32[3,8,1024]{2,1,0:T(8,128)} %refs_2_.1) | copy-start | bytes 294916
  0.6 3.3 %copy-start.2 = (f32[4,64,256]{2,1,0:T(8,128)S(1)}, f32[4,64,256]{2,1,0:T(8,128)}, u32[]{:S(2)}) copy-start(f32[4,64,256]{2,1,0:T(8,128)} %refs_4_.3) | copy-start | bytes 786436
  0.7 7.9 %copy-start.3 = (f32[3,8,1024]{2,1,0:T(8,128)S(1)}, f32[3,8,1024]{2,1,0:T(8,128)}, u32[]{:S(2)}) copy-start(f32[3,8,1024]{2,1,0:T(8,128)} %refs_7_.2) | copy-start | bytes 294916
  0.7 7.9 %copy-start.7 = (f32[8,1024]{1,0:T(8,128)S(1)}, f32[8,1024]{1,0:T(8,128)}, u32[]{:S(2)}) copy-start(f32[8,1024]{1,0:T(8,128)} %refs_8_.2) | copy-start | bytes 98308
  2.8 5.8 %collective-permute-start = (f32[288,128]{1,0:T(8,128)S(1)}, f32[288,128]{1,0:T(8,128)S(1)}, u32[]{:S(2)}, u32[]{:S(2)}) collective-permute-start(f32[288,128]{1,0:T(8,128)S(1)} %get-tuple-element.24), channel_id=1, source_target_pairs={{0,1},{1,0},{2,3},{3,2},{4,5},{5,4},{6,7},{7,6},{8,9},{9,8},{10,11... | collective-permute-start | bytes 442376 | tf_op jit(solution)/shard_map/ppermute | solution.py:775
  3.3 5.3 %collective-permute-start.1 = (f32[288,128]{1,0:T(8,128)S(1)}, f32[288,128]{1,0:T(8,128)S(1)}, u32[]{:S(2)}, u32[]{:S(2)}) collective-permute-start(f32[288,128]{1,0:T(8,128)S(1)} %get-tuple-element.25), channel_id=1, source_target_pairs={{1,2},{3,4},{5,6},{7,8},{9,10},{11,12},{13,14},{15,16},{17,18},{19... | collective-permute-start | bytes 442376 | tf_op jit(solution)/shard_map/ppermute | solution.py:779
  3.9 21.6 %collective-permute-start.5 = (f32[4,64,256]{2,1,0:T(8,128)S(1)}, f32[4,64,256]{2,1,0:T(8,128)S(1)}, u32[]{:S(2)}, u32[]{:S(2)}) collective-permute-start(f32[4,64,256]{2,1,0:T(8,128)S(1)} %copy-done.2), channel_id=1, source_target_pairs={{0,1},{1,0},{2,3},{3,2},{4,5},{5,4},{6,7},{7,6},{8,9},{9,8},{10,11... | collective-permute-start | bytes 786440 | tf_op jit(solution)/shard_map/ppermute | solution.py:775
  7.9 17.7 %collective-permute-start.6 = (f32[4,64,256]{2,1,0:T(8,128)S(1)}, f32[4,64,256]{2,1,0:T(8,128)S(1)}, u32[]{:S(2)}, u32[]{:S(2)}) collective-permute-start(f32[4,64,256]{2,1,0:T(8,128)S(1)} %copy-done.2), channel_id=1, source_target_pairs={{1,2},{3,4},{5,6},{7,8},{9,10},{11,12},{13,14},{15,16},{17,18},{19... | collective-permute-start | bytes 786440 | tf_op jit(solution)/shard_map/ppermute | solution.py:779
  8.6 4.7 %copy-start.9 = (s32[1024,1]{0,1:T(1,128)S(1)}, s32[1024,1]{0,1:T(1,128)}, u32[]{:S(2)}) copy-start(s32[1024,1]{0,1:T(1,128)} %param.14) | copy-start | bytes 12292
  8.6 5.4 %copy-start.10 = (s32[1024]{0:T(1024)S(1)}, s32[1024]{0:T(1024)}, u32[]{:S(2)}) copy-start(s32[1024]{0:T(1024)} %param.15) | copy-start | bytes 12292
  8.6 5.4 %copy-start.11 = (s32[1024]{0:T(1024)S(1)}, s32[1024]{0:T(1024)}, u32[]{:S(2)}) copy-start(s32[1024]{0:T(1024)} %param.16) | copy-start | bytes 12292
  9.2 16.4 %collective-permute-start.2 = (f32[512,128]{1,0:T(8,128)S(1)}, f32[512,128]{1,0:T(8,128)S(1)}, u32[]{:S(2)}, u32[]{:S(2)}) collective-permute-start(f32[512,128]{1,0:T(8,128)S(1)} %get-tuple-element.26.refs_0_), channel_id=1, source_target_pairs={{0,1},{1,0},{2,3},{3,2},{4,5},{5,4},{6,7},{7,6},{8,9},{9,8},{10,11... | collective-permute-start | bytes 786440 | tf_op jit(solution)/shard_map/ppermute | solution.py:775
  12.1 13.5 %collective-permute-start.3 = (f32[512,128]{1,0:T(8,128)S(1)}, f32[512,128]{1,0:T(8,128)S(1)}, u32[]{:S(2)}, u32[]{:S(2)}) collective-permute-start(f32[512,128]{1,0:T(8,128)S(1)} %get-tuple-element.26.refs_0_), channel_id=1, source_target_pairs={{1,2},{3,4},{5,6},{7,8},{9,10},{11,12},{13,14},{15,16},{17,18},{19... | collective-permute-start | bytes 786440 | tf_op jit(solution)/shard_map/ppermute | solution.py:779
  14.0 11.6 %collective-permute-start.4 = (f32[128,128]{1,0:T(8,128)S(1)}, f32[128,128]{1,0:T(8,128)S(1)}, u32[]{:S(2)}, u32[]{:S(2)}) collective-permute-start(f32[128,128]{1,0:T(8,128)S(1)} %get-tuple-element.27), channel_id=1, source_target_pairs={{2,0},{3,1},{4,2},{5,3},{6,4},{7,5},{8,6},{9,7},{10,8},{11,9},{12,... | collective-permute-start | bytes 196616 | tf_op jit(solution)/shard_map/ppermute | solution.py:817
  25.6 17.3 %copy-start = (f32[4,3,8,1024]{3,2,1,0:T(8,128)S(1)}, f32[4,3,8,1024]{3,2,1,0:T(8,128)}, u32[]{:S(2)}) copy-start(f32[4,3,8,1024]{3,2,1,0:T(8,128)} %refs_7_.3) | copy-start | bytes 1179652
  25.6 17.3 %copy-start.1 = (f32[4,3,8,1024]{3,2,1,0:T(8,128)S(1)}, f32[4,3,8,1024]{3,2,1,0:T(8,128)}, u32[]{:S(2)}) copy-start(f32[4,3,8,1024]{3,2,1,0:T(8,128)} %refs_4_.5) | copy-start | bytes 1179652
  25.6 17.3 %copy-start.4 = (f32[3,8,1024]{2,1,0:T(8,128)S(1)}, f32[3,8,1024]{2,1,0:T(8,128)}, u32[]{:S(2)}) copy-start(f32[3,8,1024]{2,1,0:T(8,128)} %refs_5_.1) | copy-start | bytes 294916
  25.6 17.2 %copy-start.6 = (f32[3,8,1024]{2,1,0:T(8,128)S(1)}, f32[3,8,1024]{2,1,0:T(8,128)}, u32[]{:S(2)}) copy-start(f32[3,8,1024]{2,1,0:T(8,128)} %refs_3_.1) | copy-start | bytes 294916
  29.2 13.7 %all-to-all-start = ((f32[32,8,128]{2,1,0:T(8,128)}), f32[32,8,128]{2,1,0:T(8,128)S(1)}, u32[]{:S(2)}, u32[]{:S(2)}) async-start(f32[32,8,128]{2,1,0:T(8,128)} %get-tuple-element.30), calls=%async_computation | async-start | bytes 262144 | tf_op jit(solution)/shard_map/all_to_all | solution.py:833
  34.7 1.4 %collective-permute-start.7 = (f32[256,128]{1,0:T(8,128)S(1)}, f32[256,128]{1,0:T(8,128)S(1)}, u32[]{:S(2)}, u32[]{:S(2)}) collective-permute-start(f32[256,128]{1,0:T(8,128)S(1)} %get-tuple-element.31.refs_1_), channel_id=1, source_target_pairs={{0,1},{1,0},{2,3},{3,2},{4,5},{5,4},{6,7},{7,6},{8,9},{9,8},{10,11... | collective-permute-start | bytes 393224 | tf_op jit(solution)/shard_map/ppermute | solution.py:775
  35.0 1.1 %collective-permute-start.8 = (f32[256,128]{1,0:T(8,128)S(1)}, f32[256,128]{1,0:T(8,128)S(1)}, u32[]{:S(2)}, u32[]{:S(2)}) collective-permute-start(f32[256,128]{1,0:T(8,128)S(1)} %get-tuple-element.31.refs_1_), channel_id=1, source_target_pairs={{1,2},{3,4},{5,6},{7,8},{9,10},{11,12},{13,14},{15,16},{17,18},{19... | collective-permute-start | bytes 393224 | tf_op jit(solution)/shard_map/ppermute | solution.py:779
  49.9 14.0 %all-to-all-start.1 = ((f32[32,3,4,128]{3,2,1,0:T(4,128)}), f32[32,3,4,128]{3,2,1,0:T(4,128)S(1)}, u32[]{:S(2)}, u32[]{:S(2)}) async-start(f32[32,3,4,128]{3,2,1,0:T(4,128)} %get-tuple-element.33), calls=%async_computation.1 | async-start | bytes 393216 | tf_op jit(solution)/shard_map/all_to_all | solution.py:849
  55.0 8.9 %copy-start.8 = (f32[8,3,8,1024]{3,2,1,0:T(8,128)S(1)}, f32[8,3,8,1024]{3,2,1,0:T(8,128)}, u32[]{:S(2)}) copy-start(f32[8,3,8,1024]{3,2,1,0:T(8,128)} %get-tuple-element.34.refs_1_) | copy-start | bytes 2359300

commit v5 on v4

--- a/solution.py
+++ b/solution.py
@@ -401,11 +401,15 @@
             work[step, x] = value
         copies[step].start()
     tile = jnp.zeros((8, 128), F32)
-    for i in range(PITERS):
-        for j in range(i, PITERS):
-            total = sum(work[i, x] * work[j, x] for x in range(4, 8))
-            value = whole(fold(total))
-            tile = place_pair(tile, 3 + i, (96 + j, 3 + j, 96 + i), value)
+    pairs = [(i, j) for i in range(PITERS) for j in range(i, PITERS)]
+    totals = [0.0] * len(pairs)
+    for x in range(4, 8):
+        for y in range(0, 64, 8):
+            for z in (0, 128):
+                tiles = [work[k, x, y : y + 8, z : z + 128] for k in range(PITERS)]
+                totals = [total + tiles[i] * tiles[j] for total, (i, j) in zip(totals, pairs)]
+    for total, (i, j) in zip(totals, pairs):
+        tile = place_pair(tile, 3 + i, (96 + j, 3 + j, 96 + i), whole(total))
     top = PITERS - 1
     total = 0.0
     for x in range(4, 8):
@@ -532,10 +536,27 @@
     return images
 
 
-def shell_kernel(
-    received, own, mate, other,
-    displacement, residual_prev, solved_prev, residual_history, solved_history,
-    payload, basis, factors, work, diagonal, table, sent, *, ranks,
+def picked_nodes(node):
+    column = lax.broadcasted_iota(jnp.int32, (1024, node.shape[1]), 0)
+    return jnp.where(column == (node & 1023), 1.0, 0.0).astype(BF16)
+
+
+def nodes_values(fields, table, pick, line):
+    for c in range(3):
+        for f in range(8):
+            value = fields[f](c) if f < len(fields) else jnp.zeros((8, 1024), F32)
+            for k in range(8):
+                table[k, pl.ds(c * 8 + f, 8, stride=24), :] = value[:, k * 128 : k * 128 + 128]
+    found = split_dot(jnp.concatenate([table[k] for k in range(8)], 1), pick, 2)
+    values = found[0:24]
+    for r in range(1, 8):
+        values = jnp.where(line == r, found[r * 24 : r * 24 + 24], values)
+    return values
+
+
+def force_kernel(
+    received, displacement, solved_prev, solved_history,
+    forces, requests, fixed, factors, table, *, ranks,
 ):
     lane8 = lax.broadcasted_iota(jnp.int32, (8, 128), 1)
     summed = received[0]
@@ -559,13 +580,11 @@
             chunks.append(chunk)
         return jnp.concatenate(chunks, 1)
 
-    left, right = sides(mate, other)
     weights = gathered(3)
     entries = ranks * CAP
     target = lax.broadcasted_iota(jnp.int32, (64, entries), 0)
     low = lax.broadcasted_iota(jnp.int32, (128, entries), 0)
     node = None
-    inside = []
     for j in range(3):
         values = gathered(j)
         numbers = values[2:3, :].astype(jnp.int32)
@@ -586,17 +605,34 @@
         scattered = added(dot(left_rows.astype(BF16), spot, True), 2)
         share = dot(jnp.where(match, weights[j : j + 1, :], 0.0).astype(BF16), spot, True)
         share = 1.0 / jnp.maximum(share, 1.0)
-        ref = (left, own, right)[j]
         for c in range(3):
             force = scattered[c * 64 : c * 64 + 64] * share
             for k in range(8):
+                forces[c, j * 8 : j * 8 + 8, k * 128 : k * 128 + 128] = force[k * 8 : k * 8 + 8]
+    requests[...] = jnp.broadcast_to(node, (8, entries))
+    pick = picked_nodes(node)
+    fields = [lambda c: displacement[c]]
+    fields += [lambda c, k=k: solved_history[k, c] for k in range(solved_history.shape[0])]
+    fields.append(lambda c: solved_prev[c])
+    fixed[...] = nodes_values(fields, table, pick, node >> 10)
+
+
+def shell_kernel(
+    forces, requests, fixed, own, mate, other, residual_prev, residual_history,
+    payload, basis, work, diagonal, table, sent, *, ranks,
+):
+    left, right = sides(mate, other)
+    inside = []
+    for j, ref in enumerate((left, own, right)):
+        stiff = []
+        for k in range(8):
+            columns = slice(k * 128, k * 128 + 128)
+            stiff.append(ref[STIFF_AT + k * 8 : STIFF_AT + k * 8 + 8, :])
+            for c in range(3):
                 place = (c * 8 + k) * 8
-                work[0, c, j * 8 : j * 8 + 8, k * 128 : k * 128 + 128] = (
-                    force[k * 8 : k * 8 + 8] + ref[place : place + 8, :]
-                )
-        stiff = jnp.concatenate(
-            [ref[STIFF_AT + k * 8 : STIFF_AT + k * 8 + 8, :] for k in range(8)], 1
-        )
+                here = slice(j * 8, j * 8 + 8)
+                work[0, c, here, columns] = forces[c, here, columns] + ref[place : place + 8, :]
+        stiff = jnp.concatenate(stiff, 1)
         if j == 1:
             stiffness = stiff
         for c in range(3):
@@ -643,21 +679,13 @@
         image = (4.0 + stiffness) * now - ahead(now, 1) - behind(now, 1) - 2.0 * after
         total = total + now * image
     tile = place_pair(tile, ENERGY_AT[0], (ENERGY_AT[1], None, None), whole(fold(total)))
-    fields = vectors[:SITERS] + [lambda c: displacement[c]]
-    fields += [lambda c, k=k: solved_history[k, c] for k in range(solved_history.shape[0])]
-    fields.append(lambda c: solved_prev[c])
-    for c in range(3):
-        for f in range(16):
-            value = fields[f](c) if f < len(fields) else jnp.zeros((8, 1024), F32)
-            for k in range(8):
-                table[k, pl.ds(c * 16 + f, 8, stride=48), :] = value[:, k * 128 : k * 128 + 128]
-    column = lax.broadcasted_iota(jnp.int32, (1024, entries), 0)
-    pick = jnp.where(column == (node & 1023), 1.0, 0.0).astype(BF16)
-    found = split_dot(jnp.concatenate([table[k] for k in range(8)], 1), pick, 2)
-    line = node >> 10
-    answer = jnp.zeros((48, entries), F32)
-    for r in range(8):
-        answer = jnp.where(line == r, found[r * 48 : r * 48 + 48], answer)
+    node = requests[0:1, :]
+    entries = node.shape[1]
+    found = nodes_values(
+        [lambda c, k=k: basis_tile(k, c) for k in range(SITERS)], table, picked_nodes(node), node >> 10
+    )
+    answer = [values[c * 8 : c * 8 + 8] for c in range(3) for values in (found, fixed)]
+    answer = jnp.concatenate(answer, 0)
     lane16 = lax.broadcasted_iota(jnp.int32, (16, 128), 1)
     row16 = lax.broadcasted_iota(jnp.int32, (16, 128), 0)
     extra = jnp.concatenate(
@@ -831,18 +859,27 @@
         ),
     )
     received = lax.all_to_all(payload, "slab", split_axis=0, concat_axis=0, tiled=True)
-    payload, shell_basis, factors = call(
+    entries = ranks * CAP
+    forces, requests, fixed, factors = call(
+        lambda *refs: force_kernel(*refs, ranks=ranks),
+        (
+            shape(3, 3 * displacement.shape[1], displacement.shape[2]),
+            shape(8, entries, dtype=jnp.int32), shape(24, entries), shape(8, 128),
+        ),
+        (received, displacement, solved_prev, solved_history),
+        scratch=(pltpu.VMEM((8, 8 * 24, 128), F32),),
+    )
+    payload, shell_basis = call(
         lambda *refs: shell_kernel(*refs, ranks=ranks),
-        (shape(ranks, 3, 4, 128), pltpu.HBM((SITERS, *displacement.shape), F32), shape(8, 128)),
+        (shape(ranks, 3, 4, 128), pltpu.HBM((SITERS, *displacement.shape), F32)),
         (
-            received, shell, shell_mate, shell_other,
-            displacement, residual_prev, solved_prev, residual_history, solved_history,
+            forces, requests, fixed, shell, shell_mate, shell_other, residual_prev, residual_history,
         ),
         direct=(1,),
         scratch=(
             pltpu.VMEM((SITERS, 3, 24, 1024), F32),
             pltpu.VMEM((72, 1024), F32),
-            pltpu.VMEM((8, 8 * 48, 128), F32),
+            pltpu.VMEM((8, 8 * 24, 128), F32),
             pltpu.SemaphoreType.DMA((SITERS,)),
         ),
     )

time: 66.2 us -> 64 us (0.967)
  starting transfers between devices: 22.2 us -> 19.9 us
    all_to_all x2, starting transfers between devices: 10.6 us -> 8.3 us  [on_device(): lax.all_to_all(payload, 'slab', split_axis=0, concat_axis=0, tiled=True)]
    pallas_call x7 -> x8, Pallas kernels: 17.4 us -> 17.4 us  [call(): pl.pallas_call(body, out_shape=outs, in_specs=[any_space if i in outside...]
  transfers between devices with their start and end apart: 11 -> 11, of which waited for: 4 -> 3; matrix products, arithmetic and copies ran while one was open for 2% -> 2% of each run, Pallas kernels for 5% -> 8%
where the time goes in v5:
time: 64 us; the launch traced here: 63.5 us
  waiting for transfers between devices  23.9 us (37%)
  starting transfers between devices  19.9 us (31%)
  Pallas kernels  17.4 us (27%)
  between operations  0.97 us (2%)
  other arithmetic  0.66 us (1%)
    pallas_call x8, Pallas kernels, call(): pl.pallas_call(body, out_shape=outs, in_specs=[any_space if i in outside...  17.4 us
    all_to_all x2, waiting for transfers between devices, on_device(): lax.all_to_all(payload, 'slab', split_axis=0, concat_axis=0, tiled=True)  13.9 us
    ppermute x1, waiting for transfers between devices, on_device(): beyond = lax.ppermute(first, 'slab', [(i, i - 2) for i in range(2, ranks)])  10 us
    all_to_all x2, starting transfers between devices, on_device(): lax.all_to_all(payload, 'slab', split_axis=0, concat_axis=0, tiled=True)  8.3 us
    ppermute x4, starting transfers between devices, with_mate(): return lax.ppermute(values, 'slab', [(i, i ^ 1) for i in range(ranks)])  7.67 us
    ppermute x4, starting transfers between devices, with_other(): return lax.ppermute(values, 'slab', pairs + [(j, i) for i, j in pairs])  2.65 us
    ppermute x1, starting transfers between devices, on_device(): beyond = lax.ppermute(first, 'slab', [(i, i - 2) for i in range(2, ranks)])  1.29 us
  transfers between devices with their start and end apart: 11, of which 3 were waited for; matrix products, arithmetic and copies ran while one was open for 2% of the time, Pallas kernels for 8%

profile of v5, /device:TPU:0, one launch (start us, length us, event | category | flops | bytes accessed | tf_op | source)
XLA Modules:
  0.0 63.5 jit_solution(226021790474394022)
XLA Ops:
  0.7 2.1 %shard_map.139 = (f32[288,128]{1,0:T(8,128)S(1)}, f32[288,128]{1,0:T(8,128)S(1)}, f32[64,256]{1,0:T(8,128)S(1)}, f32[64,256]{1,0:T(8,128)S(1)}, f32[4,64,256]{2,1,0:T(8,128)S(1)}, /*index=5*/f32[8,256]{1,0:T(8,128)S(1)}) custom-call(f32[3,4,64,256]{3,2,1,0:T(8,128)} %refs_0_.1, f32[3,8,1024]{2,1,0:T(8,128)} %refs_2_.3), custom_call_target="tpu_custom_call" | custom-call | flops 1000000000 | tf_op jit(solution)/shard_map/pallas_call | solution.py:124
  2.8 0.5 collective-permute-start
  3.3 0.7 %collective-permute-start.1 = (f32[288,128]{1,0:T(8,128)S(1)}, f32[288,128]{1,0:T(8,128)S(1)}, u32[]{:S(2)}, u32[]{:S(2)}) collective-permute-start(f32[288,128]{1,0:T(8,128)S(1)} %get-tuple-element.28), channel_id=1, source_target_pairs={{1,2},{3,4},{5,6},{7,8},{9,10},{11,12},{13,14},{15,16},{17,18},{19... | collective-permute-start | bytes 442376 | tf_op jit(solution)/shard_map/ppermute | solution.py:807
  3.9 3.9 %collective-permute-start.5 = (f32[4,64,256]{2,1,0:T(8,128)S(1)}, f32[4,64,256]{2,1,0:T(8,128)S(1)}, u32[]{:S(2)}, u32[]{:S(2)}) collective-permute-start(f32[4,64,256]{2,1,0:T(8,128)S(1)} %copy-done.2), channel_id=1, source_target_pairs={{0,1},{1,0},{2,3},{3,2},{4,5},{5,4},{6,7},{7,6},{8,9},{9,8},{10,11... | collective-permute-start | bytes 786440 | tf_op jit(solution)/shard_map/ppermute | solution.py:803
  7.9 0.7 %collective-permute-start.6 = (f32[4,64,256]{2,1,0:T(8,128)S(1)}, f32[4,64,256]{2,1,0:T(8,128)S(1)}, u32[]{:S(2)}, u32[]{:S(2)}) collective-permute-start(f32[4,64,256]{2,1,0:T(8,128)S(1)} %copy-done.2), channel_id=1, source_target_pairs={{1,2},{3,4},{5,6},{7,8},{9,10},{11,12},{13,14},{15,16},{17,18},{19... | collective-permute-start | bytes 786440 | tf_op jit(solution)/shard_map/ppermute | solution.py:807
  8.6 0.6 shard_map.140
  9.2 2.9 %collective-permute-start.2 = (f32[512,128]{1,0:T(8,128)S(1)}, f32[512,128]{1,0:T(8,128)S(1)}, u32[]{:S(2)}, u32[]{:S(2)}) collective-permute-start(f32[512,128]{1,0:T(8,128)S(1)} %get-tuple-element.29.refs_0_), channel_id=1, source_target_pairs={{0,1},{1,0},{2,3},{3,2},{4,5},{5,4},{6,7},{7,6},{8,9},{9,8},{10,11... | collective-permute-start | bytes 786440 | tf_op jit(solution)/shard_map/ppermute | solution.py:803
  12.1 0.7 %collective-permute-start.3 = (f32[512,128]{1,0:T(8,128)S(1)}, f32[512,128]{1,0:T(8,128)S(1)}, u32[]{:S(2)}, u32[]{:S(2)}) collective-permute-start(f32[512,128]{1,0:T(8,128)S(1)} %get-tuple-element.29.refs_0_), channel_id=1, source_target_pairs={{1,2},{3,4},{5,6},{7,8},{9,10},{11,12},{13,14},{15,16},{17,18},{19... | collective-permute-start | bytes 786440 | tf_op jit(solution)/shard_map/ppermute | solution.py:807
  12.8 0.5 broadcast.3
  13.3 0.7 %reduce.3 = s32[1024]{0:T(1024)S(1)} reduce(s32[1024,1]{0,1:T(1,128)S(1)} %copy-done.9, s32[]{:T(128)} %broadcast.3), dimensions={1}, to_apply=%param.14.reduce_sub_computation.3 | reduce | bytes 8196 | tf_op args[2]
  14.0 1.3 %collective-permute-start.4 = (f32[128,128]{1,0:T(8,128)S(1)}, f32[128,128]{1,0:T(8,128)S(1)}, u32[]{:S(2)}, u32[]{:S(2)}) collective-permute-start(f32[128,128]{1,0:T(8,128)S(1)} %get-tuple-element.30), channel_id=1, source_target_pairs={{2,0},{3,1},{4,2},{5,3},{6,4},{7,5},{8,6},{9,7},{10,8},{11,9},{12,... | collective-permute-start | bytes 196616 | tf_op jit(solution)/shard_map/ppermute | solution.py:845
  15.3 0.2 shard_map.141.refs_9_.refs_6_
  15.6 10.0 %collective-permute-done.4.refs_3_ = f32[128,128]{1,0:T(8,128)S(1)} collective-permute-done((f32[128,128]{1,0:T(8,128)S(1)}, f32[128,128]{1,0:T(8,128)S(1)}, u32[]{:S(2)}, u32[]{:S(2)}) %collective-permute-start.4) | collective-permute-done | bytes 65568 | tf_op jit(solution)/shard_map/ppermute | solution.py:845
  25.6 3.6 %shard_map.142 = (f32[32,8,128]{2,1,0:T(8,128)}, f32[5,4,64,256]{3,2,1,0:T(8,128)}) custom-call(f32[512,128]{1,0:T(8,128)S(1)} %get-tuple-element.29.refs_0_, f32[512,128]{1,0:T(8,128)S(1)} %collective-permute-done.2.refs_1_, f32[512,128]{1,0:T(8,128)S(1)} %collective-permute-done.3.refs_2_, f32[128,128]{1,0:T(8,128)S(1)} %collective-permute-done.4.refs_3_, ...), custom_call_target="tpu_custom_call" | custom-call | flops 1000000000 | tf_op jit(solution)/shard_map/pallas_call | solution.py:124
  29.2 5.5 %all-to-all-start = ((f32[32,8,128]{2,1,0:T(8,128)}), f32[32,8,128]{2,1,0:T(8,128)S(1)}, u32[]{:S(2)}, u32[]{:S(2)}) async-start(f32[32,8,128]{2,1,0:T(8,128)} %get-tuple-element.33), calls=%async_computation | async-start | bytes 262144 | tf_op jit(solution)/shard_map/all_to_all | solution.py:861
  34.7 0.3 collective-permute-start.7
  35.0 0.7 %collective-permute-start.8 = (f32[256,128]{1,0:T(8,128)S(1)}, f32[256,128]{1,0:T(8,128)S(1)}, u32[]{:S(2)}, u32[]{:S(2)}) collective-permute-start(f32[256,128]{1,0:T(8,128)S(1)} %get-tuple-element.38.refs_3_), channel_id=1, source_target_pairs={{1,2},{3,4},{5,6},{7,8},{9,10},{11,12},{13,14},{15,16},{17,18},{19... | collective-permute-start | bytes 393224 | tf_op jit(solution)/shard_map/ppermute | solution.py:807
  35.7 7.2 %all-to-all-done.refs_0_ = f32[32,8,128]{2,1,0:T(8,128)S(1)} async-done(((f32[32,8,128]{2,1,0:T(8,128)}), f32[32,8,128]{2,1,0:T(8,128)S(1)}, u32[]{:S(2)}, u32[]{:S(2)}) %all-to-all-start) | async-done | bytes 131104 | tf_op jit(solution)/shard_map/all_to_all | solution.py:861
  42.9 2.2 %shard_map.143 = (f32[3,24,1024]{2,1,0:T(8,128)S(1)}, s32[8,1024]{1,0:T(8,128)S(1)}, f32[24,1024]{1,0:T(8,128)S(1)}, f32[8,128]{1,0:T(8,128)S(1)}) custom-call(f32[32,8,128]{2,1,0:T(8,128)S(1)} %all-to-all-done.refs_0_, f32[3,8,1024]{2,1,0:T(8,128)S(1)} %copy-done.5, f32[3,8,1024]{2,1,0:T(8,128)S(1)} %copy-done.6, f32[4,3,8,1024]{3,2,1,0:T(8,128)S(1)} %copy-done.1), custom_call_target="tpu_custom_call" | custom-call | flops 1000000000 | tf_op jit(solution)/shard_map/pallas_call | solution.py:124
  45.2 4.8 %shard_map.145 = (f32[32,3,4,128]{3,2,1,0:T(4,128)}, f32[8,3,8,1024]{3,2,1,0:T(8,128)}) custom-call(f32[3,24,1024]{2,1,0:T(8,128)S(1)} %get-tuple-element.35.refs_0_, s32[8,1024]{1,0:T(8,128)S(1)} %get-tuple-element.36.refs_1_, f32[24,1024]{1,0:T(8,128)S(1)} %get-tuple-element.37.refs_2_, f32[256,128]{1,0:T(8,128)S(1)} %get-tuple-element.38.refs_3_, ...), custom_call_target="tpu_custom_call" | custom-call | flops 1000000000 | tf_op jit(solution)/shard_map/pallas_call | solution.py:124
  50.0 2.8 %all-to-all-start.1 = ((f32[32,3,4,128]{3,2,1,0:T(4,128)}), f32[32,3,4,128]{3,2,1,0:T(4,128)S(1)}, u32[]{:S(2)}, u32[]{:S(2)}) async-start(f32[32,3,4,128]{3,2,1,0:T(4,128)} %get-tuple-element.39), calls=%async_computation.1 | async-start | bytes 393216 | tf_op jit(solution)/shard_map/all_to_all | solution.py:886
  52.8 2.2 %shard_map.144 = f32[4,64,256]{2,1,0:T(8,128)} custom-call(f32[5,4,64,256]{3,2,1,0:T(8,128)} %get-tuple-element.32.refs_0_, f32[8,128]{1,0:T(8,128)S(1)} %get-tuple-element.34.refs_1_), custom_call_target="tpu_custom_call" | custom-call | flops 1000000000 | tf_op jit(solution)/shard_map/pallas_call | solution.py:124
  55.1 6.7 %all-to-all-done.1.refs_0_ = f32[32,3,4,128]{3,2,1,0:T(4,128)S(1)} async-done(((f32[32,3,4,128]{3,2,1,0:T(4,128)}), f32[32,3,4,128]{3,2,1,0:T(4,128)S(1)}, u32[]{:S(2)}, u32[]{:S(2)}) %all-to-all-start.1) | async-done | bytes 196640 | tf_op jit(solution)/shard_map/all_to_all | solution.py:886
  61.7 1.8 %shard_map.146 = (f32[3,8,1024]{2,1,0:T(8,128)}, f32[3,1024]{1,0:T(4,128)}) custom-call(f32[32,3,4,128]{3,2,1,0:T(4,128)S(1)} %all-to-all-done.1.refs_0_, f32[8,3,8,1024]{3,2,1,0:T(8,128)S(1)} %copy-done.8, f32[3,8,1024]{2,1,0:T(8,128)S(1)} %copy-done.5, f32[3,8,1024]{2,1,0:T(8,128)S(1)} %copy-done.6, f32[4,3,8,1024]{3,2,1,0:T(8,128)S(1)} %copy-done.1, ...), custom_call_target="tpu_custom_call" | custom-call | flops 1000000000 | tf_op jit(solution)/shard_map/pallas_call | solution.py:124
  (35 shorter events, 0.1 us)
Async XLA Ops:
  0.6 7.9 %copy-start.5 = (f32[3,8,1024]{2,1,0:T(8,128)S(1)}, f32[3,8,1024]{2,1,0:T(8,128)}, u32[]{:S(2)}) copy-start(f32[3,8,1024]{2,1,0:T(8,128)} %refs_2_.3) | copy-start | bytes 294916
  0.6 3.3 %copy-start.2 = (f32[4,64,256]{2,1,0:T(8,128)S(1)}, f32[4,64,256]{2,1,0:T(8,128)}, u32[]{:S(2)}) copy-start(f32[4,64,256]{2,1,0:T(8,128)} %refs_4_.2) | copy-start | bytes 786436
  0.7 7.9 %copy-start.3 = (f32[3,8,1024]{2,1,0:T(8,128)S(1)}, f32[3,8,1024]{2,1,0:T(8,128)}, u32[]{:S(2)}) copy-start(f32[3,8,1024]{2,1,0:T(8,128)} %refs_7_.2) | copy-start | bytes 294916
  0.7 7.9 %copy-start.7 = (f32[8,1024]{1,0:T(8,128)S(1)}, f32[8,1024]{1,0:T(8,128)}, u32[]{:S(2)}) copy-start(f32[8,1024]{1,0:T(8,128)} %refs_8_.1) | copy-start | bytes 98308
  2.8 5.8 %collective-permute-start = (f32[288,128]{1,0:T(8,128)S(1)}, f32[288,128]{1,0:T(8,128)S(1)}, u32[]{:S(2)}, u32[]{:S(2)}) collective-permute-start(f32[288,128]{1,0:T(8,128)S(1)} %get-tuple-element.27), channel_id=1, source_target_pairs={{0,1},{1,0},{2,3},{3,2},{4,5},{5,4},{6,7},{7,6},{8,9},{9,8},{10,11... | collective-permute-start | bytes 442376 | tf_op jit(solution)/shard_map/ppermute | solution.py:803
  3.3 5.3 %collective-permute-start.1 = (f32[288,128]{1,0:T(8,128)S(1)}, f32[288,128]{1,0:T(8,128)S(1)}, u32[]{:S(2)}, u32[]{:S(2)}) collective-permute-start(f32[288,128]{1,0:T(8,128)S(1)} %get-tuple-element.28), channel_id=1, source_target_pairs={{1,2},{3,4},{5,6},{7,8},{9,10},{11,12},{13,14},{15,16},{17,18},{19... | collective-permute-start | bytes 442376 | tf_op jit(solution)/shard_map/ppermute | solution.py:807
  3.9 21.6 %collective-permute-start.5 = (f32[4,64,256]{2,1,0:T(8,128)S(1)}, f32[4,64,256]{2,1,0:T(8,128)S(1)}, u32[]{:S(2)}, u32[]{:S(2)}) collective-permute-start(f32[4,64,256]{2,1,0:T(8,128)S(1)} %copy-done.2), channel_id=1, source_target_pairs={{0,1},{1,0},{2,3},{3,2},{4,5},{5,4},{6,7},{7,6},{8,9},{9,8},{10,11... | collective-permute-start | bytes 786440 | tf_op jit(solution)/shard_map/ppermute | solution.py:803
  7.9 17.7 %collective-permute-start.6 = (f32[4,64,256]{2,1,0:T(8,128)S(1)}, f32[4,64,256]{2,1,0:T(8,128)S(1)}, u32[]{:S(2)}, u32[]{:S(2)}) collective-permute-start(f32[4,64,256]{2,1,0:T(8,128)S(1)} %copy-done.2), channel_id=1, source_target_pairs={{1,2},{3,4},{5,6},{7,8},{9,10},{11,12},{13,14},{15,16},{17,18},{19... | collective-permute-start | bytes 786440 | tf_op jit(solution)/shard_map/ppermute | solution.py:807
  8.6 4.7 %copy-start.9 = (s32[1024,1]{0,1:T(1,128)S(1)}, s32[1024,1]{0,1:T(1,128)}, u32[]{:S(2)}) copy-start(s32[1024,1]{0,1:T(1,128)} %param.14) | copy-start | bytes 12292
  8.6 5.4 %copy-start.10 = (s32[1024]{0:T(1024)S(1)}, s32[1024]{0:T(1024)}, u32[]{:S(2)}) copy-start(s32[1024]{0:T(1024)} %param.15) | copy-start | bytes 12292
  8.6 5.4 %copy-start.11 = (s32[1024]{0:T(1024)S(1)}, s32[1024]{0:T(1024)}, u32[]{:S(2)}) copy-start(s32[1024]{0:T(1024)} %param.16) | copy-start | bytes 12292
  9.2 16.4 %collective-permute-start.2 = (f32[512,128]{1,0:T(8,128)S(1)}, f32[512,128]{1,0:T(8,128)S(1)}, u32[]{:S(2)}, u32[]{:S(2)}) collective-permute-start(f32[512,128]{1,0:T(8,128)S(1)} %get-tuple-element.29.refs_0_), channel_id=1, source_target_pairs={{0,1},{1,0},{2,3},{3,2},{4,5},{5,4},{6,7},{7,6},{8,9},{9,8},{10,11... | collective-permute-start | bytes 786440 | tf_op jit(solution)/shard_map/ppermute | solution.py:803
  12.1 13.5 %collective-permute-start.3 = (f32[512,128]{1,0:T(8,128)S(1)}, f32[512,128]{1,0:T(8,128)S(1)}, u32[]{:S(2)}, u32[]{:S(2)}) collective-permute-start(f32[512,128]{1,0:T(8,128)S(1)} %get-tuple-element.29.refs_0_), channel_id=1, source_target_pairs={{1,2},{3,4},{5,6},{7,8},{9,10},{11,12},{13,14},{15,16},{17,18},{19... | collective-permute-start | bytes 786440 | tf_op jit(solution)/shard_map/ppermute | solution.py:807
  14.0 11.6 %collective-permute-start.4 = (f32[128,128]{1,0:T(8,128)S(1)}, f32[128,128]{1,0:T(8,128)S(1)}, u32[]{:S(2)}, u32[]{:S(2)}) collective-permute-start(f32[128,128]{1,0:T(8,128)S(1)} %get-tuple-element.30), channel_id=1, source_target_pairs={{2,0},{3,1},{4,2},{5,3},{6,4},{7,5},{8,6},{9,7},{10,8},{11,9},{12,... | collective-permute-start | bytes 196616 | tf_op jit(solution)/shard_map/ppermute | solution.py:845
  25.6 17.3 %copy-start.1 = (f32[4,3,8,1024]{3,2,1,0:T(8,128)S(1)}, f32[4,3,8,1024]{3,2,1,0:T(8,128)}, u32[]{:S(2)}) copy-start(f32[4,3,8,1024]{3,2,1,0:T(8,128)} %refs_4_.3) | copy-start | bytes 1179652
  25.6 17.3 %copy-start.6 = (f32[3,8,1024]{2,1,0:T(8,128)S(1)}, f32[3,8,1024]{2,1,0:T(8,128)}, u32[]{:S(2)}) copy-start(f32[3,8,1024]{2,1,0:T(8,128)} %refs_3_.3) | copy-start | bytes 294916
  29.2 13.7 %all-to-all-start = ((f32[32,8,128]{2,1,0:T(8,128)}), f32[32,8,128]{2,1,0:T(8,128)S(1)}, u32[]{:S(2)}, u32[]{:S(2)}) async-start(f32[32,8,128]{2,1,0:T(8,128)} %get-tuple-element.33), calls=%async_computation | async-start | bytes 262144 | tf_op jit(solution)/shard_map/all_to_all | solution.py:861
  34.7 10.5 %copy-start = (f32[4,3,8,1024]{3,2,1,0:T(8,128)S(1)}, f32[4,3,8,1024]{3,2,1,0:T(8,128)}, u32[]{:S(2)}) copy-start(f32[4,3,8,1024]{3,2,1,0:T(8,128)} %refs_7_.3) | copy-start | bytes 1179652
  34.7 10.5 %copy-start.4 = (f32[3,8,1024]{2,1,0:T(8,128)S(1)}, f32[3,8,1024]{2,1,0:T(8,128)}, u32[]{:S(2)}) copy-start(f32[3,8,1024]{2,1,0:T(8,128)} %refs_6_.3) | copy-start | bytes 294916
  34.7 10.5 %collective-permute-start.7 = (f32[256,128]{1,0:T(8,128)S(1)}, f32[256,128]{1,0:T(8,128)S(1)}, u32[]{:S(2)}, u32[]{:S(2)}) collective-permute-start(f32[256,128]{1,0:T(8,128)S(1)} %get-tuple-element.38.refs_3_), channel_id=1, source_target_pairs={{0,1},{1,0},{2,3},{3,2},{4,5},{5,4},{6,7},{7,6},{8,9},{9,8},{10,11... | collective-permute-start | bytes 393224 | tf_op jit(solution)/shard_map/ppermute | solution.py:803
  35.0 10.2 %collective-permute-start.8 = (f32[256,128]{1,0:T(8,128)S(1)}, f32[256,128]{1,0:T(8,128)S(1)}, u32[]{:S(2)}, u32[]{:S(2)}) collective-permute-start(f32[256,128]{1,0:T(8,128)S(1)} %get-tuple-element.38.refs_3_), channel_id=1, source_target_pairs={{1,2},{3,4},{5,6},{7,8},{9,10},{11,12},{13,14},{15,16},{17,18},{19... | collective-permute-start | bytes 393224 | tf_op jit(solution)/shard_map/ppermute | solution.py:807
  50.0 11.7 %all-to-all-start.1 = ((f32[32,3,4,128]{3,2,1,0:T(4,128)}), f32[32,3,4,128]{3,2,1,0:T(4,128)S(1)}, u32[]{:S(2)}, u32[]{:S(2)}) async-start(f32[32,3,4,128]{3,2,1,0:T(4,128)} %get-tuple-element.39), calls=%async_computation.1 | async-start | bytes 393216 | tf_op jit(solution)/shard_map/all_to_all | solution.py:886
  52.8 8.9 %copy-start.8 = (f32[8,3,8,1024]{3,2,1,0:T(8,128)S(1)}, f32[8,3,8,1024]{3,2,1,0:T(8,128)}, u32[]{:S(2)}) copy-start(f32[8,3,8,1024]{3,2,1,0:T(8,128)} %get-tuple-element.40.refs_1_) | copy-start | bytes 2359300

commit v6 on v5

--- a/solution.py
+++ b/solution.py
@@ -212,26 +212,36 @@
     return sum(product[i * rows : (i + 1) * rows] for i in range(count))
 
 
-def fluid_kernel(
-    velocity_in, displacement_in, to_mate, to_other, own_left, own_right, source, wall,
+def plane_part(plane):
+    return (1.0 - 6.0 * NU) * plane + NU * plane_sum(plane)
+
+
+def edge_kernel(
+    velocity_in, displacement_in, to_mate, to_other, own_left, own_right,
     velocity, displacement, arrived,
 ):
-    copies = [pltpu.make_async_copy(velocity_in, velocity, arrived.at[0, 0])]
+    layers = velocity.shape[1]
+    last = layers - 1
+    copies = [pltpu.make_async_copy(velocity_in.at[0], velocity.at[0], arrived.at[0, 0])]
+    for c in (1, 2):
+        for x in (0, last):
+            copies.append(
+                pltpu.make_async_copy(velocity_in.at[c, x], velocity.at[c, x], arrived.at[c, x])
+            )
     copies.append(pltpu.make_async_copy(displacement_in, displacement, arrived.at[3, 0]))
     for copy in copies:
         copy.start()
     for copy in copies:
         copy.wait()
     even = even_device()
-    layers = velocity.shape[1]
-    last = layers - 1
-    field = [[velocity[c, x] for x in range(layers)] for c in range(3)]
-    own = [[(1.0 - 6.0 * NU) * f + NU * plane_sum(f) for f in rows] for rows in field]
     spread = {
-        x: NU * (difference(field[1][x], 0) + difference(field[2][x], 1)) for x in (0, last)
+        x: NU * (difference(velocity[1, x], 0) + difference(velocity[2, x], 1)) for x in (0, last)
     }
-    lefts = (own[0][0] + NU * field[0][1] + spread[0], NU * field[0][0])
-    rights = (spread[last] - own[0][last] - NU * field[0][last - 1], NU * field[0][last])
+    lefts = (plane_part(velocity[0, 0]) + NU * velocity[0, 1] + spread[0], NU * velocity[0, 0])
+    rights = (
+        spread[last] - plane_part(velocity[0, last]) - NU * velocity[0, last - 1],
+        NU * velocity[0, last],
+    )
     own_left[...] = lefts[1]
     own_right[...] = rights[1]
     edges = [
@@ -251,6 +261,13 @@
             for k in range(8):
                 place = DISP_AT + c * 8 + k
                 ref[place : place + 1, :] = row[:, k * 128 : k * 128 + 128]
+
+
+def fluid_kernel(velocity, source, wall):
+    layers = velocity.shape[1]
+    last = layers - 1
+    field = [[velocity[c, x] for x in range(layers)] for c in range(3)]
+    own = [[plane_part(f) for f in rows] for rows in field]
     zero = jnp.zeros_like(field[0][0])
     predicted = [
         [
@@ -332,8 +349,10 @@
         shell[place : place + 8, :] = stiffness[:, k * 128 : k * 128 + 128]
 
 
-def slots_kernel(owner, slots, *, ranks):
+def slots_kernel(owners, slots, owner, *, ranks):
     width = owner.shape[1]
+    for x in range(owner.shape[0]):
+        owner[x : x + 1, :] = owners[:, x * width : x * width + width]
     down = lax.broadcasted_iota(jnp.int32, (width, width), 0)
     across = lax.broadcasted_iota(jnp.int32, (width, width), 1)
     earlier = jnp.where(down < across, 1.0, 0.0).astype(BF16)
@@ -718,11 +737,8 @@
     received, basis, displacement, solved_prev, solved_history, owner, slots,
     new_displacement, wall, *, ranks,
 ):
-    blocks = [
-        jnp.concatenate([received[p, t] for t in range(3)] + [jnp.zeros((4, 128), F32)], 0)
-        for p in range(ranks)
-    ]
-    summed = sum(blocks)
+    summed = [sum(received[p, t] for p in range(ranks)) for t in range(3)]
+    summed = jnp.concatenate(summed + [jnp.zeros((4, 128), F32)], 0)
     matrix = second_gram(summed)
     gram = [column_of(matrix, k) for k in range(SITERS + 5)]
     energy = summed[ENERGY_AT[0] : ENERGY_AT[0] + 1, ENERGY_AT[1] : ENERGY_AT[1] + 1]
@@ -767,7 +783,9 @@
     stacked = []
     for c in range(3):
         scales = jnp.where(group == c, factors, jnp.where((group == 3) & (row // 2 == c), spare, 0.0))
-        stacked += [jnp.sum(block * scales, 0, keepdims=True) for block in blocks]
+        scales = [scales[t * 4 : t * 4 + 4] for t in range(3)]
+        for p in range(ranks):
+            stacked.append(jnp.sum(sum(received[p, t] * scales[t] for t in range(3)), 0, keepdims=True))
     stacked = jnp.concatenate(stacked, 0)
     slot_row = lax.broadcasted_iota(jnp.int32, (128, 256), 0) & 31
     rank = lax.broadcasted_iota(jnp.int32, (ranks, 256), 0)
@@ -806,17 +824,13 @@
         pairs = [(i, i + 1) for i in range(1, ranks - 1, 2)]
         return lax.ppermute(values, "slab", pairs + [(j, i) for i, j in pairs])
 
-    owner = owner_rank.reshape(layers, -1)
     node = node_index.reshape(layers, -1)
     weight = map_weight.reshape(layers, -1)
     plane = shape(*velocity.shape[2:])
 
-    to_mate, to_other, own_left, own_right, source, wall = call(
-        fluid_kernel,
-        (
-            shape(HALO_ROWS, 128), shape(HALO_ROWS, 128), plane, plane,
-            shape(*velocity.shape[1:]), shape(8, 256),
-        ),
+    to_mate, to_other, own_left, own_right = call(
+        edge_kernel,
+        (shape(HALO_ROWS, 128), shape(HALO_ROWS, 128), plane, plane),
         (velocity, displacement),
         outer=(0, 1),
         stored=(0, 1),
@@ -828,10 +842,11 @@
     )
     halo_other, halo_mate = with_other(to_other), with_mate(to_mate)
     shift_other, shift_mate = with_other(pressure_shift), with_mate(pressure_shift)
-    (slots,) = call(
-        lambda *refs: slots_kernel(*refs[:2], ranks=ranks),
-        (shape(layers, 256, dtype=jnp.int32),),
-        (owner,),
+    source, wall = call(fluid_kernel, (shape(*velocity.shape[1:]), shape(8, 256)), (velocity,))
+    slots, owner = call(
+        lambda *refs: slots_kernel(*refs, ranks=ranks),
+        (shape(layers, 256, dtype=jnp.int32), shape(layers, 256, dtype=jnp.int32)),
+        (owner_rank.T,),
     )
     fields, first, shell, wall = call(
         lambda *refs: source_kernel(*refs),

time: 64 us -> 63.5 us (level)
  other arithmetic: 0.66 us -> 0 us
    unnamed x1 -> x0, other arithmetic: 0.66 us -> none
    pallas_call x8 -> x9, Pallas kernels: 17.4 us -> 17.5 us  [call(): pl.pallas_call(body, out_shape=outs, in_specs=[any_space if i in outside...]
  transfers between devices with their start and end apart: 11 -> 11, of which waited for: 3 -> 3; matrix products, arithmetic and copies ran while one was open for 2% -> 0% of each run, Pallas kernels for 8% -> 10%
where the time goes in v6:
time: 63.5 us; the launch traced here: 62.9 us
  waiting for transfers between devices  24.3 us (38%)
  starting transfers between devices  20.1 us (32%)
  Pallas kernels  17.5 us (28%)
  between operations  0.96 us (2%)
    pallas_call x9, Pallas kernels, call(): pl.pallas_call(body, out_shape=outs, in_specs=[any_space if i in outside...  17.5 us
    all_to_all x2, waiting for transfers between devices, on_device(): lax.all_to_all(payload, 'slab', split_axis=0, concat_axis=0, tiled=True)  13.9 us
    ppermute x1, waiting for transfers between devices, on_device(): beyond = lax.ppermute(first, 'slab', [(i, i - 2) for i in range(2, ranks)])  10.4 us
    all_to_all x2, starting transfers between devices, on_device(): lax.all_to_all(payload, 'slab', split_axis=0, concat_axis=0, tiled=True)  8.3 us
    ppermute x4, starting transfers between devices, with_mate(): return lax.ppermute(values, 'slab', [(i, i ^ 1) for i in range(ranks)])  7.7 us
    ppermute x4, starting transfers between devices, with_other(): return lax.ppermute(values, 'slab', pairs + [(j, i) for i, j in pairs])  2.78 us
    ppermute x1, starting transfers between devices, on_device(): beyond = lax.ppermute(first, 'slab', [(i, i - 2) for i in range(2, ranks)])  1.29 us
  transfers between devices with their start and end apart: 11, of which 3 were waited for; matrix products, arithmetic and copies ran while one was open for 0% of the time, Pallas kernels for 10%

profile of v6, /device:TPU:0, one launch (start us, length us, event | category | flops | bytes accessed | tf_op | source)
XLA Modules:
  0.0 62.9 jit_solution(16667299519084003178)
XLA Ops:
  0.6 1.6 %shard_map.140 = (f32[288,128]{1,0:T(8,128)S(1)}, f32[288,128]{1,0:T(8,128)S(1)}, f32[64,256]{1,0:T(8,128)S(1)}, f32[64,256]{1,0:T(8,128)S(1)}) custom-call(f32[3,4,64,256]{3,2,1,0:T(8,128)} %refs_0_.3, f32[3,8,1024]{2,1,0:T(8,128)} %refs_2_.3), custom_call_target="tpu_custom_call" | custom-call | flops 1000000000 | tf_op jit(solution)/shard_map/pallas_call | solution.py:124
  2.2 0.5 collective-permute-start
  2.8 0.8 %collective-permute-start.1 = (f32[288,128]{1,0:T(8,128)S(1)}, f32[288,128]{1,0:T(8,128)S(1)}, u32[]{:S(2)}, u32[]{:S(2)}) collective-permute-start(f32[288,128]{1,0:T(8,128)S(1)} %get-tuple-element.30), channel_id=1, source_target_pairs={{1,2},{3,4},{5,6},{7,8},{9,10},{11,12},{13,14},{15,16},{17,18},{19... | collective-permute-start | bytes 442376 | tf_op jit(solution)/shard_map/ppermute | solution.py:825
  3.6 4.0 %collective-permute-start.5 = (f32[4,64,256]{2,1,0:T(8,128)S(1)}, f32[4,64,256]{2,1,0:T(8,128)S(1)}, u32[]{:S(2)}, u32[]{:S(2)}) collective-permute-start(f32[4,64,256]{2,1,0:T(8,128)S(1)} %copy-done.3), channel_id=1, source_target_pairs={{0,1},{1,0},{2,3},{3,2},{4,5},{5,4},{6,7},{7,6},{8,9},{9,8},{10,11... | collective-permute-start | bytes 786440 | tf_op jit(solution)/shard_map/ppermute | solution.py:821
  7.5 0.7 %collective-permute-start.6 = (f32[4,64,256]{2,1,0:T(8,128)S(1)}, f32[4,64,256]{2,1,0:T(8,128)S(1)}, u32[]{:S(2)}, u32[]{:S(2)}) collective-permute-start(f32[4,64,256]{2,1,0:T(8,128)S(1)} %copy-done.3), channel_id=1, source_target_pairs={{1,2},{3,4},{5,6},{7,8},{9,10},{11,12},{13,14},{15,16},{17,18},{19... | collective-permute-start | bytes 786440 | tf_op jit(solution)/shard_map/ppermute | solution.py:825
  8.2 0.8 %shard_map.139 = (f32[4,64,256]{2,1,0:T(8,128)S(1)}, f32[8,256]{1,0:T(8,128)S(1)}) custom-call(f32[3,4,64,256]{3,2,1,0:T(8,128)S(1)} %copy-done), custom_call_target="tpu_custom_call" | custom-call | flops 1000000000 | tf_op jit(solution)/shard_map/pallas_call | solution.py:124
  9.0 0.0 copy-start.12
  9.1 0.6 shard_map.141
  9.6 2.9 %collective-permute-start.2 = (f32[512,128]{1,0:T(8,128)S(1)}, f32[512,128]{1,0:T(8,128)S(1)}, u32[]{:S(2)}, u32[]{:S(2)}) collective-permute-start(f32[512,128]{1,0:T(8,128)S(1)} %get-tuple-element.31.refs_0_), channel_id=1, source_target_pairs={{0,1},{1,0},{2,3},{3,2},{4,5},{5,4},{6,7},{7,6},{8,9},{9,8},{10,11... | collective-permute-start | bytes 786440 | tf_op jit(solution)/shard_map/ppermute | solution.py:821
  12.5 0.7 %collective-permute-start.3 = (f32[512,128]{1,0:T(8,128)S(1)}, f32[512,128]{1,0:T(8,128)S(1)}, u32[]{:S(2)}, u32[]{:S(2)}) collective-permute-start(f32[512,128]{1,0:T(8,128)S(1)} %get-tuple-element.31.refs_0_), channel_id=1, source_target_pairs={{1,2},{3,4},{5,6},{7,8},{9,10},{11,12},{13,14},{15,16},{17,18},{19... | collective-permute-start | bytes 786440 | tf_op jit(solution)/shard_map/ppermute | solution.py:825
  13.3 1.3 %collective-permute-start.4 = (f32[128,128]{1,0:T(8,128)S(1)}, f32[128,128]{1,0:T(8,128)S(1)}, u32[]{:S(2)}, u32[]{:S(2)}) collective-permute-start(f32[128,128]{1,0:T(8,128)S(1)} %get-tuple-element.32), channel_id=1, source_target_pairs={{2,0},{3,1},{4,2},{5,3},{6,4},{7,5},{8,6},{9,7},{10,8},{11,9},{12,... | collective-permute-start | bytes 196616 | tf_op jit(solution)/shard_map/ppermute | solution.py:860
  14.6 0.2 shard_map.142
  14.8 10.4 %collective-permute-done.4.refs_3_ = f32[128,128]{1,0:T(8,128)S(1)} collective-permute-done((f32[128,128]{1,0:T(8,128)S(1)}, f32[128,128]{1,0:T(8,128)S(1)}, u32[]{:S(2)}, u32[]{:S(2)}) %collective-permute-start.4) | collective-permute-done | bytes 65568 | tf_op jit(solution)/shard_map/ppermute | solution.py:860
  25.3 3.5 %shard_map.143 = (f32[32,8,128]{2,1,0:T(8,128)}, f32[5,4,64,256]{3,2,1,0:T(8,128)}) custom-call(f32[512,128]{1,0:T(8,128)S(1)} %get-tuple-element.31.refs_0_, f32[512,128]{1,0:T(8,128)S(1)} %collective-permute-done.2.refs_1_, f32[512,128]{1,0:T(8,128)S(1)} %collective-permute-done.3.refs_2_, f32[128,128]{1,0:T(8,128)S(1)} %collective-permute-done.4.refs_3_, ...), custom_call_target="tpu_custom_call" | custom-call | flops 1000000000 | tf_op jit(solution)/shard_map/pallas_call | solution.py:124
  28.7 5.5 %all-to-all-start = ((f32[32,8,128]{2,1,0:T(8,128)}), f32[32,8,128]{2,1,0:T(8,128)S(1)}, u32[]{:S(2)}, u32[]{:S(2)}) async-start(f32[32,8,128]{2,1,0:T(8,128)} %get-tuple-element.37), calls=%async_computation | async-start | bytes 262144 | tf_op jit(solution)/shard_map/all_to_all | solution.py:876
  34.2 0.3 collective-permute-start.7
  34.6 0.7 %collective-permute-start.8 = (f32[256,128]{1,0:T(8,128)S(1)}, f32[256,128]{1,0:T(8,128)S(1)}, u32[]{:S(2)}, u32[]{:S(2)}) collective-permute-start(f32[256,128]{1,0:T(8,128)S(1)} %get-tuple-element.42.refs_3_), channel_id=1, source_target_pairs={{1,2},{3,4},{5,6},{7,8},{9,10},{11,12},{13,14},{15,16},{17,18},{19... | collective-permute-start | bytes 393224 | tf_op jit(solution)/shard_map/ppermute | solution.py:825
  35.2 7.2 %all-to-all-done.refs_0_ = f32[32,8,128]{2,1,0:T(8,128)S(1)} async-done(((f32[32,8,128]{2,1,0:T(8,128)}), f32[32,8,128]{2,1,0:T(8,128)S(1)}, u32[]{:S(2)}, u32[]{:S(2)}) %all-to-all-start) | async-done | bytes 131104 | tf_op jit(solution)/shard_map/all_to_all | solution.py:876
  42.4 2.2 %shard_map.144 = (f32[3,24,1024]{2,1,0:T(8,128)S(1)}, s32[8,1024]{1,0:T(8,128)S(1)}, f32[24,1024]{1,0:T(8,128)S(1)}, f32[8,128]{1,0:T(8,128)S(1)}) custom-call(f32[32,8,128]{2,1,0:T(8,128)S(1)} %all-to-all-done.refs_0_, f32[3,8,1024]{2,1,0:T(8,128)S(1)} %copy-done.6, f32[3,8,1024]{2,1,0:T(8,128)S(1)} %copy-done.7, f32[4,3,8,1024]{3,2,1,0:T(8,128)S(1)} %copy-done.2), custom_call_target="tpu_custom_call" | custom-call | flops 1000000000 | tf_op jit(solution)/shard_map/pallas_call | solution.py:124
  44.7 4.7 %shard_map.146 = (f32[32,3,4,128]{3,2,1,0:T(4,128)}, f32[8,3,8,1024]{3,2,1,0:T(8,128)}) custom-call(f32[3,24,1024]{2,1,0:T(8,128)S(1)} %get-tuple-element.39.refs_0_, s32[8,1024]{1,0:T(8,128)S(1)} %get-tuple-element.40.refs_1_, f32[24,1024]{1,0:T(8,128)S(1)} %get-tuple-element.41.refs_2_, f32[256,128]{1,0:T(8,128)S(1)} %get-tuple-element.42.refs_3_, ...), custom_call_target="tpu_custom_call" | custom-call | flops 1000000000 | tf_op jit(solution)/shard_map/pallas_call | solution.py:124
  49.4 2.8 %all-to-all-start.1 = ((f32[32,3,4,128]{3,2,1,0:T(4,128)}), f32[32,3,4,128]{3,2,1,0:T(4,128)S(1)}, u32[]{:S(2)}, u32[]{:S(2)}) async-start(f32[32,3,4,128]{3,2,1,0:T(4,128)} %get-tuple-element.43), calls=%async_computation.1 | async-start | bytes 393216 | tf_op jit(solution)/shard_map/all_to_all | solution.py:901
  52.3 2.2 %shard_map.145 = f32[4,64,256]{2,1,0:T(8,128)} custom-call(f32[5,4,64,256]{3,2,1,0:T(8,128)} %get-tuple-element.36.refs_0_, f32[8,128]{1,0:T(8,128)S(1)} %get-tuple-element.38.refs_1_), custom_call_target="tpu_custom_call" | custom-call | flops 1000000000 | tf_op jit(solution)/shard_map/pallas_call | solution.py:124
  54.5 6.7 %all-to-all-done.1.refs_0_ = f32[32,3,4,128]{3,2,1,0:T(4,128)S(1)} async-done(((f32[32,3,4,128]{3,2,1,0:T(4,128)}), f32[32,3,4,128]{3,2,1,0:T(4,128)S(1)}, u32[]{:S(2)}, u32[]{:S(2)}) %all-to-all-start.1) | async-done | bytes 196640 | tf_op jit(solution)/shard_map/all_to_all | solution.py:901
  61.1 1.8 %shard_map.147 = (f32[3,8,1024]{2,1,0:T(8,128)}, f32[3,1024]{1,0:T(4,128)}) custom-call(f32[32,3,4,128]{3,2,1,0:T(4,128)S(1)} %all-to-all-done.1.refs_0_, f32[8,3,8,1024]{3,2,1,0:T(8,128)S(1)} %copy-done.10, f32[3,8,1024]{2,1,0:T(8,128)S(1)} %copy-done.6, f32[3,8,1024]{2,1,0:T(8,128)S(1)} %copy-done.7, f32[4,3,8,1024]{3,2,1,0:T(8,128)S(1)} %copy-done.2, ...), custom_call_target="tpu_custom_call" | custom-call | flops 1000000000 | tf_op jit(solution)/shard_map/pallas_call | solution.py:124
  (35 shorter events, 0.1 us)
Async XLA Ops:
  0.6 7.6 %copy-start = (f32[3,4,64,256]{3,2,1,0:T(8,128)S(1)}, f32[3,4,64,256]{3,2,1,0:T(8,128)}, u32[]{:S(2)}) copy-start(f32[3,4,64,256]{3,2,1,0:T(8,128)} %refs_0_.3) | copy-start | bytes 2359300
  0.6 2.9 %copy-start.3 = (f32[4,64,256]{2,1,0:T(8,128)S(1)}, f32[4,64,256]{2,1,0:T(8,128)}, u32[]{:S(2)}) copy-start(f32[4,64,256]{2,1,0:T(8,128)} %refs_4_.2) | copy-start | bytes 786436
  2.2 6.8 %collective-permute-start = (f32[288,128]{1,0:T(8,128)S(1)}, f32[288,128]{1,0:T(8,128)S(1)}, u32[]{:S(2)}, u32[]{:S(2)}) collective-permute-start(f32[288,128]{1,0:T(8,128)S(1)} %get-tuple-element.29), channel_id=1, source_target_pairs={{0,1},{1,0},{2,3},{3,2},{4,5},{5,4},{6,7},{7,6},{8,9},{9,8},{10,11... | collective-permute-start | bytes 442376 | tf_op jit(solution)/shard_map/ppermute | solution.py:821
  2.7 6.3 %copy-start.4 = (f32[3,8,1024]{2,1,0:T(8,128)S(1)}, f32[3,8,1024]{2,1,0:T(8,128)}, u32[]{:S(2)}) copy-start(f32[3,8,1024]{2,1,0:T(8,128)} %refs_7_.2) | copy-start | bytes 294916
  2.8 6.3 %copy-start.6 = (f32[3,8,1024]{2,1,0:T(8,128)S(1)}, f32[3,8,1024]{2,1,0:T(8,128)}, u32[]{:S(2)}) copy-start(f32[3,8,1024]{2,1,0:T(8,128)} %refs_2_.3) | copy-start | bytes 294916
  2.8 6.3 %copy-start.8 = (f32[8,1024]{1,0:T(8,128)S(1)}, f32[8,1024]{1,0:T(8,128)}, u32[]{:S(2)}) copy-start(f32[8,1024]{1,0:T(8,128)} %refs_8_.1) | copy-start | bytes 98308
  2.8 6.2 %collective-permute-start.1 = (f32[288,128]{1,0:T(8,128)S(1)}, f32[288,128]{1,0:T(8,128)S(1)}, u32[]{:S(2)}, u32[]{:S(2)}) collective-permute-start(f32[288,128]{1,0:T(8,128)S(1)} %get-tuple-element.30), channel_id=1, source_target_pairs={{1,2},{3,4},{5,6},{7,8},{9,10},{11,12},{13,14},{15,16},{17,18},{19... | collective-permute-start | bytes 442376 | tf_op jit(solution)/shard_map/ppermute | solution.py:825
  3.6 21.7 %collective-permute-start.5 = (f32[4,64,256]{2,1,0:T(8,128)S(1)}, f32[4,64,256]{2,1,0:T(8,128)S(1)}, u32[]{:S(2)}, u32[]{:S(2)}) collective-permute-start(f32[4,64,256]{2,1,0:T(8,128)S(1)} %copy-done.3), channel_id=1, source_target_pairs={{0,1},{1,0},{2,3},{3,2},{4,5},{5,4},{6,7},{7,6},{8,9},{9,8},{10,11... | collective-permute-start | bytes 786440 | tf_op jit(solution)/shard_map/ppermute | solution.py:821
  7.5 17.7 %collective-permute-start.6 = (f32[4,64,256]{2,1,0:T(8,128)S(1)}, f32[4,64,256]{2,1,0:T(8,128)S(1)}, u32[]{:S(2)}, u32[]{:S(2)}) collective-permute-start(f32[4,64,256]{2,1,0:T(8,128)S(1)} %copy-done.3), channel_id=1, source_target_pairs={{1,2},{3,4},{5,6},{7,8},{9,10},{11,12},{13,14},{15,16},{17,18},{19... | collective-permute-start | bytes 786440 | tf_op jit(solution)/shard_map/ppermute | solution.py:825
  9.0 4.2 %copy-start.11 = (s32[1024]{0:T(1024)S(1)}, s32[1024]{0:T(1024)}, u32[]{:S(2)}) copy-start(s32[1024]{0:T(1024)} %param.15) | copy-start | bytes 12292
  9.0 4.2 %copy-start.12 = (s32[1024]{0:T(1024)S(1)}, s32[1024]{0:T(1024)}, u32[]{:S(2)}) copy-start(s32[1024]{0:T(1024)} %param.16) | copy-start | bytes 12292
  9.1 5.5 %copy-start.9 = (s32[1024,1]{0,1:T(1,128)S(1)}, s32[1024,1]{0,1:T(1,128)}, u32[]{:S(2)}) copy-start(s32[1024,1]{0,1:T(1,128)} %param.14) | copy-start | bytes 12292
  9.6 15.6 %collective-permute-start.2 = (f32[512,128]{1,0:T(8,128)S(1)}, f32[512,128]{1,0:T(8,128)S(1)}, u32[]{:S(2)}, u32[]{:S(2)}) collective-permute-start(f32[512,128]{1,0:T(8,128)S(1)} %get-tuple-element.31.refs_0_), channel_id=1, source_target_pairs={{0,1},{1,0},{2,3},{3,2},{4,5},{5,4},{6,7},{7,6},{8,9},{9,8},{10,11... | collective-permute-start | bytes 786440 | tf_op jit(solution)/shard_map/ppermute | solution.py:821
  12.5 12.7 %collective-permute-start.3 = (f32[512,128]{1,0:T(8,128)S(1)}, f32[512,128]{1,0:T(8,128)S(1)}, u32[]{:S(2)}, u32[]{:S(2)}) collective-permute-start(f32[512,128]{1,0:T(8,128)S(1)} %get-tuple-element.31.refs_0_), channel_id=1, source_target_pairs={{1,2},{3,4},{5,6},{7,8},{9,10},{11,12},{13,14},{15,16},{17,18},{19... | collective-permute-start | bytes 786440 | tf_op jit(solution)/shard_map/ppermute | solution.py:825
  13.3 12.0 %collective-permute-start.4 = (f32[128,128]{1,0:T(8,128)S(1)}, f32[128,128]{1,0:T(8,128)S(1)}, u32[]{:S(2)}, u32[]{:S(2)}) collective-permute-start(f32[128,128]{1,0:T(8,128)S(1)} %get-tuple-element.32), channel_id=1, source_target_pairs={{2,0},{3,1},{4,2},{5,3},{6,4},{7,5},{8,6},{9,7},{10,8},{11,9},{12,... | collective-permute-start | bytes 196616 | tf_op jit(solution)/shard_map/ppermute | solution.py:860
  25.2 17.2 %copy-start.2 = (f32[4,3,8,1024]{3,2,1,0:T(8,128)S(1)}, f32[4,3,8,1024]{3,2,1,0:T(8,128)}, u32[]{:S(2)}) copy-start(f32[4,3,8,1024]{3,2,1,0:T(8,128)} %refs_4_.3) | copy-start | bytes 1179652
  25.3 17.2 %copy-start.7 = (f32[3,8,1024]{2,1,0:T(8,128)S(1)}, f32[3,8,1024]{2,1,0:T(8,128)}, u32[]{:S(2)}) copy-start(f32[3,8,1024]{2,1,0:T(8,128)} %refs_3_.3) | copy-start | bytes 294916
  28.7 13.7 %all-to-all-start = ((f32[32,8,128]{2,1,0:T(8,128)}), f32[32,8,128]{2,1,0:T(8,128)S(1)}, u32[]{:S(2)}, u32[]{:S(2)}) async-start(f32[32,8,128]{2,1,0:T(8,128)} %get-tuple-element.37), calls=%async_computation | async-start | bytes 262144 | tf_op jit(solution)/shard_map/all_to_all | solution.py:876
  34.2 10.5 %copy-start.1 = (f32[4,3,8,1024]{3,2,1,0:T(8,128)S(1)}, f32[4,3,8,1024]{3,2,1,0:T(8,128)}, u32[]{:S(2)}) copy-start(f32[4,3,8,1024]{3,2,1,0:T(8,128)} %refs_7_.3) | copy-start | bytes 1179652
  34.2 10.5 %copy-start.5 = (f32[3,8,1024]{2,1,0:T(8,128)S(1)}, f32[3,8,1024]{2,1,0:T(8,128)}, u32[]{:S(2)}) copy-start(f32[3,8,1024]{2,1,0:T(8,128)} %refs_6_.3) | copy-start | bytes 294916
  34.2 10.5 %collective-permute-start.7 = (f32[256,128]{1,0:T(8,128)S(1)}, f32[256,128]{1,0:T(8,128)S(1)}, u32[]{:S(2)}, u32[]{:S(2)}) collective-permute-start(f32[256,128]{1,0:T(8,128)S(1)} %get-tuple-element.42.refs_3_), channel_id=1, source_target_pairs={{0,1},{1,0},{2,3},{3,2},{4,5},{5,4},{6,7},{7,6},{8,9},{9,8},{10,11... | collective-permute-start | bytes 393224 | tf_op jit(solution)/shard_map/ppermute | solution.py:821
  34.6 10.1 %collective-permute-start.8 = (f32[256,128]{1,0:T(8,128)S(1)}, f32[256,128]{1,0:T(8,128)S(1)}, u32[]{:S(2)}, u32[]{:S(2)}) collective-permute-start(f32[256,128]{1,0:T(8,128)S(1)} %get-tuple-element.42.refs_3_), channel_id=1, source_target_pairs={{1,2},{3,4},{5,6},{7,8},{9,10},{11,12},{13,14},{15,16},{17,18},{19... | collective-permute-start | bytes 393224 | tf_op jit(solution)/shard_map/ppermute | solution.py:825
  49.4 11.7 %all-to-all-start.1 = ((f32[32,3,4,128]{3,2,1,0:T(4,128)}), f32[32,3,4,128]{3,2,1,0:T(4,128)S(1)}, u32[]{:S(2)}, u32[]{:S(2)}) async-start(f32[32,3,4,128]{3,2,1,0:T(4,128)} %get-tuple-element.43), calls=%async_computation.1 | async-start | bytes 393216 | tf_op jit(solution)/shard_map/all_to_all | solution.py:901
  52.3 8.9 %copy-start.10 = (f32[8,3,8,1024]{3,2,1,0:T(8,128)S(1)}, f32[8,3,8,1024]{3,2,1,0:T(8,128)}, u32[]{:S(2)}) copy-start(f32[8,3,8,1024]{3,2,1,0:T(8,128)} %get-tuple-element.44.refs_1_) | copy-start | bytes 2359300

commit v7 on v6

--- a/solution.py
+++ b/solution.py
@@ -17,6 +17,7 @@
 S_SHIFT = (5.7, 5.09, 4.26, 4.26, 4.08, 4.17, 4.1, 4.18)
 S_BACK = (2.53, 3.17, 4.07, 3.95, 4.22, 4.01, 4.14)
 TINY = 1e-7
+LEAST_SHARE = 0.01
 
 VMEM = pl.BlockSpec(memory_space=pltpu.VMEM)
 F32 = jnp.float32
@@ -515,12 +516,14 @@
 
 def eliminate(columns, right, first):
     row = at(right, 0)
+    share = jnp.ones((1, 1), F32)
     lengths = [TINY * column[first + k : first + k + 1] for k, column in enumerate(columns)]
     for k in range(len(columns)):
         column = columns[k]
         here = first + k
         pivot = column[here : here + 1]
         good = pivot > lengths[k]
+        share = jnp.minimum(share, jnp.where(good, pivot * TINY / jnp.where(good, lengths[k], 1.0), 0.0))
         inverse = jnp.where(good, 1.0 / jnp.where(good, pivot, 1.0), 0.0)
         factor = column * inverse
 
@@ -530,7 +533,7 @@
 
         columns = columns[: k + 1] + [reduced(values) for values in columns[k + 1 :]]
         right = reduced(right)
-    return right
+    return right, share
 
 
 def galerkin(gram, first, shifts, back, energy):
@@ -583,9 +586,10 @@
         summed = summed + received[p]
     gram = [column_of(summed, 96 + k) for k in range(PITERS + 1)]
     system = galerkin(gram[:PITERS], 3, P_SHIFT, P_BACK, gram[PITERS][7:8])
-    solved = eliminate(system, gram[0], 3)
+    solved, share = eliminate(system, gram[0], 3)
     solved = jnp.where(lax.broadcasted_iota(jnp.int32, (8, 1), 0) >= 3, solved, 0.0)
-    factors[...] = jnp.broadcast_to(solved, (8, 128))
+    first_row = lax.broadcasted_iota(jnp.int32, (8, 1), 0) == 0
+    factors[...] = jnp.broadcast_to(jnp.where(first_row, share, solved), (8, 128))
     groups = [lane8 // 32 == q for q in range(4)]
 
     def gathered(j):
@@ -622,10 +626,10 @@
             [jnp.where(match, piece[c : c + 1], 0.0) for piece in pieces for c in range(3)], 0
         )
         scattered = added(dot(left_rows.astype(BF16), spot, True), 2)
-        share = dot(jnp.where(match, weights[j : j + 1, :], 0.0).astype(BF16), spot, True)
-        share = 1.0 / jnp.maximum(share, 1.0)
+        total_weight = dot(jnp.where(match, weights[j : j + 1, :], 0.0).astype(BF16), spot, True)
+        inverse = 1.0 / jnp.maximum(total_weight, 1.0)
         for c in range(3):
-            force = scattered[c * 64 : c * 64 + 64] * share
+            force = scattered[c * 64 : c * 64 + 64] * inverse
             for k in range(8):
                 forces[c, j * 8 : j * 8 + 8, k * 128 : k * 128 + 128] = force[k * 8 : k * 8 + 8]
     requests[...] = jnp.broadcast_to(node, (8, entries))
@@ -734,8 +738,8 @@
 
 
 def update_kernel(
-    received, basis, displacement, solved_prev, solved_history, owner, slots,
-    new_displacement, wall, *, ranks,
+    received, basis, displacement, solved_prev, solved_history, owner, slots, pressure_factors,
+    new_displacement, wall, shares, *, ranks,
 ):
     summed = [sum(received[p, t] for p in range(ranks)) for t in range(3)]
     summed = jnp.concatenate(summed + [jnp.zeros((4, 128), F32)], 0)
@@ -743,7 +747,7 @@
     gram = [column_of(matrix, k) for k in range(SITERS + 5)]
     energy = summed[ENERGY_AT[0] : ENERGY_AT[0] + 1, ENERGY_AT[1] : ENERGY_AT[1] + 1]
     system = galerkin(gram[:SITERS], 0, S_SHIFT, S_BACK, energy)
-    steps = eliminate(system, gram[0], 0)
+    steps, share = eliminate(system, gram[0], 0)
     down = lax.broadcasted_iota(jnp.int32, (16, 1), 0)
     steps = jnp.where(down < SITERS, steps, 0.0)
     base, count = SITERS, 1 + solved_history.shape[0]
@@ -759,7 +763,12 @@
     for k in range(1, count):
         columns.append(jnp.where(down == base, with_newest[base + k : base + k + 1], gram[base + k]))
     right = jnp.where(down == base, newest_moved, with_moved)
-    coefficients = -eliminate(columns, right, base)
+    coefficients, newest_share = eliminate(columns, right, base)
+    coefficients = -coefficients
+    together = newest_moved + with_newest[base : base + 1] + 2.0 * gram[base][base : base + 1]
+    kept = newest_newest / jnp.maximum(together, 1e-30)
+    share = jnp.minimum(jnp.minimum(share, newest_share), jnp.minimum(kept, pressure_factors[0:1, 0:1]))
+    shares[...] = jnp.broadcast_to(share, (8, 128))
     newest = row_of(coefficients, base)
     factors = jnp.where(
         down < base,
@@ -799,6 +808,183 @@
             )
 
 
+def with_halo(cells, sides, width):
+    for axis, dim in sides:
+        count = lax.axis_size(axis)
+        ends = count - 1
+        head = lax.slice_in_dim(cells, 0, width, axis=dim)
+        tail = lax.slice_in_dim(cells, cells.shape[dim] - width, cells.shape[dim], axis=dim)
+        cells = jnp.concatenate(
+            [
+                lax.ppermute(tail, axis, [(i, (i + 1) % count) for i in range(ends)]),
+                cells,
+                lax.ppermute(head, axis, [((i + 1) % count, i) for i in range(ends)]),
+            ],
+            axis=dim,
+        )
+    return cells
+
+
+def both_ways(core, axis):
+    length = core.shape[axis]
+    zero_slab = jnp.zeros_like(lax.slice_in_dim(core, 0, 1, axis=axis))
+    ahead = jnp.concatenate([lax.slice_in_dim(core, 1, length, axis=axis), zero_slab], axis)
+    behind = jnp.concatenate([zero_slab, lax.slice_in_dim(core, 0, length - 1, axis=axis)], axis)
+    return (ahead, behind)
+
+
+def grid_plane_sum(core):
+    ahead_y, behind_y = both_ways(core, core.ndim - 2)
+    ahead_z, behind_z = both_ways(core, core.ndim - 1)
+    return ahead_y + behind_y + ahead_z + behind_z
+
+
+def pressure_apply(field, shift):
+    extended = with_halo(field, (("slab", 0),), 1)
+    beside = extended[2:] + extended[:-2] + grid_plane_sum(field)
+    return (6.0 + shift) * field - beside
+
+
+def pressure_total(value):
+    return lax.psum(value, "slab")
+
+
+def grid_shell_apply(field, stiffness):
+    extended = with_halo(field, (("slab", 1),), 1)
+    ahead_c, behind_c = both_ways(field, 2)
+    beside = extended[:, 2:] + extended[:, :-2] + ahead_c + behind_c
+    return (4.0 + stiffness) * field - beside
+
+
+def shell_total(value):
+    return lax.psum(value, "slab")
+
+
+def small_solve(gram, target):
+    factor = jnp.linalg.cholesky(gram)
+    gram_size = gram.shape[0]
+    forward = []
+    for across in range(gram_size):
+        partial_sum = target[across] - sum(
+            (factor[across, within] * forward[within] for within in range(across))
+        )
+        forward.append(partial_sum / factor[across, across])
+    backward = [None] * gram_size
+    for across in reversed(range(gram_size)):
+        partial_sum = forward[across] - sum(
+            (factor[within, across] * backward[within] for within in range(across + 1, gram_size))
+        )
+        backward[across] = partial_sum / factor[across, across]
+    return jnp.stack(backward)
+
+
+def step_by_step(
+    velocity,
+    pressure_shift,
+    owner_rank,
+    node_index,
+    map_weight,
+    shell_load,
+    shell_stiffness,
+    displacement,
+    residual_prev,
+    solved_prev,
+    residual_history,
+    solved_history,
+):
+    slab_count = lax.axis_size("slab")
+    kept = residual_history.shape[0]
+    shell_rows = displacement.shape[1]
+    shell_cols = displacement.shape[2]
+    node_count = shell_rows * shell_cols
+    extended = with_halo(velocity, (("slab", 1),), 1)
+    predicted = velocity + NU * (
+        extended[:, 2:] + extended[:, :-2] + grid_plane_sum(velocity) - 6.0 * velocity
+    )
+    along_first = with_halo(predicted[0], (("slab", 0),), 1)
+    ahead_y, behind_y = both_ways(predicted[1], 1)
+    ahead_z, behind_z = both_ways(predicted[2], 2)
+    spread = along_first[2:] - along_first[:-2] + ahead_y - behind_y + ahead_z - behind_z
+    source = -0.5 * spread
+    pressure = jnp.zeros_like(source)
+    residual = source
+    direction = source
+    norm_now = pressure_total(jnp.sum(residual * residual))
+    for sweep in range(PITERS):
+        image = pressure_apply(direction, pressure_shift)
+        step_size = norm_now / lax.psum(jnp.sum(direction * image), "slab")
+        pressure = pressure + step_size * direction
+        residual = residual - step_size * image
+        norm_next = pressure_total(jnp.sum(residual * residual))
+        direction = residual + norm_next / norm_now * direction
+        norm_now = norm_next
+    traction = jnp.stack(
+        [
+            MU * (predicted[0, :, 1, :] - predicted[0, :, 0, :]),
+            WALL * pressure[:, 0, :],
+            MU * (predicted[2, :, 1, :] - predicted[2, :, 0, :]),
+        ]
+    ).reshape(3, -1)
+    owners = owner_rank[:, 0]
+    ranks = jnp.arange(slab_count, dtype=jnp.int32)
+    member = (owners[:, None] == ranks[None, :]).astype(jnp.int32)
+    slots = jnp.sum((jnp.cumsum(member, 0) - 1) * member, 1)
+    scaled = map_weight.astype(jnp.float32)
+    packed = jnp.concatenate([traction * scaled[None, :], scaled[None, :]], 0).T
+    send_values = (
+        jnp.zeros((slab_count, 4, CAP), jnp.float32)
+        .at[owners, :, slots]
+        .set(packed)
+        .reshape(slab_count, 4 * CAP)
+    )
+    send_nodes = (
+        jnp.full((slab_count, CAP), node_count, jnp.int32).at[owners, slots].set(node_index)
+    )
+    got_values, got_nodes = (
+        lax.all_to_all(send_values, "slab", split_axis=0, concat_axis=0, tiled=True),
+        lax.all_to_all(send_nodes, "slab", split_axis=0, concat_axis=0, tiled=True),
+    )
+    flat_values = got_values.reshape(slab_count, 4, CAP).transpose(0, 2, 1).reshape(-1, 4)
+    totals = jax.ops.segment_sum(flat_values, got_nodes.reshape(-1), num_segments=node_count + 1)[
+        :node_count
+    ]
+    force = (totals[:, :3] / jnp.maximum(totals[:, 3], 1.0)[:, None]).T.reshape(
+        3, shell_rows, shell_cols
+    )
+    shell_source = force + shell_load
+    solved = displacement
+    residual = shell_source - grid_shell_apply(solved, shell_stiffness)
+    direction = residual
+    norm_now = shell_total(jnp.sum(residual * residual))
+    for sweep in range(SITERS):
+        image = grid_shell_apply(direction, shell_stiffness)
+        step_size = norm_now / lax.psum(jnp.sum(direction * image), "slab")
+        solved = solved + step_size * direction
+        residual = residual - step_size * image
+        norm_next = shell_total(jnp.sum(residual * residual))
+        direction = residual + norm_next / norm_now * direction
+        norm_now = norm_next
+    moved = solved - displacement
+    newest_v = moved - residual_prev
+    newest_w = solved - solved_prev
+    columns = jnp.concatenate([newest_v[None], residual_history], 0).reshape(kept + 1, -1)
+    outputs_w = jnp.concatenate([newest_w[None], solved_history], 0)
+    moved_flat = moved.reshape(-1)
+    gram_local = jnp.dot(columns, columns.T, precision=lax.Precision.HIGHEST)
+    target_local = jnp.dot(columns, moved_flat, precision=lax.Precision.HIGHEST)
+    gram, target = lax.psum((gram_local, target_local), "slab")
+    coefficients = -small_solve(gram, target)
+    new_displacement = solved + jnp.einsum(
+        "k,kabc->abc", coefficients, outputs_w, precision=lax.Precision.HIGHEST
+    )
+    shell_flat = new_displacement.reshape(3, node_count)
+    requested = jnp.minimum(got_nodes, node_count - 1)
+    answers = shell_flat[:, requested].transpose(1, 0, 2)
+    returned = lax.all_to_all(answers, "slab", split_axis=0, concat_axis=0, tiled=True)
+    wall_displacement = returned[owners, :, slots].T
+    return (pressure, new_displacement, wall_displacement)
+
+
 def on_device(
     velocity,
     pressure_shift,
@@ -906,12 +1092,19 @@
         late=(0,),
         stored=(0,),
     )
-    new_displacement, wall_displacement = call(
+    new_displacement, wall_displacement, shares = call(
         lambda *refs: update_kernel(*refs, ranks=ranks),
-        (shape(*displacement.shape), shape(3, owner_rank.shape[0])),
-        (answers, shell_basis, displacement, solved_prev, solved_history, owner, slots),
-    )
-    return (pressure, new_displacement, wall_displacement)
+        (shape(*displacement.shape), shape(3, owner_rank.shape[0]), shape(8, 128)),
+        (answers, shell_basis, displacement, solved_prev, solved_history, owner, slots, factors),
+    )
+    return lax.cond(
+        shares[0, 0] > LEAST_SHARE,
+        lambda: (pressure, new_displacement, wall_displacement),
+        lambda: step_by_step(
+            velocity, pressure_shift, owner_rank, node_index, map_weight, shell_load, shell_stiffness,
+            displacement, residual_prev, solved_prev, residual_history, solved_history,
+        ),
+    )
 
 
 def solution(mesh):

time: 63.5 us -> 66.6 us (1.049)
  local copies, waits for them, and re-layouts: 0.09 us -> 1.82 us
  Pallas kernels: 17.5 us -> 18.7 us
  between operations: 0.96 us -> 1.88 us
  waiting for transfers between devices: 24.3 us -> 23.4 us
    pallas_call x9, Pallas kernels: 17.5 us -> 18.7 us  [call(): pl.pallas_call(body, out_shape=outs, in_specs=[any_space if i in outside...]
    unnamed x26 -> x28, local copies, waits for them, and re-layouts: 0.07 us -> 1.21 us
    ppermute x1, waiting for transfers between devices: 10.4 us -> 9.37 us  [on_device(): beyond = lax.ppermute(first, 'slab', [(i, i - 2) for i in range(2, ranks)])]
  transfers between devices with their start and end apart: 11 -> 11, of which waited for: 3 -> 3; matrix products, arithmetic and copies ran while one was open for 0% -> 0% of each run, Pallas kernels for 10% -> 11%
where the time goes in v7:
time: 66.6 us; the launch traced here: 65.9 us
  waiting for transfers between devices  23.4 us (35%)
  starting transfers between devices  19.9 us (30%)
  Pallas kernels  18.7 us (28%)
  between operations  1.88 us (3%)
  local copies, waits for them, and re-layouts  1.82 us (3%)
    pallas_call x9, Pallas kernels, call(): pl.pallas_call(body, out_shape=outs, in_specs=[any_space if i in outside...  18.7 us
    all_to_all x2, waiting for transfers between devices, on_device(): lax.all_to_all(payload, 'slab', split_axis=0, concat_axis=0, tiled=True)  14 us
    ppermute x1, waiting for transfers between devices, on_device(): beyond = lax.ppermute(first, 'slab', [(i, i - 2) for i in range(2, ranks)])  9.37 us
    all_to_all x2, starting transfers between devices, on_device(): lax.all_to_all(payload, 'slab', split_axis=0, concat_axis=0, tiled=True)  8.3 us
    ppermute x4, starting transfers between devices, with_mate(): return lax.ppermute(values, 'slab', [(i, i ^ 1) for i in range(ranks)])  7.67 us
    ppermute x4, starting transfers between devices, with_other(): return lax.ppermute(values, 'slab', pairs + [(j, i) for i, j in pairs])  2.65 us
  transfers between devices with their start and end apart: 11, of which 3 were waited for; matrix products, arithmetic and copies ran while one was open for 0% of the time, Pallas kernels for 11%

profile of v7, /device:TPU:0, one launch (start us, length us, event | category | flops | bytes accessed | tf_op | source)
XLA Modules:
  0.0 65.9 jit_solution(8989664357302527836)
XLA Ops:
  0.7 1.5 %shard_map.146 = (f32[288,128]{1,0:T(8,128)S(1)}, f32[288,128]{1,0:T(8,128)S(1)}, f32[64,256]{1,0:T(8,128)S(1)}, f32[64,256]{1,0:T(8,128)S(1)}) custom-call(f32[3,4,64,256]{3,2,1,0:T(8,128)} %refs_0_.3, f32[3,8,1024]{2,1,0:T(8,128)} %refs_2_.3), custom_call_target="tpu_custom_call" | custom-call | flops 1000000000 | tf_op jit(solution)/shard_map/pallas_call | solution.py:125
  2.2 0.5 collective-permute-start.32
  2.8 0.7 collective-permute-start.33
  3.4 3.9 %collective-permute-start.37 = (f32[4,64,256]{2,1,0:T(8,128)}, f32[4,64,256]{2,1,0:T(8,128)S(1)}, u32[]{:S(2)}, u32[]{:S(2)}) collective-permute-start(f32[4,64,256]{2,1,0:T(8,128)} %refs_4_.2), channel_id=1, source_target_pairs={{0,1},{1,0},{2,3},{3,2},{4,5},{5,4},{6,7},{7,6},{8,9},{9,8},{10,11... | collective-permute-start | bytes 786440 | tf_op jit(solution)/shard_map/ppermute | solution.py:1007
  7.4 0.7 %collective-permute-start.38 = (f32[4,64,256]{2,1,0:T(8,128)}, f32[4,64,256]{2,1,0:T(8,128)S(1)}, u32[]{:S(2)}, u32[]{:S(2)}) collective-permute-start(f32[4,64,256]{2,1,0:T(8,128)} %refs_4_.2), channel_id=1, source_target_pairs={{1,2},{3,4},{5,6},{7,8},{9,10},{11,12},{13,14},{15,16},{17,18},{19... | collective-permute-start | bytes 786440 | tf_op jit(solution)/shard_map/ppermute | solution.py:1011
  8.0 1.9 %shard_map.145 = (f32[4,64,256]{2,1,0:T(8,128)S(1)}, f32[8,256]{1,0:T(8,128)S(1)}) custom-call(f32[3,4,64,256]{3,2,1,0:T(8,128)} %refs_0_.3), custom_call_target="tpu_custom_call" | custom-call | flops 1000000000 | tf_op jit(solution)/shard_map/pallas_call | solution.py:125
  10.0 0.6 shard_map.147
  10.6 2.9 %collective-permute-start.34 = (f32[512,128]{1,0:T(8,128)S(1)}, f32[512,128]{1,0:T(8,128)S(1)}, u32[]{:S(2)}, u32[]{:S(2)}) collective-permute-start(f32[512,128]{1,0:T(8,128)S(1)} %get-tuple-element.74.refs_0_), channel_id=1, source_target_pairs={{0,1},{1,0},{2,3},{3,2},{4,5},{5,4},{6,7},{7,6},{8,9},{9,8},{10,11... | collective-permute-start | bytes 786440 | tf_op jit(solution)/shard_map/ppermute | solution.py:1007
  13.5 0.7 %collective-permute-start.35 = (f32[512,128]{1,0:T(8,128)S(1)}, f32[512,128]{1,0:T(8,128)S(1)}, u32[]{:S(2)}, u32[]{:S(2)}) collective-permute-start(f32[512,128]{1,0:T(8,128)S(1)} %get-tuple-element.74.refs_0_), channel_id=1, source_target_pairs={{1,2},{3,4},{5,6},{7,8},{9,10},{11,12},{13,14},{15,16},{17,18},{19... | collective-permute-start | bytes 786440 | tf_op jit(solution)/shard_map/ppermute | solution.py:1011
  14.2 1.3 %collective-permute-start.36 = (f32[128,128]{1,0:T(8,128)S(1)}, f32[128,128]{1,0:T(8,128)S(1)}, u32[]{:S(2)}, u32[]{:S(2)}) collective-permute-start(f32[128,128]{1,0:T(8,128)S(1)} %get-tuple-element.75), channel_id=1, source_target_pairs={{2,0},{3,1},{4,2},{5,3},{6,4},{7,5},{8,6},{9,7},{10,8},{11,9},{12,... | collective-permute-start | bytes 196616 | tf_op jit(solution)/shard_map/ppermute | solution.py:1046
  15.8 9.4 %collective-permute-done.36.refs_3_ = f32[128,128]{1,0:T(8,128)S(1)} collective-permute-done((f32[128,128]{1,0:T(8,128)S(1)}, f32[128,128]{1,0:T(8,128)S(1)}, u32[]{:S(2)}, u32[]{:S(2)}) %collective-permute-start.36) | collective-permute-done | bytes 65568 | tf_op jit(solution)/shard_map/ppermute | solution.py:1046
  25.2 3.5 %shard_map.149 = (f32[32,8,128]{2,1,0:T(8,128)}, f32[5,4,64,256]{3,2,1,0:T(8,128)}) custom-call(f32[512,128]{1,0:T(8,128)S(1)} %get-tuple-element.74.refs_0_, f32[512,128]{1,0:T(8,128)S(1)} %collective-permute-done.34.refs_1_, f32[512,128]{1,0:T(8,128)S(1)} %collective-permute-done.35.refs_2_, f32[128,128]{1,0:T(8,128)S(1)} %collective-permute-done.36.refs_3_, ...), custom_call_target="tpu_custom_call" | custom-call | flops 1000000000 | tf_op jit(solution)/shard_map/pallas_call | solution.py:125
  28.7 5.5 %all-to-all-start.3 = ((f32[32,8,128]{2,1,0:T(8,128)}), f32[32,8,128]{2,1,0:T(8,128)S(1)}, u32[]{:S(2)}, u32[]{:S(2)}) async-start(f32[32,8,128]{2,1,0:T(8,128)} %get-tuple-element.79), calls=%async_computation.3 | async-start | bytes 262144 | tf_op jit(solution)/shard_map/all_to_all | solution.py:1062
  34.2 0.3 collective-permute-start.39
  34.5 0.7 collective-permute-start.40
  35.2 7.2 %all-to-all-done.3.refs_0_ = f32[32,8,128]{2,1,0:T(8,128)S(1)} async-done(((f32[32,8,128]{2,1,0:T(8,128)}), f32[32,8,128]{2,1,0:T(8,128)S(1)}, u32[]{:S(2)}, u32[]{:S(2)}) %all-to-all-start.3) | async-done | bytes 131104 | tf_op jit(solution)/shard_map/all_to_all | solution.py:1062
  42.5 2.2 %shard_map.150 = (f32[3,24,1024]{2,1,0:T(8,128)S(1)}, s32[8,1024]{1,0:T(8,128)S(1)}, f32[24,1024]{1,0:T(8,128)S(1)}, f32[8,128]{1,0:T(8,128)S(1)}) custom-call(f32[32,8,128]{2,1,0:T(8,128)S(1)} %all-to-all-done.3.refs_0_, f32[3,8,1024]{2,1,0:T(8,128)S(1)} %copy-done.3, f32[3,8,1024]{2,1,0:T(8,128)S(1)} %copy-done.13, f32[4,3,8,1024]{3,2,1,0:T(8,128)S(1)} %copy-done.7), custom_call_target="tpu_custom_call" | custom-call | flops 1000000000 | tf_op jit(solution)/shard_map/pallas_call | solution.py:125
  44.7 4.8 %shard_map.151 = (f32[32,3,4,128]{3,2,1,0:T(4,128)}, f32[8,3,8,1024]{3,2,1,0:T(8,128)}) custom-call(f32[3,24,1024]{2,1,0:T(8,128)S(1)} %get-tuple-element.80.refs_0_, s32[8,1024]{1,0:T(8,128)S(1)} %get-tuple-element.81.refs_1_, f32[24,1024]{1,0:T(8,128)S(1)} %get-tuple-element.82.refs_2_, f32[256,128]{1,0:T(8,128)S(1)} %get-tuple-element.83.refs_3_, ...), custom_call_target="tpu_custom_call" | custom-call | flops 1000000000 | tf_op jit(solution)/shard_map/pallas_call | solution.py:125
  49.6 2.8 %all-to-all-start.4 = ((f32[32,3,4,128]{3,2,1,0:T(4,128)}), f32[32,3,4,128]{3,2,1,0:T(4,128)S(1)}, u32[]{:S(2)}, u32[]{:S(2)}) async-start(f32[32,3,4,128]{3,2,1,0:T(4,128)} %get-tuple-element.84), calls=%async_computation.4 | async-start | bytes 393216 | tf_op jit(solution)/shard_map/all_to_all | solution.py:1087
  52.4 2.1 %shard_map.153 = f32[4,64,256]{2,1,0:T(8,128)} custom-call(f32[5,4,64,256]{3,2,1,0:T(8,128)} %get-tuple-element.88.refs_0_, f32[8,128]{1,0:T(8,128)S(1)} %get-tuple-element.86.refs_7_.refs_1_), custom_call_target="tpu_custom_call" | custom-call | flops 1000000000 | tf_op jit(solution)/shard_map/pallas_call | solution.py:125
  54.5 6.7 %all-to-all-done.4.refs_0_ = f32[32,3,4,128]{3,2,1,0:T(4,128)S(1)} async-done(((f32[32,3,4,128]{3,2,1,0:T(4,128)}), f32[32,3,4,128]{3,2,1,0:T(4,128)S(1)}, u32[]{:S(2)}, u32[]{:S(2)}) %all-to-all-start.4) | async-done | bytes 196640 | tf_op jit(solution)/shard_map/all_to_all | solution.py:1087
  61.3 1.1 %copy-done = f32[8,3,8,1024]{3,2,1,0:T(8,128)S(1)} copy-done((f32[8,3,8,1024]{3,2,1,0:T(8,128)S(1)}, f32[8,3,8,1024]{3,2,1,0:T(8,128)}, u32[]{:S(2)}) %copy-start) | copy-done | bytes 786456
  62.4 1.8 %shard_map.152 = (f32[3,8,1024]{2,1,0:T(8,128)}, f32[3,1024]{1,0:T(4,128)}, f32[8,128]{1,0:T(8,128)S(1)}) custom-call(f32[32,3,4,128]{3,2,1,0:T(4,128)S(1)} %all-to-all-done.4.refs_0_, f32[8,3,8,1024]{3,2,1,0:T(8,128)S(1)} %copy-done, f32[3,8,1024]{2,1,0:T(8,128)S(1)} %copy-done.3, f32[3,8,1024]{2,1,0:T(8,128)S(1)} %copy-done.13, ...), custom_call_target="tpu_custom_call" | custom-call | flops 1000000000 | tf_op jit(solution)/shard_map/pallas_call | solution.py:125
  64.2 0.6 slice.493
  (39 shorter events, 0.6 us)
Async XLA Ops:
  0.6 9.3 %copy-start.3 = (f32[3,8,1024]{2,1,0:T(8,128)S(1)}, f32[3,8,1024]{2,1,0:T(8,128)}, u32[]{:S(2)}) copy-start(f32[3,8,1024]{2,1,0:T(8,128)} %refs_2_.3) | copy-start | bytes 294916
  0.6 9.3 %copy-start.11 = (f32[3,8,1024]{2,1,0:T(8,128)S(1)}, f32[3,8,1024]{2,1,0:T(8,128)}, u32[]{:S(2)}) copy-start(f32[3,8,1024]{2,1,0:T(8,128)} %refs_7_.2) | copy-start | bytes 294916
  0.7 9.3 %copy-start.21 = (f32[8,1024]{1,0:T(8,128)S(1)}, f32[8,1024]{1,0:T(8,128)}, u32[]{:S(2)}) copy-start(f32[8,1024]{1,0:T(8,128)} %refs_8_.1) | copy-start | bytes 98308
  2.2 11.9 %copy-start.24 = (s32[1024]{0:T(1024)S(1)}, s32[1024]{0:T(1024)}, u32[]{:S(2)}) copy-start(s32[1024]{0:T(1024)} %param.17) | copy-start | bytes 12292
  2.2 11.9 %copy-start.23 = (s32[1024]{0:T(1024)S(1)}, s32[1024]{0:T(1024)}, u32[]{:S(2)}) copy-start(s32[1024]{0:T(1024)} %param.18) | copy-start | bytes 12292
  2.2 13.3 %copy-start.20 = (s32[1024,1]{0,1:T(1,128)S(1)}, s32[1024,1]{0,1:T(1,128)}, u32[]{:S(2)}) copy-start(s32[1024,1]{0,1:T(1,128)} %param.16) | copy-start | bytes 12292
  2.2 7.7 %collective-permute-start.32 = (f32[288,128]{1,0:T(8,128)S(1)}, f32[288,128]{1,0:T(8,128)S(1)}, u32[]{:S(2)}, u32[]{:S(2)}) collective-permute-start(f32[288,128]{1,0:T(8,128)S(1)} %get-tuple-element.72), channel_id=1, source_target_pairs={{0,1},{1,0},{2,3},{3,2},{4,5},{5,4},{6,7},{7,6},{8,9},{9,8},{10,11... | collective-permute-start | bytes 442376 | tf_op jit(solution)/shard_map/ppermute | solution.py:1007
  2.8 7.2 %collective-permute-start.33 = (f32[288,128]{1,0:T(8,128)S(1)}, f32[288,128]{1,0:T(8,128)S(1)}, u32[]{:S(2)}, u32[]{:S(2)}) collective-permute-start(f32[288,128]{1,0:T(8,128)S(1)} %get-tuple-element.73), channel_id=1, source_target_pairs={{1,2},{3,4},{5,6},{7,8},{9,10},{11,12},{13,14},{15,16},{17,18},{19... | collective-permute-start | bytes 442376 | tf_op jit(solution)/shard_map/ppermute | solution.py:1011
  3.4 21.7 %collective-permute-start.37 = (f32[4,64,256]{2,1,0:T(8,128)}, f32[4,64,256]{2,1,0:T(8,128)S(1)}, u32[]{:S(2)}, u32[]{:S(2)}) collective-permute-start(f32[4,64,256]{2,1,0:T(8,128)} %refs_4_.2), channel_id=1, source_target_pairs={{0,1},{1,0},{2,3},{3,2},{4,5},{5,4},{6,7},{7,6},{8,9},{9,8},{10,11... | collective-permute-start | bytes 786440 | tf_op jit(solution)/shard_map/ppermute | solution.py:1007
  7.4 17.8 %collective-permute-start.38 = (f32[4,64,256]{2,1,0:T(8,128)}, f32[4,64,256]{2,1,0:T(8,128)S(1)}, u32[]{:S(2)}, u32[]{:S(2)}) collective-permute-start(f32[4,64,256]{2,1,0:T(8,128)} %refs_4_.2), channel_id=1, source_target_pairs={{1,2},{3,4},{5,6},{7,8},{9,10},{11,12},{13,14},{15,16},{17,18},{19... | collective-permute-start | bytes 786440 | tf_op jit(solution)/shard_map/ppermute | solution.py:1011
  9.9 15.3 %copy-start.2 = (f32[4,64,256]{2,1,0:T(8,128)S(1)}, f32[4,64,256]{2,1,0:T(8,128)}, u32[]{:S(2)}) copy-start(f32[4,64,256]{2,1,0:T(8,128)} %refs_4_.2) | copy-start | bytes 786436
  10.5 31.9 %copy-start.7 = (f32[4,3,8,1024]{3,2,1,0:T(8,128)S(1)}, f32[4,3,8,1024]{3,2,1,0:T(8,128)}, u32[]{:S(2)}) copy-start(f32[4,3,8,1024]{3,2,1,0:T(8,128)} %refs_4_.3) | copy-start | bytes 1179652
  10.6 31.9 %copy-start.13 = (f32[3,8,1024]{2,1,0:T(8,128)S(1)}, f32[3,8,1024]{2,1,0:T(8,128)}, u32[]{:S(2)}) copy-start(f32[3,8,1024]{2,1,0:T(8,128)} %refs_3_.3) | copy-start | bytes 294916
  10.6 14.6 %collective-permute-start.34 = (f32[512,128]{1,0:T(8,128)S(1)}, f32[512,128]{1,0:T(8,128)S(1)}, u32[]{:S(2)}, u32[]{:S(2)}) collective-permute-start(f32[512,128]{1,0:T(8,128)S(1)} %get-tuple-element.74.refs_0_), channel_id=1, source_target_pairs={{0,1},{1,0},{2,3},{3,2},{4,5},{5,4},{6,7},{7,6},{8,9},{9,8},{10,11... | collective-permute-start | bytes 786440 | tf_op jit(solution)/shard_map/ppermute | solution.py:1007
  13.5 11.7 %collective-permute-start.35 = (f32[512,128]{1,0:T(8,128)S(1)}, f32[512,128]{1,0:T(8,128)S(1)}, u32[]{:S(2)}, u32[]{:S(2)}) collective-permute-start(f32[512,128]{1,0:T(8,128)S(1)} %get-tuple-element.74.refs_0_), channel_id=1, source_target_pairs={{1,2},{3,4},{5,6},{7,8},{9,10},{11,12},{13,14},{15,16},{17,18},{19... | collective-permute-start | bytes 786440 | tf_op jit(solution)/shard_map/ppermute | solution.py:1011
  14.2 10.9 %collective-permute-start.36 = (f32[128,128]{1,0:T(8,128)S(1)}, f32[128,128]{1,0:T(8,128)S(1)}, u32[]{:S(2)}, u32[]{:S(2)}) collective-permute-start(f32[128,128]{1,0:T(8,128)S(1)} %get-tuple-element.75), channel_id=1, source_target_pairs={{2,0},{3,1},{4,2},{5,3},{6,4},{7,5},{8,6},{9,7},{10,8},{11,9},{12,... | collective-permute-start | bytes 196616 | tf_op jit(solution)/shard_map/ppermute | solution.py:1046
  15.7 29.0 %copy-start.5 = (f32[4,3,8,1024]{3,2,1,0:T(8,128)S(1)}, f32[4,3,8,1024]{3,2,1,0:T(8,128)}, u32[]{:S(2)}) copy-start(f32[4,3,8,1024]{3,2,1,0:T(8,128)} %refs_7_.3) | copy-start | bytes 1179652
  15.8 29.0 %copy-start.16 = (f32[3,8,1024]{2,1,0:T(8,128)S(1)}, f32[3,8,1024]{2,1,0:T(8,128)}, u32[]{:S(2)}) copy-start(f32[3,8,1024]{2,1,0:T(8,128)} %refs_6_.3) | copy-start | bytes 294916
  28.7 13.7 %all-to-all-start.3 = ((f32[32,8,128]{2,1,0:T(8,128)}), f32[32,8,128]{2,1,0:T(8,128)S(1)}, u32[]{:S(2)}, u32[]{:S(2)}) async-start(f32[32,8,128]{2,1,0:T(8,128)} %get-tuple-element.79), calls=%async_computation.3 | async-start | bytes 262144 | tf_op jit(solution)/shard_map/all_to_all | solution.py:1062
  34.2 10.5 %collective-permute-start.39 = (f32[256,128]{1,0:T(8,128)S(1)}, f32[256,128]{1,0:T(8,128)S(1)}, u32[]{:S(2)}, u32[]{:S(2)}) collective-permute-start(f32[256,128]{1,0:T(8,128)S(1)} %get-tuple-element.83.refs_3_), channel_id=1, source_target_pairs={{0,1},{1,0},{2,3},{3,2},{4,5},{5,4},{6,7},{7,6},{8,9},{9,8},{10,11... | collective-permute-start | bytes 393224 | tf_op jit(solution)/shard_map/ppermute | solution.py:1007
  34.5 10.2 %collective-permute-start.40 = (f32[256,128]{1,0:T(8,128)S(1)}, f32[256,128]{1,0:T(8,128)S(1)}, u32[]{:S(2)}, u32[]{:S(2)}) collective-permute-start(f32[256,128]{1,0:T(8,128)S(1)} %get-tuple-element.83.refs_3_), channel_id=1, source_target_pairs={{1,2},{3,4},{5,6},{7,8},{9,10},{11,12},{13,14},{15,16},{17,18},{19... | collective-permute-start | bytes 393224 | tf_op jit(solution)/shard_map/ppermute | solution.py:1011
  49.5 16.0 %copy-start.4 = (f32[3,4,64,256]{3,2,1,0:T(8,128)S(1)}, f32[3,4,64,256]{3,2,1,0:T(8,128)}, u32[]{:S(2)}) copy-start(f32[3,4,64,256]{3,2,1,0:T(8,128)} %refs_0_.3) | copy-start | bytes 2359300
  49.6 16.0 %copy-start.22 = (f32[8,1024]{1,0:T(8,128)S(1)}, f32[8,1024]{1,0:T(8,128)}, u32[]{:S(2)}) copy-start(f32[8,1024]{1,0:T(8,128)} %refs_8_.1) | copy-start | bytes 98308
  49.6 11.7 %all-to-all-start.4 = ((f32[32,3,4,128]{3,2,1,0:T(4,128)}), f32[32,3,4,128]{3,2,1,0:T(4,128)S(1)}, u32[]{:S(2)}, u32[]{:S(2)}) async-start(f32[32,3,4,128]{3,2,1,0:T(4,128)} %get-tuple-element.84), calls=%async_computation.4 | async-start | bytes 393216 | tf_op jit(solution)/shard_map/all_to_all | solution.py:1087
  (1 other events, 1.1 us)
